TPU v7x, 256 devices: a whole 4x4x8 slice. The times are simulated.
256 devices in a mesh: cells: 64 (over z, y, core), sub: 4 (over x).
Axes of the slice: x: 4, y: 4, z: 8, core: 2. Of those that a mesh axis runs over, the one named last changes fastest.
Arguments:
- leaf_multipoles: bfloat16 [262144, 296], P(('cells', 'sub')), may hold values from -6 to 6
- occupancy: int32 [262144], P(('cells', 'sub')), may hold values 0 or 1
- upward_maps: bfloat16 [2368, 296], replicated, may hold values from -0.125 to 0.125
- transfer_maps: bfloat16 [9472, 296], replicated, may hold values from -0.125 to 0.125
- downward_maps: bfloat16 [296, 2368], replicated, may hold values from -0.375 to 0.375
- sources_seven: int32 [262144, 8], P(('cells', 'sub')), may hold values from 0 to 262143, as said below
- classes_seven: int32 [262144, 8], P(('cells', 'sub')), may hold values from 0 to 31
- sources_six: int32 [32768, 8], P(('cells', 'sub')), may hold values from 0 to 32767, as said below
- classes_six: int32 [32768, 8], P(('cells', 'sub')), may hold values from 0 to 31
- sources_five: int32 [4096, 8], P(('cells', 'sub')), may hold values from 0 to 4095
- classes_five: int32 [4096, 8], P(('cells', 'sub')), may hold values from 0 to 31
- sources_four: int32 [512, 8], P(('cells', 'sub')), may hold values from 0 to 511
- classes_four: int32 [512, 8], P(('cells', 'sub')), may hold values from 0 to 31
Outputs:
- leaf_locals: bfloat16 [262144, 296], P(('cells', 'sub'))
Inputs may be any that keep to these rules, and one draw needn't show every extreme that they name: `sources_seven`: each entry lies within half of 1024 positions of its own cell's index. `sources_six`: each entry lies within half of 128 positions of its own cell's index.
All inputs are finite; a program needn't handle non-finite values. No bound on the sum of `occupancy` on one device may be relied on, other than what follows from the above.
Results may differ from a plain program's by a relative error of at most 0.015.
Values may be sent and summed in bfloat16 or wider, within the bound.
No kernel may reach another device: no remote copies, remote signals or barrier semaphores. Data moves between devices by JAX's collectives and lax.ppermute only.
A program may use at most 128 MiB of HBM per device.

v0:
```python
import jax
import jax.numpy as jnp
from jax import lax
from jax.sharding import PartitionSpec as P


def shifted(value, axis, steps):
    count = lax.axis_size(axis)
    first, last = (max(0, -steps), min(count, count - steps))
    return lax.ppermute(value, axis, [(source, source + steps) for source in range(first, last)])


def ascend(children, upward_maps):
    width = children.shape[1]
    merged = children.reshape(-1, 8 * width)
    return jnp.dot(merged, upward_maps, preferred_element_type=jnp.float32).astype(jnp.bfloat16)


def descend(parents, downward_maps):
    width = parents.shape[1]
    spread = jnp.dot(parents, downward_maps, preferred_element_type=jnp.float32)
    return spread.reshape(-1, width)


def translate(table, indices, classes, transfer_maps):
    count = indices.shape[0]
    entries = indices.shape[1]
    width = table.shape[1]
    kinds = transfer_maps.shape[0] // width
    blocked = min(count, 512)
    labels = jnp.arange(kinds, dtype=jnp.int32)

    def one_block(pair):
        index_rows, class_rows = pair
        total = jnp.zeros((blocked, kinds, width), jnp.float32)
        for entry in range(entries):
            picked = jnp.take(table, index_rows[:, entry], axis=0).astype(jnp.float32)
            match = class_rows[:, entry][:, None] == labels[None, :]
            total = total + jnp.where(match[:, :, None], picked[:, None, :], 0.0)
        grouped = total.astype(jnp.bfloat16).reshape(blocked, kinds * width)
        return jnp.dot(grouped, transfer_maps, preferred_element_type=jnp.float32)

    result = lax.map(
        one_block, (indices.reshape(-1, blocked, entries), classes.reshape(-1, blocked, entries))
    )
    return result.reshape(count, width)


def neighbour_rows(multi):
    count = multi.shape[0]
    below = shifted(multi, ("cells", "sub"), 1)
    above = shifted(multi, ("cells", "sub"), -1)
    return (below, above, count)


def near_table(multi, below, above, leading, sources):
    count = multi.shape[0]
    place = lax.axis_index(("cells", "sub"))
    first_row = place * count - leading
    window = jnp.concatenate([below, multi, above], axis=0)
    return (window, sources - first_row)


def body(
    leaf_multipoles,
    occupancy,
    upward_maps,
    transfer_maps,
    downward_maps,
    sources_seven,
    classes_seven,
    sources_six,
    classes_six,
    sources_five,
    classes_five,
    sources_four,
    classes_four,
):
    multi_seven = jnp.where(
        occupancy[:, None] > 0, leaf_multipoles, jnp.zeros_like(leaf_multipoles)
    )
    multi_six = ascend(multi_seven, upward_maps)
    multi_five = ascend(multi_six, upward_maps)
    below_seven, above_seven, lead_seven = neighbour_rows(multi_seven)
    table_seven, index_seven = near_table(
        multi_seven, below_seven, above_seven, lead_seven, sources_seven
    )
    below_six, above_six, lead_six = neighbour_rows(multi_six)
    table_six, index_six = near_table(multi_six, below_six, above_six, lead_six, sources_six)
    multi_four = ascend(multi_five, upward_maps)
    gathered, gathered_four = (
        lax.all_gather(multi_five, ("cells", "sub"), axis=0, tiled=True),
        lax.all_gather(multi_four, ("cells", "sub"), axis=0, tiled=True),
    )
    table_five, index_five = (gathered, sources_five)
    table_four, index_four = (gathered_four, sources_four)
    local_four = translate(table_four, index_four, classes_four, transfer_maps).astype(jnp.bfloat16)
    local_five = (
        descend(local_four, downward_maps)
        + translate(table_five, index_five, classes_five, transfer_maps)
    ).astype(jnp.bfloat16)
    local_six = (
        descend(local_five, downward_maps)
        + translate(table_six, index_six, classes_six, transfer_maps)
    ).astype(jnp.bfloat16)
    local_seven = (
        descend(local_six, downward_maps)
        + translate(table_seven, index_seven, classes_seven, transfer_maps)
    ).astype(jnp.bfloat16)
    return local_seven


def solution(mesh):
    in_specs = (
        P(("cells", "sub"), None),
        P(("cells", "sub")),
        P(),
        P(),
        P(),
        P(("cells", "sub"), None),
        P(("cells", "sub"), None),
        P(("cells", "sub"), None),
        P(("cells", "sub"), None),
        P(("cells", "sub"), None),
        P(("cells", "sub"), None),
        P(("cells", "sub"), None),
        P(("cells", "sub"), None),
    )
    out_specs = P(("cells", "sub"), None)
    return jax.shard_map(body, mesh=mesh, in_specs=in_specs, out_specs=out_specs, check_vma=False)
```

profile of v0, /device:TPU:1, one launch (start us, length us, event | category | flops | bytes accessed | tf_op | source)
XLA Modules:
  0.0 395.6 jit_solution(1165598431126465467)
XLA Ops:
  9.8 2.5 reshape.990
  12.3 2.7 convolution_convert_fusion
  15.0 3.9 collective-permute-start
  18.9 3.8 collective-permute-start.1
  22.7 1.9 collective-permute-start.2
  24.6 4.9 %collective-permute-start.3 = (bf16[1024,296]{0,1:T(8,128)(2,1)S(1)}, bf16[1024,296]{0,1:T(8,128)(2,1)}, u32[]{:S(2)}, u32[]{:S(2)}) collective-permute-start(bf16[1024,296]{0,1:T(8,128)(2,1)S(1)} %broadcast_select_fusion), channel_id=1, source_target_pairs={{1,0},{2,1},{3,2},{4,3},{5,4},{6,5},{7,6},{8,7},{9,8},{10,9},{11,1... | collective-permute-start | bytes 1818632 | tf_op jit(solution)/shard_map/ppermute | solution.py:10
  32.8 2.0 convolution_convert_fusion.1
  52.5 75.2 %all-gather = bf16[256,2,296]{2,1,0:T(2,128)(2,1)S(1)} all-gather(bf16[1,2,296]{2,1,0:T(2,128)(2,1)S(1)} %fusion.8), channel_id=1, replica_groups=mesh['cells'=64,'sub'=4] {'cells','sub'}, dimensions={0}, use_global_device_ids=true | all-gather | bytes 304288 | tf_op jit(solution)/shard_map/all_gather | solution.py:93
  143.6 4.8 %fusion.9 = f32[2,2368]{1,0:T(2,128)S(1)} fusion(bf16[296,2368]{1,0:T(8,128)(2,1)S(1)} %copy-done, bf16[2,9472]{1,0:T(2,128)(2,1)S(1)} %reshape.1272, bf16[9472,296]{0,1:T(8,128)(2,1)} %param.26), kind=kOutput, calls=%fused_computation.93 | convolution fusion | flops 14019152 | bytes 7066112 | tf_op jit(solution)/shard_map/dot_general | solution.py:21
  162.9 5.8 %add_convert_fusion.1 = bf16[128,32,296]{0,2,1:T(8,128)(2,1)} fusion(f32[128,296]{0,1:T(8,128)S(1)} %get-tuple-element.343, f32[128,296]{0,1:T(8,128)S(1)} %get-tuple-element.344, f32[128,296]{0,1:T(8,128)S(1)} %get-tuple-element.345, f32[128,296]{0,1:T(8,128)S(1)} %get-tuple-element.346, f32[128,296]{0,1:T(8,128)S(1)} %get-tuple-element.347, ...), kind=kLoop, calls=%fused_computation.78 | loop fusion | flops 19398656 | bytes 3670016 | tf_op jit(solution)/shard_map/while/body/eval_jaxpr/convert_element_type | solution.py:40
  170.3 2.5 copy.112
  172.8 166.5 %while.8 = (s32[]{:T(128)}, f32[2,512,296]{1,2,0:T(8,128)}, s32[2,512,8]{1,2,0:T(8,128)S(1)}, s32[2,512,8]{1,2,0:T(8,128)S(1)}, bf16[3072,296]{1,0:T(8,128)(2,1)}, /*index=5*/bf16[9472,296]{0,1:T(8,128)(2,1)}, s32[]{:T(128)}) while((s32[]{:T(128)}, f32[2,512,296]{1,2,0:T(8,128)}, s32[2,512,8]{1,2,0:T(8,128)S(1)}, ...), condition=%wide.region_1.6_spmd.clone.clone, body=%wide.region_0.5_spmd.clone.clone.sunk | while | flops 2951196672 | bytes 64791168 | solution.py:43
  183.8 3.8 gather_fusion.1
  187.9 3.8 gather_fusion.2
  191.9 3.8 gather_fusion.3
  197.7 4.4 %gather_fusion.4 = bf16[512,296]{1,0:T(8,128)(2,1)} fusion(bf16[3072,296]{1,0:T(8,128)(2,1)} %get-tuple-element.450, s32[1024]{0:T(1024)S(1)} %pad_clamp_fusion.44), kind=kCustom, calls=%fused_computation.27.clone.clone.1 | custom fusion | bytes 608256 | tf_op jit(solution)/shard_map/while/body/eval_jaxpr/jit(_take)/gather | solution.py:37
  205.8 4.4 %gather_fusion.5 = bf16[512,296]{1,0:T(8,128)(2,1)} fusion(bf16[3072,296]{1,0:T(8,128)(2,1)} %get-tuple-element.450, s32[1024]{0:T(1024)S(1)} %pad_clamp_fusion.45), kind=kCustom, calls=%fused_computation.26.clone.clone.1 | custom fusion | bytes 608256 | tf_op jit(solution)/shard_map/while/body/eval_jaxpr/jit(_take)/gather | solution.py:37
  210.2 1.9 copy.129
  213.9 4.4 %gather_fusion.6 = bf16[512,296]{1,0:T(8,128)(2,1)} fusion(bf16[3072,296]{1,0:T(8,128)(2,1)} %get-tuple-element.450, s32[1024]{0:T(1024)S(1)} %pad_clamp_fusion.46), kind=kCustom, calls=%fused_computation.25.clone.clone.1 | custom fusion | bytes 608256 | tf_op jit(solution)/shard_map/while/body/eval_jaxpr/jit(_take)/gather | solution.py:37
  218.3 1.9 copy.130
  222.1 4.4 %gather_fusion.7 = bf16[512,296]{1,0:T(8,128)(2,1)} fusion(bf16[3072,296]{1,0:T(8,128)(2,1)} %get-tuple-element.450, s32[1024]{0:T(1024)S(1)} %pad_clamp_fusion.47), kind=kCustom, calls=%fused_computation.3.clone.clone.1 | custom fusion | bytes 608256 | tf_op jit(solution)/shard_map/while/body/eval_jaxpr/jit(_take)/gather | solution.py:37
  230.2 4.4 %gather_fusion = bf16[512,296]{1,0:T(8,128)(2,1)} fusion(bf16[3072,296]{1,0:T(8,128)(2,1)} %get-tuple-element.450, s32[1024]{0:T(1024)S(1)} %pad_clamp_fusion.40), kind=kCustom, calls=%fused_computation.31.clone.clone.1 | custom fusion | bytes 608256 | tf_op jit(solution)/shard_map/while/body/eval_jaxpr/jit(_take)/gather | solution.py:37
  237.8 19.8 %add_convert_fusion.5 = bf16[512,32,296]{0,2,1:T(8,128)(2,1)S(1)} fusion(f32[512,296]{0,1:T(8,128)S(1)} %select_convert_fusion.32, f32[512,296]{0,1:T(8,128)S(1)} %select_convert_fusion.33, f32[512,296]{0,1:T(8,128)S(1)} %select_convert_fusion.34, f32[512,296]{0,1:T(8,128)S(1)} %select_convert_fusion.35, f32[512,296]{0,1:T(8,128)} %select_convert_fusion.36, ...), kind=kLoop, calls=%fused_computation.33.clone.1 | loop fusion | flops 77594624 | bytes 14680064 | tf_op jit(solution)/shard_map/while/body/eval_jaxpr/convert_element_type | solution.py:40
  257.7 3.9 fusion.46
  261.6 3.8 gather_fusion.1
  265.7 3.8 gather_fusion.2
  269.7 3.8 gather_fusion.3
  275.5 4.4 %gather_fusion.4 = bf16[512,296]{1,0:T(8,128)(2,1)} fusion(bf16[3072,296]{1,0:T(8,128)(2,1)} %get-tuple-element.450, s32[1024]{0:T(1024)S(1)} %pad_clamp_fusion.44), kind=kCustom, calls=%fused_computation.27.clone.clone.1 | custom fusion | bytes 608256 | tf_op jit(solution)/shard_map/while/body/eval_jaxpr/jit(_take)/gather | solution.py:37
  283.6 4.4 %gather_fusion.5 = bf16[512,296]{1,0:T(8,128)(2,1)} fusion(bf16[3072,296]{1,0:T(8,128)(2,1)} %get-tuple-element.450, s32[1024]{0:T(1024)S(1)} %pad_clamp_fusion.45), kind=kCustom, calls=%fused_computation.26.clone.clone.1 | custom fusion | bytes 608256 | tf_op jit(solution)/shard_map/while/body/eval_jaxpr/jit(_take)/gather | solution.py:37
  288.0 1.9 copy.129
  291.7 4.4 %gather_fusion.6 = bf16[512,296]{1,0:T(8,128)(2,1)} fusion(bf16[3072,296]{1,0:T(8,128)(2,1)} %get-tuple-element.450, s32[1024]{0:T(1024)S(1)} %pad_clamp_fusion.46), kind=kCustom, calls=%fused_computation.25.clone.clone.1 | custom fusion | bytes 608256 | tf_op jit(solution)/shard_map/while/body/eval_jaxpr/jit(_take)/gather | solution.py:37
  299.9 4.4 %gather_fusion.7 = bf16[512,296]{1,0:T(8,128)(2,1)} fusion(bf16[3072,296]{1,0:T(8,128)(2,1)} %get-tuple-element.450, s32[1024]{0:T(1024)S(1)} %pad_clamp_fusion.47), kind=kCustom, calls=%fused_computation.3.clone.clone.1 | custom fusion | bytes 608256 | tf_op jit(solution)/shard_map/while/body/eval_jaxpr/jit(_take)/gather | solution.py:37
  308.0 4.4 %gather_fusion = bf16[512,296]{1,0:T(8,128)(2,1)} fusion(bf16[3072,296]{1,0:T(8,128)(2,1)} %get-tuple-element.450, s32[1024]{0:T(1024)S(1)} %pad_clamp_fusion.40), kind=kCustom, calls=%fused_computation.31.clone.clone.1 | custom fusion | bytes 608256 | tf_op jit(solution)/shard_map/while/body/eval_jaxpr/jit(_take)/gather | solution.py:37
  315.7 19.8 %add_convert_fusion.5 = bf16[512,32,296]{0,2,1:T(8,128)(2,1)S(1)} fusion(f32[512,296]{0,1:T(8,128)S(1)} %select_convert_fusion.32, f32[512,296]{0,1:T(8,128)S(1)} %select_convert_fusion.33, f32[512,296]{0,1:T(8,128)S(1)} %select_convert_fusion.34, f32[512,296]{0,1:T(8,128)S(1)} %select_convert_fusion.35, f32[512,296]{0,1:T(8,128)} %select_convert_fusion.36, ...), kind=kLoop, calls=%fused_computation.33.clone.1 | loop fusion | flops 77594624 | bytes 14680064 | tf_op jit(solution)/shard_map/while/body/eval_jaxpr/convert_element_type | solution.py:40
  335.5 3.9 fusion.46
  341.2 3.0 gather_fusion.16
  344.2 3.0 gather_fusion.17
  347.3 3.0 gather_fusion.18
  350.3 3.0 gather_fusion.19
  353.4 3.0 gather_fusion.20
  356.4 3.0 gather_fusion.21
  360.1 3.0 gather_fusion.22
  363.1 3.0 gather_fusion.23
  369.0 4.9 %fusion.7 = f32[16,2368]{1,0:T(8,128)S(1)} fusion(bf16[296,2368]{1,0:T(8,128)(2,1)S(1)} %copy-done, f32[16,296]{1,0:T(8,128)S(1)} %copy-done.4, bf16[16,9472]{1,0:T(8,128)(2,1)} %reshape.1273, bf16[9472,296]{0,1:T(8,128)(2,1)} %get-tuple-element.454), kind=kOutput, calls=%fused_computation.89 | convolution fusion | flops 112157952 | bytes 7482880 | tf_op jit(solution)/shard_map/dot_general | solution.py:21
  374.2 6.7 %fusion.5 = f32[128,2368]{1,0:T(8,128)} fusion(bf16[296,2368]{1,0:T(8,128)(2,1)S(1)} %copy-done, f32[128,296]{0,1:T(8,128)S(1)} %copy.110, bf16[128,9472]{0,1:T(8,128)(2,1)} %bitcast.176, bf16[9472,296]{0,1:T(8,128)(2,1)} %get-tuple-element.454), kind=kOutput, calls=%fused_computation.85 | convolution fusion | flops 897263616 | bytes 10798080 | tf_op jit(solution)/shard_map/dot_general | solution.py:21
  380.8 3.0 reshape.995
  383.9 2.5 fusion.3
  386.4 2.2 copy.114
  (318 shorter events, 96.8 us)
Async XLA Ops:
  6.5 137.1 %copy-start = (bf16[296,2368]{1,0:T(8,128)(2,1)S(1)}, bf16[296,2368]{1,0:T(8,128)(2,1)}, u32[]{:S(2)}) copy-start(bf16[296,2368]{1,0:T(8,128)(2,1)} %param.27) | copy-start | bytes 4205572
  6.5 26.2 %copy-start.1 = (bf16[2368,296]{0,1:T(8,128)(2,1)S(1)}, bf16[2368,296]{0,1:T(8,128)(2,1)}, u32[]{:S(2)}) copy-start(bf16[2368,296]{0,1:T(8,128)(2,1)} %param.25) | copy-start | bytes 4205572
  6.5 29.1 %copy-start.5 = (s32[2,8]{1,0:T(2,128)S(1)}, s32[2,8]{1,0:T(2,128)}, u32[]{:S(2)}) copy-start(s32[2,8]{1,0:T(2,128)} %param.34) | copy-start | bytes 196
  6.5 33.9 %copy-start.9 = (s32[128,8]{0,1:T(8,128)S(1)}, s32[128,8]{0,1:T(8,128)}, u32[]{:S(2)}) copy-start(s32[128,8]{0,1:T(8,128)} %param.30) | copy-start | bytes 12292
  6.5 39.3 %copy-start.10 = (s32[128,8]{0,1:T(8,128)S(1)}, s32[128,8]{0,1:T(8,128)}, u32[]{:S(2)}) copy-start(s32[128,8]{0,1:T(8,128)} %param.31) | copy-start | bytes 12292
  6.5 39.9 %copy-start.8 = (s32[16,8]{0,1:T(8,128)S(1)}, s32[16,8]{0,1:T(8,128)}, u32[]{:S(2)}) copy-start(s32[16,8]{0,1:T(8,128)} %param.32) | copy-start | bytes 1540
  6.6 44.7 %copy-start.11 = (s32[16,8]{0,1:T(8,128)S(1)}, s32[16,8]{0,1:T(8,128)}, u32[]{:S(2)}) copy-start(s32[16,8]{0,1:T(8,128)} %param.33) | copy-start | bytes 1540
  6.6 334.6 %all-gather.3.cloned.1.call-start = ((), (), s32[]{:S(2)}) async-start(), calls=%async_computation | async-start | bytes 3158016 | tf_op jit(solution)/shard_map/all_gather | solution.py:92
  8.6 119.4 %copy-start.2 = (bf16[1024,296]{0,1:T(8,128)(2,1)}, bf16[1024,296]{0,1:T(8,128)(2,1)S(1)}, u32[]{:S(2)}) copy-start(bf16[1024,296]{0,1:T(8,128)(2,1)S(1)} %broadcast_select_fusion) | copy-start | bytes 1818628
  8.6 128.3 %copy-start.6 = (s32[2,8]{1,0:T(2,128)S(1)}, s32[2,8]{1,0:T(2,128)}, u32[]{:S(2)}) copy-start(s32[2,8]{1,0:T(2,128)} %param.35) | copy-start | bytes 196
  15.0 137.5 %collective-permute-start = (bf16[128,296]{0,1:T(8,128)(2,1)}, bf16[128,296]{0,1:T(8,128)(2,1)}, u32[]{:S(2)}, u32[]{:S(2)}) collective-permute-start(bf16[128,296]{0,1:T(8,128)(2,1)} %convolution_convert_fusion), channel_id=1, source_target_pairs={{0,1},{1,2},{2,3},{3,4},{4,5},{5,6},{6,7},{7,8},{8,9},{9,10},{10,1... | collective-permute-start | bytes 227336 | tf_op jit(solution)/shard_map/ppermute | solution.py:10
  18.9 133.6 %collective-permute-start.1 = (bf16[128,296]{0,1:T(8,128)(2,1)}, bf16[128,296]{0,1:T(8,128)(2,1)}, u32[]{:S(2)}, u32[]{:S(2)}) collective-permute-start(bf16[128,296]{0,1:T(8,128)(2,1)} %convolution_convert_fusion), channel_id=1, source_target_pairs={{1,0},{2,1},{3,2},{4,3},{5,4},{6,5},{7,6},{8,7},{9,8},{10,9},{11,1... | collective-permute-start | bytes 227336 | tf_op jit(solution)/shard_map/ppermute | solution.py:10
  22.7 146.0 %collective-permute-start.2 = (bf16[1024,296]{0,1:T(8,128)(2,1)S(1)}, bf16[1024,296]{0,1:T(8,128)(2,1)}, u32[]{:S(2)}, u32[]{:S(2)}) collective-permute-start(bf16[1024,296]{0,1:T(8,128)(2,1)S(1)} %broadcast_select_fusion), channel_id=1, source_target_pairs={{0,1},{1,2},{2,3},{3,4},{4,5},{5,6},{6,7},{7,8},{8,9},{9,10},{10,1... | collective-permute-start | bytes 1818632 | tf_op jit(solution)/shard_map/ppermute | solution.py:10
  24.6 144.1 %collective-permute-start.3 = (bf16[1024,296]{0,1:T(8,128)(2,1)S(1)}, bf16[1024,296]{0,1:T(8,128)(2,1)}, u32[]{:S(2)}, u32[]{:S(2)}) collective-permute-start(bf16[1024,296]{0,1:T(8,128)(2,1)S(1)} %broadcast_select_fusion), channel_id=1, source_target_pairs={{1,0},{2,1},{3,2},{4,3},{5,4},{6,5},{7,6},{8,7},{9,8},{10,9},{11,1... | collective-permute-start | bytes 1818632 | tf_op jit(solution)/shard_map/ppermute | solution.py:10
  51.8 100.1 %copy-start.7 = (s32[1024,8]{0,1:T(8,128)S(1)}, s32[1024,8]{0,1:T(8,128)}, u32[]{:S(2)}) copy-start(s32[1024,8]{0,1:T(8,128)} %param.28) | copy-start | bytes 98308
  52.3 96.8 %copy-start.35 = (s32[128]{0:T(128)S(1)}, s32[128]{0:T(128)}, u32[]{:S(2)}) copy-start(s32[128]{0:T(128)} %get-tuple-element.265) | copy-start | bytes 1540
  52.3 96.8 %copy-start.36 = (s32[128]{0:T(128)S(1)}, s32[128]{0:T(128)}, u32[]{:S(2)}) copy-start(s32[128]{0:T(128)} %get-tuple-element.266) | copy-start | bytes 1540
  52.3 96.8 %copy-start.33 = (s32[128]{0:T(128)S(1)}, s32[128]{0:T(128)}, u32[]{:S(2)}) copy-start(s32[128]{0:T(128)} %get-tuple-element.260) | copy-start | bytes 1540
  52.3 96.8 %copy-start.34 = (s32[128]{0:T(128)S(1)}, s32[128]{0:T(128)}, u32[]{:S(2)}) copy-start(s32[128]{0:T(128)} %get-tuple-element.261) | copy-start | bytes 1540
  52.4 96.8 %copy-start.31 = (s32[128]{0:T(128)S(1)}, s32[128]{0:T(128)}, u32[]{:S(2)}) copy-start(s32[128]{0:T(128)} %get-tuple-element.262) | copy-start | bytes 1540
  52.4 96.8 %copy-start.32 = (s32[128]{0:T(128)S(1)}, s32[128]{0:T(128)}, u32[]{:S(2)}) copy-start(s32[128]{0:T(128)} %get-tuple-element.263) | copy-start | bytes 1540
  52.4 96.8 %copy-start.29 = (s32[128]{0:T(128)S(1)}, s32[128]{0:T(128)}, u32[]{:S(2)}) copy-start(s32[128]{0:T(128)} %get-tuple-element.259) | copy-start | bytes 1540
  52.4 96.8 %copy-start.30 = (s32[128]{0:T(128)S(1)}, s32[128]{0:T(128)}, u32[]{:S(2)}) copy-start(s32[128]{0:T(128)} %get-tuple-element.264) | copy-start | bytes 1540
  52.4 96.8 %copy-start.43 = (s32[16]{0:T(128)S(1)}, s32[16]{0:T(128)}, u32[]{:S(2)}) copy-start(s32[16]{0:T(128)} %get-tuple-element.287) | copy-start | bytes 196
  52.4 96.8 %copy-start.44 = (s32[16]{0:T(128)S(1)}, s32[16]{0:T(128)}, u32[]{:S(2)}) copy-start(s32[16]{0:T(128)} %get-tuple-element.288) | copy-start | bytes 196
  52.4 97.5 %copy-start.41 = (s32[16]{0:T(128)S(1)}, s32[16]{0:T(128)}, u32[]{:S(2)}) copy-start(s32[16]{0:T(128)} %get-tuple-element.282) | copy-start | bytes 196
  52.4 97.5 %copy-start.42 = (s32[16]{0:T(128)S(1)}, s32[16]{0:T(128)}, u32[]{:S(2)}) copy-start(s32[16]{0:T(128)} %get-tuple-element.283) | copy-start | bytes 196
  52.4 98.1 %copy-start.39 = (s32[16]{0:T(128)S(1)}, s32[16]{0:T(128)}, u32[]{:S(2)}) copy-start(s32[16]{0:T(128)} %get-tuple-element.284) | copy-start | bytes 196
  52.4 98.1 %copy-start.40 = (s32[16]{0:T(128)S(1)}, s32[16]{0:T(128)}, u32[]{:S(2)}) copy-start(s32[16]{0:T(128)} %get-tuple-element.285) | copy-start | bytes 196
  52.5 98.8 %copy-start.37 = (s32[16]{0:T(128)S(1)}, s32[16]{0:T(128)}, u32[]{:S(2)}) copy-start(s32[16]{0:T(128)} %get-tuple-element.281) | copy-start | bytes 196
  52.5 98.8 %copy-start.38 = (s32[16]{0:T(128)S(1)}, s32[16]{0:T(128)}, u32[]{:S(2)}) copy-start(s32[16]{0:T(128)} %get-tuple-element.286) | copy-start | bytes 196
  52.5 99.4 %copy-start.28 = (s32[16]{0:T(128)S(1)}, s32[16]{0:T(128)}, u32[]{:S(2)}) copy-start(s32[16]{0:T(128)} %get-tuple-element.300) | copy-start | bytes 196
  148.4 14.3 %copy-start.26 = (pred[128]{0:T(512)(128)(4,1)S(1)}, pred[128]{0:T(512)(128)(4,1)}, u32[]{:S(2)}) copy-start(pred[128]{0:T(512)(128)(4,1)} %get-tuple-element.209) | copy-start | bytes 388
  148.4 14.3 %copy-start.27 = (pred[128]{0:T(512)(128)(4,1)S(1)}, pred[128]{0:T(512)(128)(4,1)}, u32[]{:S(2)}) copy-start(pred[128]{0:T(512)(128)(4,1)} %get-tuple-element.279) | copy-start | bytes 388
  152.5 10.3 %copy-start.25 = (pred[128]{0:T(512)(128)(4,1)S(1)}, pred[128]{0:T(512)(128)(4,1)}, u32[]{:S(2)}) copy-start(pred[128]{0:T(512)(128)(4,1)} %get-tuple-element.277) | copy-start | bytes 388
  172.8 174.4 %copy-start.18 = (pred[16]{0:T(512)(128)(4,1)S(1)}, pred[16]{0:T(512)(128)(4,1)}, u32[]{:S(2)}) copy-start(pred[16]{0:T(512)(128)(4,1)} %get-tuple-element.225) | copy-start | bytes 52
  172.8 174.4 %copy-start.19 = (pred[16]{0:T(512)(128)(4,1)S(1)}, pred[16]{0:T(512)(128)(4,1)}, u32[]{:S(2)}) copy-start(pred[16]{0:T(512)(128)(4,1)} %get-tuple-element.297) | copy-start | bytes 52
  172.8 180.5 %copy-start.16 = (pred[16]{0:T(512)(128)(4,1)S(1)}, pred[16]{0:T(512)(128)(4,1)}, u32[]{:S(2)}) copy-start(pred[16]{0:T(512)(128)(4,1)} %get-tuple-element.293) | copy-start | bytes 52
  172.8 180.5 %copy-start.17 = (pred[16]{0:T(512)(128)(4,1)S(1)}, pred[16]{0:T(512)(128)(4,1)}, u32[]{:S(2)}) copy-start(pred[16]{0:T(512)(128)(4,1)} %get-tuple-element.295) | copy-start | bytes 52
  172.8 186.6 %copy-start.14 = (pred[16]{0:T(512)(128)(4,1)S(1)}, pred[16]{0:T(512)(128)(4,1)}, u32[]{:S(2)}) copy-start(pred[16]{0:T(512)(128)(4,1)} %get-tuple-element.289) | copy-start | bytes 52
  172.8 186.6 %copy-start.15 = (pred[16]{0:T(512)(128)(4,1)S(1)}, pred[16]{0:T(512)(128)(4,1)}, u32[]{:S(2)}) copy-start(pred[16]{0:T(512)(128)(4,1)} %get-tuple-element.291) | copy-start | bytes 52
  172.8 193.3 %copy-start.12 = (pred[16]{0:T(512)(128)(4,1)S(1)}, pred[16]{0:T(512)(128)(4,1)}, u32[]{:S(2)}) copy-start(pred[16]{0:T(512)(128)(4,1)} %get-tuple-element.299) | copy-start | bytes 52
  172.8 193.3 %copy-start.13 = (pred[16]{0:T(512)(128)(4,1)S(1)}, pred[16]{0:T(512)(128)(4,1)}, u32[]{:S(2)}) copy-start(pred[16]{0:T(512)(128)(4,1)} %get-tuple-element.301) | copy-start | bytes 52
  236.5 21.2 %slice-start = ((s8[5607424]{0:T(1024)(128)(4,1)}), s8[4194304]{0:T(1024)(128)(4,1)S(1)}, s32[]{:S(2)}) async-start(s8[5607424]{0:T(1024)(128)(4,1)} %bitcast.174), calls=%async_computation.1 | async-start | bytes 8388608 | tf_op jit(solution)/shard_map/while
  237.8 19.8 %slice-start.1 = ((s8[5607424]{0:T(1024)(128)(4,1)}), s8[1413120]{0:T(1024)(128)(4,1)S(1)}, s32[]{:S(2)}) async-start(s8[5607424]{0:T(1024)(128)(4,1)} %bitcast.174), calls=%async_computation.2 | async-start | bytes 2826240 | tf_op jit(solution)/shard_map/while
  314.3 21.2 %slice-start = ((s8[5607424]{0:T(1024)(128)(4,1)}), s8[4194304]{0:T(1024)(128)(4,1)S(1)}, s32[]{:S(2)}) async-start(s8[5607424]{0:T(1024)(128)(4,1)} %bitcast.174), calls=%async_computation.1 | async-start | bytes 8388608 | tf_op jit(solution)/shard_map/while
  315.6 19.8 %slice-start.1 = ((s8[5607424]{0:T(1024)(128)(4,1)}), s8[1413120]{0:T(1024)(128)(4,1)S(1)}, s32[]{:S(2)}) async-start(s8[5607424]{0:T(1024)(128)(4,1)} %bitcast.174), calls=%async_computation.2 | async-start | bytes 2826240 | tf_op jit(solution)/shard_map/while
  339.4 29.6 %copy-start.4 = (f32[16,296]{1,0:T(8,128)S(1)}, f32[16,296]{1,0:T(8,128)}, u32[]{:S(2)}) copy-start(f32[16,296]{1,0:T(8,128)} %reshape.993) | copy-start | bytes 56836
  (6 other events, 57.0 us)
Sparse Core Ops, SparseCore 0:
  34.9 112.2 all-gather.2
where the time goes:
time: 402 us; the launch traced here: 396 us
  local copies, waits for them, and re-layouts  147 us (37%)
  other arithmetic  103 us (26%)
  blocking collectives  75.2 us (19%)
  matrix products  29.4 us (7%)
  starting transfers between devices  14.5 us (4%)
  between operations  14.4 us (4%)
  loops' own time  11.4 us (3%)
    gather x64, local copies, waits for them, and re-layouts, one_block(): picked = jnp.take(table, index_rows[:, entry], axis=0).astype(jnp.float32)  125 us
    all_gather x1, blocking collectives, body(): lax.all_gather(multi_four, ('cells', 'sub'), axis=0, tiled=True)  75.2 us
    convert_element_type x5, other arithmetic, one_block(): grouped = total.astype(jnp.bfloat16).reshape(blocked, kinds * width)  47.1 us
    convert_element_type x32, other arithmetic, one_block(): picked = jnp.take(table, index_rows[:, entry], axis=0).astype(jnp.float32)  26 us
    dot_general x3, matrix products, descend(): spread = jnp.dot(parents, downward_maps, preferred_element_type=jnp.float32)  16.4 us
    ppermute x4, starting transfers between devices, shifted(): lax.ppermute(value, axis, [(source, source + steps) for source in range(f...  14.5 us
    gather x40, other arithmetic  14 us
    another operation x1, loops' own time, translate(): lax.map(one_block, (indices.reshape(-1, blocked, entries), classes.reshap...  11.4 us
  transfers between devices with their start and end apart: 5, of which 0 were waited for; matrix products, arithmetic and copies ran while one was open for 57% of the time, Pallas kernels for 0%

commit v1 on v0

v1 whole, which is shorter than its diff:
```python
import functools

import jax
import jax.numpy as jnp
from jax import lax
from jax.experimental import pallas as pl
from jax.experimental.pallas import tpu as pltpu
from jax.sharding import PartitionSpec as P

F = 296
KINDS = 32
LIST = 8
BF = jnp.bfloat16
F32 = jnp.float32
VM = pl.BlockSpec(memory_space=pltpu.VMEM)
ANY = pl.BlockSpec(memory_space=pl.ANY)
SM = pl.BlockSpec(memory_space=pltpu.SMEM)


def dot(a, b):
    return jnp.dot(a, b, preferred_element_type=F32)


def onehot(rel, depth):
    count = rel.shape[1]
    rows = lax.broadcasted_iota(jnp.int32, (depth, count), 0)
    return jnp.where(rows == rel, 1.0, 0.0).astype(BF)


def split_octants(children, first, width):
    count = children.shape[1]
    source = lax.broadcasted_iota(jnp.int32, (count, 2 * width), 0)
    place = lax.broadcasted_iota(jnp.int32, (count, 2 * width), 1)
    second = (place >= width).astype(jnp.int32)
    wanted = 8 * (place - width * second) + first + second
    return dot(children, jnp.where(source == wanted, 1.0, 0.0).astype(BF))


def ascend(children, up_ref, stack):
    for pair in range(4):
        both = split_octants(children, 2 * pair, 128)
        stack[2 * pair * F : (2 * pair + 1) * F, :] = both[:, :128]
        stack[(2 * pair + 1) * F : (2 * pair + 2) * F, :] = both[:, 128:]
    return dot(up_ref[...], stack[...].astype(BF))


def rise_body(lo_ref, hi_ref, up_ref, six_ref, five_ref, stack):
    children = jnp.concatenate([lo_ref[...], hi_ref[...]], axis=1)
    six = ascend(children, up_ref, stack).astype(BF)
    six_ref[...] = six
    five = ascend(six, up_ref, stack)
    five_ref[...] = five.T[:16, :].astype(BF)


def rise(lo, hi, up):
    return pl.pallas_call(
        rise_body,
        out_shape=(
            jax.ShapeDtypeStruct((F, 128), BF),
            jax.ShapeDtypeStruct((16, F), BF),
        ),
        in_specs=[VM] * 3,
        out_specs=(VM, VM),
        scratch_shapes=[pltpu.VMEM((8 * F, 128), F32)],
        compiler_params=pltpu.CompilerParams(vmem_limit_bytes=24 * 2**20),
        cost_estimate=pl.CostEstimate(flops=2 * 10**9, bytes_accessed=3 * 10**6, transcendentals=0),
        name="rise",
    )(lo, hi, up)


def spread(value, even, odd, slot, lanes):
    blank = jnp.zeros((8, value.shape[1]), F32)
    even[slot, :, lanes] = jnp.concatenate([value, blank], axis=0).astype(BF)
    odd[slot, :, lanes] = jnp.concatenate([blank, value], axis=0).astype(BF)


def stack_pair(grouped, row, lanes, even_tile, odd_tile):
    for i in range(18):
        grouped[pl.ds(row + 16 * i, 16), lanes] = even_tile(i)
    grouped[pl.ds(row + 288, 16), lanes] = even_tile(18) + odd_tile(0)
    for i in range(1, 19):
        grouped[pl.ds(row + 288 + 16 * i, 16), lanes] = odd_tile(i)


def group(labels, even, odd, grouped):
    count = grouped.shape[1]
    wide = [jnp.broadcast_to(label, (16, count)) for label in labels]

    def masks(kind):
        return [jnp.where(label == kind, 1.0, 0.0).astype(BF) for label in wide]

    def total(ref, mask, i):
        terms = [ref[j, 16 * i : 16 * i + 16, :] * mask[j] for j in range(LIST)]
        while len(terms) > 1:
            terms = [terms[q] + terms[q + 1] for q in range(0, len(terms), 2)]
        return terms[0]

    def pair(p, carry):
        first, second = masks(2 * p), masks(2 * p + 1)
        stack_pair(
            grouped,
            pl.multiple_of(p * 2 * F, 16),
            slice(None),
            lambda i: total(even, first, i),
            lambda i: total(odd, second, i),
        )
        return carry

    lax.fori_loop(0, KINDS // 2, pair, 0)


def transfer(maps, grouped, out_ref):
    out_ref[...] = dot(maps[:, :256], grouped[:256, :])

    def part(i, carry):
        at = pl.multiple_of(256 + i * 2304, 256)
        out_ref[...] += dot(maps[:, pl.ds(at, 2304)], grouped[pl.ds(at, 2304), :])
        return carry

    lax.fori_loop(0, 4, part, 0)


def near_body(block, a_ref, b_ref, c_ref, src_ref, cls_ref, maps_hbm, out_ref, maps, even, odd, grouped, sem):
    copy = pltpu.make_async_copy(maps_hbm, maps, sem)
    copy.start()
    lanes = slice(256 * block, 256 * block + 256)
    first = (a_ref, b_ref, c_ref)
    base = 256 * block if block < 2 else 256 * block - 512
    window = jnp.concatenate([ref[...] for ref in first], axis=1)[:, base : base + 1280]

    def one(j, carry):
        rel = src_ref[pl.ds(j, 1), lanes] - 256 * block
        spread(dot(window, onehot(rel, 1280)), even, odd, j, slice(None))
        return carry

    lax.fori_loop(0, LIST, one, 0)
    group([cls_ref[j : j + 1, lanes] for j in range(LIST)], even, odd, grouped)
    copy.wait()
    transfer(maps, grouped, out_ref)


def far_scratch(count):
    return [
        pltpu.VMEM((F, KINDS * F), BF),
        pltpu.VMEM((LIST, F + 8, count), BF),
        pltpu.VMEM((LIST, F + 8, count), BF),
        pltpu.VMEM((KINDS * F, count), BF),
        pltpu.SemaphoreType.DMA,
    ]


def near(block, a, b, c, src, cls, maps):
    return pl.pallas_call(
        functools.partial(near_body, block),
        out_shape=jax.ShapeDtypeStruct((F, 256), F32),
        in_specs=[VM] * 5 + [ANY],
        out_specs=VM,
        scratch_shapes=far_scratch(256),
        compiler_params=pltpu.CompilerParams(vmem_limit_bytes=28 * 2**20),
        cost_estimate=pl.CostEstimate(flops=6 * 10**9, bytes_accessed=6 * 10**6, transcendentals=0),
        name=f"near{block}",
    )(a, b, c, src, cls, maps)


def middle_body(below_ref, above_ref, six_ref, up_ref, src_ref, cls_ref, maps_hbm, out_ref, maps, even, odd, grouped, sem, stack):
    copy = pltpu.make_async_copy(maps_hbm, maps, sem)
    copy.start()
    children = jnp.concatenate([below_ref[...], above_ref[...]], axis=1)
    halo = ascend(children, up_ref, stack).astype(BF)
    window = jnp.concatenate([six_ref[...], halo], axis=1)

    def one(j, carry):
        rel = src_ref[pl.ds(j, 1), :]
        spread(dot(window, onehot(rel, 256)), even, odd, j, slice(None))
        return carry

    lax.fori_loop(0, LIST, one, 0)
    group([cls_ref[j : j + 1, :] for j in range(LIST)], even, odd, grouped)
    copy.wait()
    transfer(maps, grouped, out_ref)


def middle(below, above, six, up, src, cls, maps):
    return pl.pallas_call(
        middle_body,
        out_shape=jax.ShapeDtypeStruct((F, 128), F32),
        in_specs=[VM] * 6 + [ANY],
        out_specs=VM,
        scratch_shapes=far_scratch(128) + [pltpu.VMEM((8 * F, 128), F32)],
        compiler_params=pltpu.CompilerParams(vmem_limit_bytes=28 * 2**20),
        cost_estimate=pl.CostEstimate(flops=4 * 10**9, bytes_accessed=6 * 10**6, transcendentals=0),
        name="middle",
    )(below, above, six, up, src, cls, maps)


def descend(parents, down_ref, even, odd, stack, count):
    wide = min(count, 256)

    def chunk(q, carry):
        parent = lax.broadcasted_iota(jnp.int32, (128, wide), 0)
        child = lax.broadcasted_iota(jnp.int32, (128, wide), 1) + q * wide
        copies = dot(parents, jnp.where(child // 8 == parent, 1.0, 0.0).astype(BF))
        spread(copies, even, odd, 0, slice(0, wide))
        octant = lax.broadcasted_iota(jnp.int32, (16, wide), 1) % 8
        lanes = pl.ds(pl.multiple_of(q * wide, wide), wide)
        for p in range(4):
            first = jnp.where(octant == 2 * p, 1.0, 0.0).astype(BF)
            second = jnp.where(octant == 2 * p + 1, 1.0, 0.0).astype(BF)
            stack_pair(
                stack,
                p * 2 * F,
                lanes,
                lambda i: even[0, 16 * i : 16 * i + 16, :wide] * first,
                lambda i: odd[0, 16 * i : 16 * i + 16, :wide] * second,
            )
        return carry

    if count == wide:
        chunk(0, 0)
    else:
        lax.fori_loop(0, count // wide, chunk, 0)


def last_body(
    t0, t1, t2, t3, t4, t5, t6, t7, index_ref, cls_ref, up_ref, down_ref, six_ref,
    s0, s1, s2, s3, maps_hbm, out_ref,
    maps, even, odd, grouped, sem, rise_stack, coarse, fall_stack, wide_even, wide_odd,
):
    copy = pltpu.make_async_copy(maps_hbm, maps, sem)
    copy.start()
    wanted = index_ref[...]
    picked = jnp.zeros((F, 256), F32)
    for k, table in enumerate((t0, t1, t2, t3, t4, t5, t6, t7)):
        picked += dot(table[...], onehot(wanted - 512 * k, 512))
    even[...] = jnp.zeros(even.shape, BF)
    odd[...] = jnp.zeros(odd.shape, BF)
    rise_stack[...] = jnp.zeros(rise_stack.shape, F32)
    for o in range(8):
        rise_stack[o * F : (o + 1) * F, :16] = picked[:, 128 + 16 * o : 144 + 16 * o]
    four = dot(up_ref[...], rise_stack[...].astype(BF)).astype(BF).astype(F32)
    blank = jnp.zeros((F, 110), F32)
    for j in range(LIST):
        both = jnp.concatenate([picked[:, 16 * j : 16 * j + 16], four[:, 2 * j : 2 * j + 2], blank], axis=1)
        spread(both, even, odd, j, slice(None))
    group([cls_ref[j : j + 1, :] for j in range(LIST)], even, odd, grouped)
    copy.wait()
    transfer(maps, grouped, coarse)
    lane = lax.broadcasted_iota(jnp.int32, (F, 128), 1)
    far_five = jnp.where(lane < 16, coarse[...], 0.0)
    take = lax.broadcasted_iota(jnp.int32, (128, 128), 0) == lax.broadcasted_iota(jnp.int32, (128, 128), 1) + 16
    local = dot(coarse[...].astype(BF), jnp.where(take, 1.0, 0.0).astype(BF)).astype(BF)
    descend(local, down_ref, wide_even, wide_odd, fall_stack, 128)
    local = (dot(down_ref[...], fall_stack[:, :128]) + far_five).astype(BF)
    descend(local, down_ref, wide_even, wide_odd, fall_stack, 128)
    local = (dot(down_ref[...], fall_stack[:, :128]) + six_ref[...]).astype(BF)
    descend(local, down_ref, wide_even, wide_odd, fall_stack, 1024)
    for q, seven in enumerate((s0, s1, s2, s3)):
        lanes = slice(256 * q, 256 * q + 256)
        out_ref[:, lanes] = (dot(down_ref[...], fall_stack[:, lanes]) + seven[...]).astype(BF)


def last(tables, index, cls, up, down, six, sevens, maps):
    return pl.pallas_call(
        last_body,
        out_shape=jax.ShapeDtypeStruct((F, 1024), BF),
        in_specs=[VM] * 17 + [ANY],
        out_specs=VM,
        scratch_shapes=far_scratch(128)
        + [
            pltpu.VMEM((8 * F, 128), F32),
            pltpu.VMEM((F, 128), F32),
            pltpu.VMEM((8 * F, 1024), BF),
            pltpu.VMEM((1, F + 8, 256), BF),
            pltpu.VMEM((1, F + 8, 256), BF),
        ],
        compiler_params=pltpu.CompilerParams(vmem_limit_bytes=40 * 2**20),
        cost_estimate=pl.CostEstimate(flops=8 * 10**9, bytes_accessed=12 * 10**6, transcendentals=0),
        name="last",
    )(*tables, index, cls, up, down, six, *sevens, maps)


def shifted(value, axis, steps):
    count = lax.axis_size(axis)
    first, last_one = (max(0, -steps), min(count, count - steps))
    return lax.ppermute(value, axis, [(source, source + steps) for source in range(first, last_one)])


def turned(value, axis, size, stride, steps):
    pairs = []
    for source in range(lax.axis_size(axis)):
        position = (source // stride) % size
        target = source + ((position + steps) % size - position) * stride
        pairs.append((source, target))
    return lax.ppermute(value, axis, pairs)


along_z = lambda value, steps: turned(value, "cells", 8, 8, steps)
along_y = lambda value, steps: turned(value, "cells", 4, 2, steps)
along_core = lambda value, steps: turned(value, "cells", 2, 1, steps)
along_x = lambda value, steps: turned(value, "sub", 4, 1, steps)


def body(
    leaf_multipoles,
    occupancy,
    upward_maps,
    transfer_maps,
    downward_maps,
    sources_seven,
    classes_seven,
    sources_six,
    classes_six,
    sources_five,
    classes_five,
    sources_four,
    classes_four,
):
    leaves = leaf_multipoles.T
    up, maps = upward_maps.T, transfer_maps.T
    down = downward_maps.reshape(F, 8, F).transpose(2, 1, 0).reshape(F, 8 * F)
    masked = jnp.where(occupancy[None, :] > 0, leaves, jnp.zeros_like(leaves))
    lo, hi = masked[:, :512], masked[:, 512:]
    below = shifted(hi, ("cells", "sub"), 1)
    above = shifted(lo, ("cells", "sub"), -1)
    six, five = rise(lo, hi, up)

    cells, sub = lax.axis_index("cells"), lax.axis_index("sub")
    place = cells * 4 + sub
    src_seven = sources_seven.T - (place * 1024 - 512)
    cls_seven = classes_seven.T
    rel_six = sources_six.T - (place * 128 - 64)
    src_six = jnp.where(rel_six < 64, rel_six + 128, jnp.where(rel_six < 192, rel_six - 64, rel_six))

    minus, plus = along_z(five, 1), along_z(five, -1)
    three = jnp.stack([minus, five, plus])
    upper = along_z(three, -3)
    lower = along_z(three[1:], 3)
    column = jnp.concatenate([lower, three, upper], axis=0).reshape(128, F).T
    plane = jnp.concatenate([column, along_y(column, -1), along_y(column, 2), along_y(column, 1)], axis=1)
    tables = [plane, along_x(plane, -1), along_x(plane, 2), along_x(plane, 1)]
    tables = tables + [along_core(table, 1) for table in tables]

    def where_held(cell):
        device = cell // 16
        there = (device // 4, device % 4)
        dz = (there[0] // 8 - cells // 8 + 3) % 8
        dy = (there[0] // 2 - cells // 2) % 4
        dc = (there[0] - cells) % 2
        dx = (there[1] - sub) % 4
        return (dc * 4 + dx) * 512 + dy * 128 + dz * 16 + cell % 16

    entries_five = sources_five.T.reshape(1, 128)
    entries_four = sources_four.T.reshape(1, 16)
    octants = jnp.arange(8, dtype=jnp.int32)[:, None]
    children = (8 * entries_four + octants).reshape(1, 128)
    index = where_held(jnp.concatenate([entries_five, children], axis=1))
    cls_coarse = jnp.concatenate(
        [classes_five.T, classes_four.T, jnp.full((LIST, 110), KINDS, jnp.int32)], axis=1
    )

    sevens = [
        near(0, below, lo, hi, src_seven, cls_seven, maps),
        near(1, below, lo, hi, src_seven, cls_seven, maps),
        near(2, lo, hi, above, src_seven, cls_seven, maps),
        near(3, lo, hi, above, src_seven, cls_seven, maps),
    ]
    far_six = middle(below, above, six, up, src_six, classes_six.T, maps)
    return last(tables, index, cls_coarse, up, down, far_six, sevens, maps).T


def solution(mesh):
    in_specs = (
        P(("cells", "sub"), None),
        P(("cells", "sub")),
        P(),
        P(),
        P(),
        P(("cells", "sub"), None),
        P(("cells", "sub"), None),
        P(("cells", "sub"), None),
        P(("cells", "sub"), None),
        P(("cells", "sub"), None),
        P(("cells", "sub"), None),
        P(("cells", "sub"), None),
        P(("cells", "sub"), None),
    )
    out_specs = P(("cells", "sub"), None)
    return jax.shard_map(body, mesh=mesh, in_specs=in_specs, out_specs=out_specs, check_vma=False)
```

time: 402 us -> 122 us (0.30); the launches traced: 396 us -> 120 us
  local copies, waits for them, and re-layouts: 147 us -> 17.1 us
  other arithmetic: 103 us -> 3.12 us
  blocking collectives: 75.2 us -> 0 us
  Pallas kernels: 0 us -> 66.4 us
  matrix products: 29.4 us -> 0 us
  starting transfers between devices: 14.5 us -> 31 us
  between operations: 14.4 us -> 0.52 us
  loops' own time: 11.4 us -> 0 us
    gather x64 -> x0, local copies, waits for them, and re-layouts: 125 us -> none  [one_block(): picked = jnp.take(table, index_rows[:, entry], axis=0).astype(jnp.float32)]
    convert_element_type x38 -> x0, other arithmetic: 75.5 us -> none  [the longest x5 47.1 us: one_block(): grouped = total.astype(jnp.bfloat16).reshape(blocked, kinds * width)]
    all_gather x1 -> x0, blocking collectives: 75.2 us -> none  [body(): lax.all_gather(multi_four, ('cells', 'sub'), axis=0, tiled=True)]
    pallas_call x0 -> x7, Pallas kernels: none -> 66.4 us  [the longest x4 39.1 us: near(): pl.pallas_call(functools.partial(near_body, block), out_shape=jax.ShapeDt...]
    dot_general x8 -> x0, matrix products: 29.4 us -> none  [the longest x3 16.4 us: descend(): spread = jnp.dot(parents, downward_maps, preferred_element_type=jnp.float32)]
    ppermute x0 -> x14, starting transfers between devices: none -> 23.9 us  [turned(): return lax.ppermute(value, axis, pairs)]
    gather x40 -> x0, other arithmetic: 14 us -> none
    another operation x1 -> x0, loops' own time: 11.4 us -> none  [translate(): lax.map(one_block, (indices.reshape(-1, blocked, entries), classes.reshap...]
  transfers between devices with their start and end apart: 5 -> 16, of which waited for: 0 -> 2; matrix products, arithmetic and copies ran while one was open for 57% -> 12% of each run, Pallas kernels for 0% -> 41%
where the time goes in v1:
time: 122 us; the launch traced here: 120 us
  Pallas kernels  66.4 us (54%)
  starting transfers between devices  31 us (25%)
  local copies, waits for them, and re-layouts  17.1 us (14%)
  other arithmetic  3.12 us (3%)
  waiting for transfers between devices  2.16 us (2%)
    pallas_call x4, Pallas kernels, near(): pl.pallas_call(functools.partial(near_body, block), out_shape=jax.ShapeDt...  39.1 us
    ppermute x14, starting transfers between devices, turned(): return lax.ppermute(value, axis, pairs)  23.9 us
    pallas_call x1, Pallas kernels, last(): pl.pallas_call(last_body, out_shape=jax.ShapeDtypeStruct((F, 1024), BF),...  14.5 us
    reshape x3, local copies, waits for them, and re-layouts, body(): down = downward_maps.reshape(F, 8, F).transpose(2, 1, 0).reshape(F, 8 * F)  12.4 us
    pallas_call x1, Pallas kernels, middle(): pl.pallas_call(middle_body, out_shape=jax.ShapeDtypeStruct((F, 128), F32)...  9.82 us
    ppermute x2, starting transfers between devices, shifted(): lax.ppermute(value, axis, [(source, source + steps) for source in range(f...  7.14 us
    unnamed x34, local copies, waits for them, and re-layouts  3.53 us
    pallas_call x1, Pallas kernels, rise(): pl.pallas_call(rise_body, out_shape=(jax.ShapeDtypeStruct((F, 128), BF),...  3 us
  transfers between devices with their start and end apart: 16, of which 2 were waited for; matrix products, arithmetic and copies ran while one was open for 12% of the time, Pallas kernels for 41%

profile of v1, /device:TPU:1, one launch (start us, length us, event | category | flops | bytes accessed | tf_op | source)
XLA Modules:
  0.0 120.3 jit_solution(6314103233953193626)
XLA Ops:
  0.0 0.8 broadcast_compare_fusion
  0.8 1.1 select_bitcast_fusion
  2.0 0.0 copy-start.8
  2.0 0.0 copy-start.11
  2.0 0.0 copy-start.6
  2.0 0.0 copy-start.7
  2.1 3.0 %rise.1 = (bf16[296,128]{1,0:T(8,128)(2,1)S(1)}, bf16[16,296]{1,0:T(8,128)(2,1)S(1)}) custom-call(bf16[296,512]{1,0:T(8,128)(2,1)S(1)} %get-tuple-element.10.lo_ref.b_ref.a_ref, bf16[296,512]{1,0:T(8,128)(2,1)S(1)} %get-tuple-element.9.hi_ref.c_ref.b_ref, bf16[296,2368]{1,0:T(8,128)(2,1)S(1)} %bitcast.41), custom_call_target="tpu_custom_call" | custom-call | flops 2000000000 | bytes 3000000 | tf_op jit(solution)/shard_map/rise/pallas_call | solution.py:56
  5.1 6.5 %collective-permute-start = (bf16[16,296]{1,0:T(8,128)(2,1)S(1)}, bf16[16,296]{1,0:T(8,128)(2,1)S(1)}, u32[]{:S(2)}, u32[]{:S(2)}) collective-permute-start(bf16[16,296]{1,0:T(8,128)(2,1)S(1)} %get-tuple-element.7), channel_id=1, source_target_pairs={{0,224},{4,228},{8,232},{12,236},{16,240},{20,244},{24,248},{28,25... | collective-permute-start | bytes 28424 | tf_op jit(solution)/shard_map/ppermute | solution.py:294
  11.5 3.1 %collective-permute-start.14 = (bf16[296,512]{1,0:T(8,128)(2,1)S(1)}, bf16[296,512]{1,0:T(8,128)(2,1)}, u32[]{:S(2)}, u32[]{:S(2)}) collective-permute-start(bf16[296,512]{1,0:T(8,128)(2,1)S(1)} %get-tuple-element.9.hi_ref.c_ref.b_ref), channel_id=1, source_target_pairs={{0,1},{1,2},{2,3},{3,4},{4,5},{5,6},{6,7},{7,8},{8,9},{9,10},{10,1... | collective-permute-start | bytes 909320 | tf_op jit(solution)/shard_map/ppermute | solution.py:285
  14.6 4.0 %collective-permute-start.15 = (bf16[296,512]{1,0:T(8,128)(2,1)S(1)}, bf16[296,512]{1,0:T(8,128)(2,1)}, u32[]{:S(2)}, u32[]{:S(2)}) collective-permute-start(bf16[296,512]{1,0:T(8,128)(2,1)S(1)} %get-tuple-element.10.lo_ref.b_ref.a_ref), channel_id=1, source_target_pairs={{1,0},{2,1},{3,2},{4,3},{5,4},{6,5},{7,6},{8,7},{9,8},{10,9},{11,1... | collective-permute-start | bytes 909320 | tf_op jit(solution)/shard_map/ppermute | solution.py:285
  18.7 0.1 concatenate.66
  18.8 0.1 copy.19
  18.9 0.1 mul.77
  19.0 0.1 concatenate.67
  19.0 0.1 copy.20
  19.1 0.1 pad.2.clone
  19.2 0.0 copy-done.6
  19.2 0.1 add_add_fusion.cls_ref
  19.3 1.8 %collective-permute-start.1 = (bf16[2,16,296]{2,1,0:T(8,128)(2,1)S(1)}, bf16[2,16,296]{2,1,0:T(8,128)(2,1)S(1)}, u32[]{:S(2)}, u32[]{:S(2)}) collective-permute-start(bf16[2,16,296]{2,1,0:T(8,128)(2,1)S(1)} %pad_maximum_fusion.2), channel_id=1, source_target_pairs={{0,96},{4,100},{8,104},{12,108},{16,112},{20,116},{24,120},{28,124... | collective-permute-start | bytes 56840 | tf_op jit(solution)/shard_map/ppermute | solution.py:294
  21.2 2.8 %collective-permute-start.3 = (bf16[3,16,296]{2,1,0:T(8,128)(2,1)S(1)}, bf16[3,16,296]{2,1,0:T(8,128)(2,1)S(1)}, u32[]{:S(2)}, u32[]{:S(2)}) collective-permute-start(bf16[3,16,296]{2,1,0:T(8,128)(2,1)S(1)} %pad_maximum_fusion.1), channel_id=1, source_target_pairs={{0,160},{4,164},{8,168},{12,172},{16,176},{20,180},{24,184},{28,18... | collective-permute-start | bytes 85256 | tf_op jit(solution)/shard_map/ppermute | solution.py:294
  24.0 1.1 collective-permute-done.1
  25.1 1.0 collective-permute-done.3
  26.2 0.7 copy.18
  26.9 1.0 collective-permute-start.6
  27.9 2.6 %collective-permute-start.5 = (bf16[296,128]{1,0:T(8,128)(2,1)}, bf16[296,128]{1,0:T(8,128)(2,1)}, u32[]{:S(2)}, u32[]{:S(2)}) collective-permute-start(bf16[296,128]{1,0:T(8,128)(2,1)} %bitcast.6), channel_id=1, source_target_pairs={{0,16},{4,20},{8,24},{12,28},{16,0},{20,4},{24,8},{28,12},{32,48},... | collective-permute-start | bytes 227336 | tf_op jit(solution)/shard_map/ppermute | solution.py:294
  30.6 1.1 collective-permute-start.4
  31.6 0.1 fusion.2.index_ref
  31.7 4.7 %reshape.712 = bf16[296,8,296]{2,1,0:T(8,128)(2,1)} reshape(bf16[296,2368]{1,0:T(8,128)(2,1)} %param.17) | data formatting | bytes 2803712 | tf_op jit(solution)/shard_map/reshape | solution.py:320
  36.4 4.4 %copy.21 = bf16[296,8,296]{0,1,2:T(8,128)(2,1)} copy(bf16[296,8,296]{2,1,0:T(8,128)(2,1)} %reshape.712) | data formatting | bytes 2803712 | tf_op jit(solution)/shard_map/reshape | solution.py:320
  40.8 3.2 %reshape.713.down_ref = bf16[296,2368]{1,0:T(8,128)(2,1)S(1)} reshape(bf16[296,8,296]{2,1,0:T(8,128)(2,1)} %bitcast.49) | data formatting | bytes 2803712 | tf_op jit(solution)/shard_map/reshape | solution.py:320
  44.1 1.0 pad_maximum_fusion.t0
  45.1 1.1 collective-permute-start.7
  46.2 0.2 collective-permute-start.8
  46.4 0.6 collective-permute-start.9
  47.0 5.3 %collective-permute-start.10 = (bf16[296,512]{1,0:T(8,128)(2,1)S(1)}, bf16[296,512]{1,0:T(8,128)(2,1)S(1)}, u32[]{:S(2)}, u32[]{:S(2)}) collective-permute-start(bf16[296,512]{1,0:T(8,128)(2,1)S(1)} %pad_maximum_fusion.t0), channel_id=1, source_target_pairs={{0,4},{4,0},{8,12},{12,8},{16,20},{20,16},{24,28},{28,24},{32,36},... | collective-permute-start | bytes 909320 | tf_op jit(solution)/shard_map/ppermute | solution.py:294
  52.3 2.6 %copy-done = bf16[9472,296]{0,1:T(8,128)(2,1)S(1)} copy-done((bf16[9472,296]{0,1:T(8,128)(2,1)S(1)}, bf16[9472,296]{0,1:T(8,128)(2,1)}, u32[]{:S(2)}) %copy-start) | copy-done | bytes 5607448
  54.9 0.8 copy-done.2
  55.7 9.7 %near0.1.s0 = f32[296,256]{1,0:T(8,128)S(1)} custom-call(bf16[296,512]{1,0:T(8,128)(2,1)} %collective-permute-done.14.below_ref.a_ref, bf16[296,512]{1,0:T(8,128)(2,1)S(1)} %get-tuple-element.10.lo_ref.b_ref.a_ref, bf16[296,512]{1,0:T(8,128)(2,1)S(1)} %get-tuple-element.9.hi_ref.c_ref.b_ref, s32[8,1024]{1,0:T(8,128)S(1)} %subtract_bitcast_fusion.src_ref, ...), custom_call_target="tpu_custom_call" | custom-call | flops 6000000000 | bytes 6000000 | tf_op jit(solution)/shard_map/near0/pallas_call | solution.py:153
  65.4 9.7 %near1.1.s1 = f32[296,256]{1,0:T(8,128)S(1)} custom-call(bf16[296,512]{1,0:T(8,128)(2,1)} %collective-permute-done.14.below_ref.a_ref, bf16[296,512]{1,0:T(8,128)(2,1)S(1)} %get-tuple-element.10.lo_ref.b_ref.a_ref, bf16[296,512]{1,0:T(8,128)(2,1)S(1)} %get-tuple-element.9.hi_ref.c_ref.b_ref, s32[8,1024]{1,0:T(8,128)S(1)} %subtract_bitcast_fusion.src_ref, ...), custom_call_target="tpu_custom_call" | custom-call | flops 6000000000 | bytes 6000000 | tf_op jit(solution)/shard_map/near1/pallas_call | solution.py:153
  75.1 0.0 slice-start
  75.1 9.8 %near2.1.s2 = f32[296,256]{1,0:T(8,128)S(1)} custom-call(bf16[296,512]{1,0:T(8,128)(2,1)S(1)} %get-tuple-element.10.lo_ref.b_ref.a_ref, bf16[296,512]{1,0:T(8,128)(2,1)S(1)} %get-tuple-element.9.hi_ref.c_ref.b_ref, bf16[296,512]{1,0:T(8,128)(2,1)} %collective-permute-done.15.above_ref.c_ref, s32[8,1024]{1,0:T(8,128)S(1)} %subtract_bitcast_fusion.src_ref, ...), custom_call_target="tpu_custom_call" | custom-call | flops 6000000000 | bytes 6000000 | tf_op jit(solution)/shard_map/near2/pallas_call | solution.py:153
  85.0 0.0 slice-start.1
  85.0 9.8 %near3.1.s3 = f32[296,256]{1,0:T(8,128)S(1)} custom-call(bf16[296,512]{1,0:T(8,128)(2,1)S(1)} %get-tuple-element.10.lo_ref.b_ref.a_ref, bf16[296,512]{1,0:T(8,128)(2,1)S(1)} %get-tuple-element.9.hi_ref.c_ref.b_ref, bf16[296,512]{1,0:T(8,128)(2,1)} %collective-permute-done.15.above_ref.c_ref, s32[8,1024]{1,0:T(8,128)S(1)} %subtract_bitcast_fusion.src_ref, ...), custom_call_target="tpu_custom_call" | custom-call | flops 6000000000 | bytes 6000000 | tf_op jit(solution)/shard_map/near3/pallas_call | solution.py:153
  94.8 0.1 collective-permute-start.11
  95.0 0.5 collective-permute-start.12
  95.5 0.3 collective-permute-start.13
  95.8 9.8 %middle.1.six_ref = f32[296,128]{1,0:T(8,128)S(1)} custom-call(bf16[296,512]{1,0:T(8,128)(2,1)} %collective-permute-done.14.below_ref.a_ref, bf16[296,512]{1,0:T(8,128)(2,1)} %collective-permute-done.15.above_ref.c_ref, bf16[296,128]{1,0:T(8,128)(2,1)S(1)} %copy-done.5, bf16[296,2368]{1,0:T(8,128)(2,1)S(1)} %bitcast.42, s32[8,128]{1,0:T(8,128)S(1)} %fusion.src_ref, ...), custom_call_target="tpu_custom_call" | custom-call | flops 4000000000 | bytes 6000000 | tf_op jit(solution)/shard_map/middle/pallas_call | solution.py:184
  105.6 14.5 %last.1 = bf16[296,1024]{1,0:T(8,128)(2,1)} custom-call(bf16[296,512]{1,0:T(8,128)(2,1)S(1)} %pad_maximum_fusion.t0, bf16[296,512]{1,0:T(8,128)(2,1)S(1)} %collective-permute-done.7.t1, bf16[296,512]{1,0:T(8,128)(2,1)S(1)} %collective-permute-done.8.t2, bf16[296,512]{1,0:T(8,128)(2,1)S(1)} %collective-permute-done.9.t3, ...), custom_call_target="tpu_custom_call" | custom-call | flops 8000000000 | bytes 12000000 | tf_op jit(solution)/shard_map/last/pallas_call | solution.py:263
  (50 shorter events, 0.2 us)
Async XLA Ops:
  0.0 2.0 %copy-start.1 = (bf16[2368,296]{0,1:T(8,128)(2,1)S(1)}, bf16[2368,296]{0,1:T(8,128)(2,1)}, u32[]{:S(2)}) copy-start(bf16[2368,296]{0,1:T(8,128)(2,1)} %param.15) | copy-start | bytes 4205572
  2.0 16.7 %copy-start.8 = (s32[16,8]{0,1:T(8,128)S(1)}, s32[16,8]{0,1:T(8,128)}, u32[]{:S(2)}) copy-start(s32[16,8]{0,1:T(8,128)} %param.22) | copy-start | bytes 1540
  2.0 16.8 %copy-start.11 = (s32[2,8]{1,0:T(2,128)S(1)}, s32[2,8]{1,0:T(2,128)}, u32[]{:S(2)}) copy-start(s32[2,8]{1,0:T(2,128)} %param.24) | copy-start | bytes 196
  2.0 17.0 %copy-start.10 = (s32[2,8]{1,0:T(2,128)S(1)}, s32[2,8]{1,0:T(2,128)}, u32[]{:S(2)}) copy-start(s32[2,8]{1,0:T(2,128)} %param.25) | copy-start | bytes 196
  2.0 17.2 %copy-start.9 = (s32[128,8]{0,1:T(8,128)S(1)}, s32[128,8]{0,1:T(8,128)}, u32[]{:S(2)}) copy-start(s32[128,8]{0,1:T(8,128)} %param.20) | copy-start | bytes 12292
  2.0 17.2 %copy-start.6 = (s32[1024,8]{0,1:T(8,128)S(1)}, s32[1024,8]{0,1:T(8,128)}, u32[]{:S(2)}) copy-start(s32[1024,8]{0,1:T(8,128)} %param.18) | copy-start | bytes 98308
  2.0 17.2 %copy-start.7 = (s32[16,8]{0,1:T(8,128)S(1)}, s32[16,8]{0,1:T(8,128)}, u32[]{:S(2)}) copy-start(s32[16,8]{0,1:T(8,128)} %param.23) | copy-start | bytes 1540
  5.1 31.3 %copy-start.4 = (bf16[296,128]{1,0:T(8,128)(2,1)}, bf16[296,128]{1,0:T(8,128)(2,1)S(1)}, u32[]{:S(2)}) copy-start(bf16[296,128]{1,0:T(8,128)(2,1)S(1)} %get-tuple-element.8.six_ref) | copy-start | bytes 227332
  5.1 14.3 %collective-permute-start = (bf16[16,296]{1,0:T(8,128)(2,1)S(1)}, bf16[16,296]{1,0:T(8,128)(2,1)S(1)}, u32[]{:S(2)}, u32[]{:S(2)}) collective-permute-start(bf16[16,296]{1,0:T(8,128)(2,1)S(1)} %get-tuple-element.7), channel_id=1, source_target_pairs={{0,224},{4,228},{8,232},{12,236},{16,240},{20,244},{24,248},{28,25... | collective-permute-start | bytes 28424 | tf_op jit(solution)/shard_map/ppermute | solution.py:294
  11.5 9.6 %collective-permute-start.2 = (bf16[16,296]{1,0:T(8,128)(2,1)S(1)}, bf16[16,296]{1,0:T(8,128)(2,1)S(1)}, u32[]{:S(2)}, u32[]{:S(2)}) collective-permute-start(bf16[16,296]{1,0:T(8,128)(2,1)S(1)} %get-tuple-element.7), channel_id=1, source_target_pairs={{0,32},{4,36},{8,40},{12,44},{16,48},{20,52},{24,56},{28,60},{32,6... | collective-permute-start | bytes 28424 | tf_op jit(solution)/shard_map/ppermute | solution.py:294
  11.5 35.5 %collective-permute-start.14 = (bf16[296,512]{1,0:T(8,128)(2,1)S(1)}, bf16[296,512]{1,0:T(8,128)(2,1)}, u32[]{:S(2)}, u32[]{:S(2)}) collective-permute-start(bf16[296,512]{1,0:T(8,128)(2,1)S(1)} %get-tuple-element.9.hi_ref.c_ref.b_ref), channel_id=1, source_target_pairs={{0,1},{1,2},{2,3},{3,4},{4,5},{5,6},{6,7},{7,8},{8,9},{9,10},{10,1... | collective-permute-start | bytes 909320 | tf_op jit(solution)/shard_map/ppermute | solution.py:285
  14.6 60.5 %collective-permute-start.15 = (bf16[296,512]{1,0:T(8,128)(2,1)S(1)}, bf16[296,512]{1,0:T(8,128)(2,1)}, u32[]{:S(2)}, u32[]{:S(2)}) collective-permute-start(bf16[296,512]{1,0:T(8,128)(2,1)S(1)} %get-tuple-element.10.lo_ref.b_ref.a_ref), channel_id=1, source_target_pairs={{1,0},{2,1},{3,2},{4,3},{5,4},{6,5},{7,6},{8,7},{9,8},{10,9},{11,1... | collective-permute-start | bytes 909320 | tf_op jit(solution)/shard_map/ppermute | solution.py:285
  19.3 5.8 %collective-permute-start.1 = (bf16[2,16,296]{2,1,0:T(8,128)(2,1)S(1)}, bf16[2,16,296]{2,1,0:T(8,128)(2,1)S(1)}, u32[]{:S(2)}, u32[]{:S(2)}) collective-permute-start(bf16[2,16,296]{2,1,0:T(8,128)(2,1)S(1)} %pad_maximum_fusion.2), channel_id=1, source_target_pairs={{0,96},{4,100},{8,104},{12,108},{16,112},{20,116},{24,120},{28,124... | collective-permute-start | bytes 56840 | tf_op jit(solution)/shard_map/ppermute | solution.py:294
  21.2 5.0 %collective-permute-start.3 = (bf16[3,16,296]{2,1,0:T(8,128)(2,1)S(1)}, bf16[3,16,296]{2,1,0:T(8,128)(2,1)S(1)}, u32[]{:S(2)}, u32[]{:S(2)}) collective-permute-start(bf16[3,16,296]{2,1,0:T(8,128)(2,1)S(1)} %pad_maximum_fusion.1), channel_id=1, source_target_pairs={{0,160},{4,164},{8,168},{12,172},{16,176},{20,180},{24,184},{28,18... | collective-permute-start | bytes 85256 | tf_op jit(solution)/shard_map/ppermute | solution.py:294
  26.9 17.2 %collective-permute-start.6 = (bf16[296,128]{1,0:T(8,128)(2,1)}, bf16[296,128]{1,0:T(8,128)(2,1)}, u32[]{:S(2)}, u32[]{:S(2)}) collective-permute-start(bf16[296,128]{1,0:T(8,128)(2,1)} %bitcast.6), channel_id=1, source_target_pairs={{0,8},{4,12},{8,16},{12,20},{16,24},{20,28},{24,0},{28,4},{32,40},... | collective-permute-start | bytes 227336 | tf_op jit(solution)/shard_map/ppermute | solution.py:294
  27.9 16.1 %collective-permute-start.5 = (bf16[296,128]{1,0:T(8,128)(2,1)}, bf16[296,128]{1,0:T(8,128)(2,1)}, u32[]{:S(2)}, u32[]{:S(2)}) collective-permute-start(bf16[296,128]{1,0:T(8,128)(2,1)} %bitcast.6), channel_id=1, source_target_pairs={{0,16},{4,20},{8,24},{12,28},{16,0},{20,4},{24,8},{28,12},{32,48},... | collective-permute-start | bytes 227336 | tf_op jit(solution)/shard_map/ppermute | solution.py:294
  30.6 13.5 %collective-permute-start.4 = (bf16[296,128]{1,0:T(8,128)(2,1)}, bf16[296,128]{1,0:T(8,128)(2,1)}, u32[]{:S(2)}, u32[]{:S(2)}) collective-permute-start(bf16[296,128]{1,0:T(8,128)(2,1)} %bitcast.6), channel_id=1, source_target_pairs={{0,24},{4,28},{8,0},{12,4},{16,8},{20,12},{24,16},{28,20},{32,56},... | collective-permute-start | bytes 227336 | tf_op jit(solution)/shard_map/ppermute | solution.py:294
  45.1 49.7 %collective-permute-start.7 = (bf16[296,512]{1,0:T(8,128)(2,1)S(1)}, bf16[296,512]{1,0:T(8,128)(2,1)S(1)}, u32[]{:S(2)}, u32[]{:S(2)}) collective-permute-start(bf16[296,512]{1,0:T(8,128)(2,1)S(1)} %pad_maximum_fusion.t0), channel_id=1, source_target_pairs={{0,3},{1,0},{2,1},{3,2},{4,7},{5,4},{6,5},{7,6},{8,11},{9,8},{10,9... | collective-permute-start | bytes 909320 | tf_op jit(solution)/shard_map/ppermute | solution.py:294
  46.2 48.7 %collective-permute-start.8 = (bf16[296,512]{1,0:T(8,128)(2,1)S(1)}, bf16[296,512]{1,0:T(8,128)(2,1)S(1)}, u32[]{:S(2)}, u32[]{:S(2)}) collective-permute-start(bf16[296,512]{1,0:T(8,128)(2,1)S(1)} %pad_maximum_fusion.t0), channel_id=1, source_target_pairs={{0,2},{1,3},{2,0},{3,1},{4,6},{5,7},{6,4},{7,5},{8,10},{9,11},{10,... | collective-permute-start | bytes 909320 | tf_op jit(solution)/shard_map/ppermute | solution.py:294
  46.4 49.0 %collective-permute-start.9 = (bf16[296,512]{1,0:T(8,128)(2,1)S(1)}, bf16[296,512]{1,0:T(8,128)(2,1)S(1)}, u32[]{:S(2)}, u32[]{:S(2)}) collective-permute-start(bf16[296,512]{1,0:T(8,128)(2,1)S(1)} %pad_maximum_fusion.t0), channel_id=1, source_target_pairs={{0,1},{1,2},{2,3},{3,0},{4,5},{5,6},{6,7},{7,4},{8,9},{9,10},{10,1... | collective-permute-start | bytes 909320 | tf_op jit(solution)/shard_map/ppermute | solution.py:294
  47.0 58.6 %collective-permute-start.10 = (bf16[296,512]{1,0:T(8,128)(2,1)S(1)}, bf16[296,512]{1,0:T(8,128)(2,1)S(1)}, u32[]{:S(2)}, u32[]{:S(2)}) collective-permute-start(bf16[296,512]{1,0:T(8,128)(2,1)S(1)} %pad_maximum_fusion.t0), channel_id=1, source_target_pairs={{0,4},{4,0},{8,12},{12,8},{16,20},{20,16},{24,28},{28,24},{32,36},... | collective-permute-start | bytes 909320 | tf_op jit(solution)/shard_map/ppermute | solution.py:294
  52.3 2.6 %copy-start = (bf16[9472,296]{0,1:T(8,128)(2,1)S(1)}, bf16[9472,296]{0,1:T(8,128)(2,1)}, u32[]{:S(2)}) copy-start(bf16[9472,296]{0,1:T(8,128)(2,1)} %param.16) | copy-start | bytes 16822276
  54.9 0.8 copy-start.2
  75.1 20.6 %slice-start = ((s8[5607424]{0:T(1024)(128)(4,1)}), s8[4194304]{0:T(1024)(128)(4,1)S(1)}, s32[]{:S(2)}) async-start(s8[5607424]{0:T(1024)(128)(4,1)} %bitcast.37), calls=%async_computation | async-start | bytes 8388608
  85.0 10.8 %slice-start.1 = ((s8[5607424]{0:T(1024)(128)(4,1)}), s8[1413120]{0:T(1024)(128)(4,1)S(1)}, s32[]{:S(2)}) async-start(s8[5607424]{0:T(1024)(128)(4,1)} %bitcast.37), calls=%async_computation.1 | async-start | bytes 2826240
  85.0 10.8 %copy-start.3 = (s32[128,8]{0,1:T(8,128)S(1)}, s32[128,8]{0,1:T(8,128)}, u32[]{:S(2)}) copy-start(s32[128,8]{0,1:T(8,128)} %param.21) | copy-start | bytes 12292
  85.0 10.8 %copy-start.5 = (bf16[296,128]{1,0:T(8,128)(2,1)S(1)}, bf16[296,128]{1,0:T(8,128)(2,1)}, u32[]{:S(2)}) copy-start(bf16[296,128]{1,0:T(8,128)(2,1)} %copy-done.4) | copy-start | bytes 227332
  94.8 10.8 %collective-permute-start.11 = (bf16[296,512]{1,0:T(8,128)(2,1)S(1)}, bf16[296,512]{1,0:T(8,128)(2,1)S(1)}, u32[]{:S(2)}, u32[]{:S(2)}) collective-permute-start(bf16[296,512]{1,0:T(8,128)(2,1)S(1)} %collective-permute-done.7.t1), channel_id=1, source_target_pairs={{0,4},{4,0},{8,12},{12,8},{16,20},{20,16},{24,28},{28,24},{32,36},... | collective-permute-start | bytes 909320 | tf_op jit(solution)/shard_map/ppermute | solution.py:294
  95.0 10.7 %collective-permute-start.12 = (bf16[296,512]{1,0:T(8,128)(2,1)S(1)}, bf16[296,512]{1,0:T(8,128)(2,1)S(1)}, u32[]{:S(2)}, u32[]{:S(2)}) collective-permute-start(bf16[296,512]{1,0:T(8,128)(2,1)S(1)} %collective-permute-done.8.t2), channel_id=1, source_target_pairs={{0,4},{4,0},{8,12},{12,8},{16,20},{20,16},{24,28},{28,24},{32,36},... | collective-permute-start | bytes 909320 | tf_op jit(solution)/shard_map/ppermute | solution.py:294
  95.5 10.2 %collective-permute-start.13 = (bf16[296,512]{1,0:T(8,128)(2,1)S(1)}, bf16[296,512]{1,0:T(8,128)(2,1)S(1)}, u32[]{:S(2)}, u32[]{:S(2)}) collective-permute-start(bf16[296,512]{1,0:T(8,128)(2,1)S(1)} %collective-permute-done.9.t3), channel_id=1, source_target_pairs={{0,4},{4,0},{8,12},{12,8},{16,20},{20,16},{24,28},{28,24},{32,36},... | collective-permute-start | bytes 909320 | tf_op jit(solution)/shard_map/ppermute | solution.py:294

commit v2 on v1

v2 whole, which is shorter than its diff:
```python
import functools

import jax
import jax.numpy as jnp
from jax import lax
from jax.experimental import pallas as pl
from jax.experimental.pallas import tpu as pltpu
from jax.sharding import PartitionSpec as P

F = 296
KINDS = 32
LIST = 8
BF = jnp.bfloat16
F32 = jnp.float32
VM = pl.BlockSpec(memory_space=pltpu.VMEM)


def dot(a, b):
    return jnp.dot(a, b, preferred_element_type=F32)


def onehot(rel, depth):
    count = rel.shape[1]
    rows = lax.broadcasted_iota(jnp.int32, (depth, count), 0)
    return jnp.where(rows == rel, 1.0, 0.0).astype(BF)


def split_octants(children, first, width):
    count = children.shape[1]
    source = lax.broadcasted_iota(jnp.int32, (count, 2 * width), 0)
    place = lax.broadcasted_iota(jnp.int32, (count, 2 * width), 1)
    second = (place >= width).astype(jnp.int32)
    wanted = 8 * (place - width * second) + first + second
    return dot(children, jnp.where(source == wanted, 1.0, 0.0).astype(BF))


def ascend(children, up_ref, stack):
    for pair in range(4):
        both = split_octants(children, 2 * pair, 128)
        stack[2 * pair * F : (2 * pair + 1) * F, :] = both[:, :128]
        stack[(2 * pair + 1) * F : (2 * pair + 2) * F, :] = both[:, 128:]
    return dot(up_ref[...], stack[...].astype(BF))


def rise_body(leaf_ref, held_ref, up_ref, lo_ref, hi_ref, six_ref, five_ref, stack):
    held = jnp.concatenate([held_ref[r : r + 1, :] for r in range(8)], axis=1)
    children = leaf_ref[...] * jnp.where(held > 0, 1.0, 0.0).astype(BF)
    lo_ref[...] = children[:, :512]
    hi_ref[...] = children[:, 512:]
    six = ascend(children, up_ref, stack).astype(BF)
    six_ref[...] = six
    five = ascend(six, up_ref, stack)
    five_ref[...] = five.T[:16, :].astype(BF)


def rise(leaves, held, up):
    return pl.pallas_call(
        rise_body,
        out_shape=(
            jax.ShapeDtypeStruct((F, 512), BF),
            jax.ShapeDtypeStruct((F, 512), BF),
            jax.ShapeDtypeStruct((F, 128), BF),
            jax.ShapeDtypeStruct((16, F), BF),
        ),
        in_specs=[VM] * 3,
        out_specs=(VM,) * 4,
        scratch_shapes=[pltpu.VMEM((8 * F, 128), F32)],
        compiler_params=pltpu.CompilerParams(vmem_limit_bytes=16 * 2**20),
        cost_estimate=pl.CostEstimate(flops=2 * 10**9, bytes_accessed=3 * 10**6, transcendentals=0),
        name="rise",
    )(leaves, held, up)


def spread(value, even, odd, slot, lanes):
    blank = jnp.zeros((8, value.shape[1]), F32)
    even[slot, :, lanes] = jnp.concatenate([value, blank], axis=0).astype(BF)
    odd[slot, :, lanes] = jnp.concatenate([blank, value], axis=0).astype(BF)


def stack_pair(grouped, row, lanes, even_tile, odd_tile):
    for i in range(18):
        grouped[pl.ds(row + 16 * i, 16), lanes] = even_tile(i)
    grouped[pl.ds(row + 288, 16), lanes] = even_tile(18) + odd_tile(0)
    for i in range(1, 19):
        grouped[pl.ds(row + 288 + 16 * i, 16), lanes] = odd_tile(i)


def group(labels, even, odd, grouped, p):
    wide = [jnp.broadcast_to(label, (16, 256)) for label in labels]

    def masks(kind):
        return [jnp.where(label == kind, 1.0, 0.0).astype(BF) for label in wide]

    first, second = masks(2 * p), masks(2 * p + 1)

    def total(ref, mask, i):
        terms = [ref[j, 16 * i : 16 * i + 16, :] * mask[j] for j in range(LIST)]
        while len(terms) > 1:
            terms = [terms[q] + terms[q + 1] for q in range(0, len(terms), 2)]
        return terms[0]

    stack_pair(
        grouped,
        pl.multiple_of(p * 2 * F, 16),
        slice(None),
        lambda i: total(even, first, i),
        lambda i: total(odd, second, i),
    )


def near_body(block, count, a_ref, b_ref, c_ref, src_ref, cls_ref, maps_ref, out_ref, window, even, odd, grouped):
    side = block % 2
    for k in range(4 + count):
        half = k + side
        window[:, 256 * k : 256 * k + 256] = (a_ref, b_ref, c_ref)[half // 2][:, 256 * (half % 2) : 256 * (half % 2) + 256]

    def pick(i, carry):
        local, four = i // 2, i % 2
        base = pl.multiple_of(local * 256, 256)
        lanes = pl.ds(pl.multiple_of((block + local) * 256, 256), 256)
        start = (block + local) * 256
        wanted = [onehot(src_ref[pl.ds(4 * four + q, 1), lanes] - start, 1280) for q in range(4)]
        value = dot(window[:, pl.ds(base, 1280)], jnp.concatenate(wanted, axis=1))
        for q in range(4):
            spread(value[:, 256 * q : 256 * q + 256], even.at[local], odd.at[local], 4 * four + q, slice(None))
        return carry

    lax.fori_loop(0, 2 * count, pick, 0)

    def sums(i, carry):
        local, p = i // 16, i % 16
        lanes = pl.ds(pl.multiple_of((block + local) * 256, 256), 256)
        labels = [cls_ref[j : j + 1, lanes] for j in range(LIST)]
        group(labels, even.at[local], odd.at[local], grouped.at[local], p)
        return carry

    lax.fori_loop(0, 16 * count, sums, 0)

    def send(i, carry):
        out_ref[i] = dot(maps_ref[...], grouped[i])
        return carry

    lax.fori_loop(0, count, send, 0)


def near(block, count, a, b, c, src, cls, maps):
    return pl.pallas_call(
        functools.partial(near_body, block, count),
        out_shape=jax.ShapeDtypeStruct((count, F, 256), F32),
        in_specs=[VM] * 6,
        out_specs=VM,
        scratch_shapes=[
            pltpu.VMEM((F, 1024 + 256 * count), BF),
            pltpu.VMEM((count, LIST, F + 8, 256), BF),
            pltpu.VMEM((count, LIST, F + 8, 256), BF),
            pltpu.VMEM((count, KINDS * F, 256), BF),
        ],
        compiler_params=pltpu.CompilerParams(vmem_limit_bytes=(22 if count > 1 else 16) * 2**20),
        cost_estimate=pl.CostEstimate(flops=count * 6 * 10**9, bytes_accessed=6 * 10**6, transcendentals=0),
        name=f"near{block}",
    )(a, b, c, src, cls, maps)


def halo_body(below_ref, above_ref, up_ref, out_ref, stack):
    children = jnp.concatenate([below_ref[...], above_ref[...]], axis=1)
    out_ref[...] = ascend(children, up_ref, stack).astype(BF)


def halo_six(below, above, up):
    return pl.pallas_call(
        halo_body,
        out_shape=jax.ShapeDtypeStruct((F, 128), BF),
        in_specs=[VM] * 3,
        out_specs=VM,
        scratch_shapes=[pltpu.VMEM((8 * F, 128), F32)],
        compiler_params=pltpu.CompilerParams(vmem_limit_bytes=16 * 2**20),
        cost_estimate=pl.CostEstimate(flops=2 * 10**9, bytes_accessed=3 * 10**6, transcendentals=0),
        name="halo",
    )(below, above, up)


def flip_body(down_ref, out_ref):
    out_ref[...] = down_ref[...].T


def flip(down):
    return pl.pallas_call(
        flip_body,
        out_shape=jax.ShapeDtypeStruct((8 * F, F), BF),
        in_specs=[VM],
        out_specs=VM,
        compiler_params=pltpu.CompilerParams(vmem_limit_bytes=16 * 2**20),
        cost_estimate=pl.CostEstimate(flops=10**9, bytes_accessed=3 * 10**6, transcendentals=0),
        name="flip",
    )(down)


def last_body(
    t0, t1, t2, t3, t4, t5, t6, t7, index_ref, six_ref, halo_ref, src_ref, cls_ref, up_ref, down_ref,
    s0, s1, s2, maps_ref, out_ref,
    even, odd, grouped, stack, coarse, both, weave, fars, local,
):
    window = jnp.concatenate([six_ref[...], halo_ref[...]], axis=1)

    def pick(i, carry):
        wanted = jnp.concatenate([src_ref[pl.ds(2 * i, 1), :], src_ref[pl.ds(2 * i + 1, 1), :]], axis=1)
        value = dot(window, onehot(wanted, 256))
        for q in range(2):
            spread(value[:, 128 * q : 128 * q + 128], even, odd, 2 * i + q, slice(128, 256))
        return carry

    lax.fori_loop(0, LIST // 2, pick, 0)

    wanted = index_ref[...]
    picked = jnp.zeros((F, 256), F32)
    for k, table in enumerate((t0, t1, t2, t3, t4, t5, t6, t7)):
        picked += dot(table[...], onehot(wanted - 512 * k, 512))
    stack[...] = jnp.zeros(stack.shape, F32)
    for o in range(8):
        stack[o * F : (o + 1) * F, :16] = picked[:, 128 + 16 * o : 144 + 16 * o]
    four = dot(up_ref[...], stack[...].astype(BF)).astype(BF).astype(F32)
    blank = jnp.zeros((F, 110), F32)
    for j in range(LIST):
        value = jnp.concatenate([picked[:, 16 * j : 16 * j + 16], four[:, 2 * j : 2 * j + 2], blank], axis=1)
        spread(value, even, odd, j, slice(0, 128))

    def sums(p, carry):
        group([cls_ref[j : j + 1, :] for j in range(LIST)], even, odd, grouped, p)
        return carry

    lax.fori_loop(0, KINDS // 2, sums, 0)
    coarse[...] = dot(maps_ref[...], grouped[...])

    def fill(o, carry):
        row = lax.broadcasted_iota(jnp.int32, (128, 1024), 0)
        cell = lax.broadcasted_iota(jnp.int32, (128, 1024), 1)
        weave[pl.ds(pl.multiple_of(o * 128, 128), 128), :] = jnp.where(cell == 8 * row + o, 1.0, 0.0).astype(BF)
        return carry

    lax.fori_loop(0, 8, fill, 0)
    both[...] = jnp.zeros(both.shape, BF)
    lane = lax.broadcasted_iota(jnp.int32, (F, 128), 1)
    fars[0] = jnp.where(lane < 16, coarse[:, :128], 0.0)
    fars[1] = coarse[:, 128:]
    take = lax.broadcasted_iota(jnp.int32, (128, 128), 0) == lax.broadcasted_iota(jnp.int32, (128, 128), 1) + 16
    local[...] = dot(coarse[:, :128].astype(BF), jnp.where(take, 1.0, 0.0).astype(BF)).astype(BF)

    def woven(lanes):
        pieces = dot(both[...], weave[:, lanes])
        return pieces[:F, :] + pieces[304 : 304 + F, :]

    def fall(level, carry):
        children = dot(down_ref[...], local[...])
        for o in range(8):
            part = children[o * F : (o + 1) * F, :]
            high = part.astype(BF)
            both[:F, 128 * o : 128 * o + 128] = high
            both[304 : 304 + F, 128 * o : 128 * o + 128] = (part - high.astype(F32)).astype(BF)

        @pl.when(level < 2)
        def _():
            local[...] = (woven(slice(0, 128)) + fars[jnp.minimum(level, 1)]).astype(BF)

        return carry

    lax.fori_loop(0, 3, fall, 0)
    for q, seven in enumerate((s0.at[0], s1.at[0], s2.at[0], s2.at[1])):
        lanes = slice(256 * q, 256 * q + 256)
        out_ref[:, lanes] = (woven(lanes) + seven[...]).astype(BF)


def last(tables, index, six, halo, src, cls, up, down, sevens, maps):
    return pl.pallas_call(
        last_body,
        out_shape=jax.ShapeDtypeStruct((F, 1024), BF),
        in_specs=[VM] * 19,
        out_specs=VM,
        scratch_shapes=[
            pltpu.VMEM((LIST, F + 8, 256), BF),
            pltpu.VMEM((LIST, F + 8, 256), BF),
            pltpu.VMEM((KINDS * F, 256), BF),
            pltpu.VMEM((8 * F, 128), F32),
            pltpu.VMEM((F, 256), F32),
            pltpu.VMEM((608, 1024), BF),
            pltpu.VMEM((1024, 1024), BF),
            pltpu.VMEM((2, F, 128), F32),
            pltpu.VMEM((F, 128), BF),
        ],
        compiler_params=pltpu.CompilerParams(vmem_limit_bytes=24 * 2**20),
        cost_estimate=pl.CostEstimate(flops=8 * 10**9, bytes_accessed=12 * 10**6, transcendentals=0),
        name="last",
    )(*tables, index, six, halo, src, cls, up, down, *sevens, maps)


def shifted(value, axis, steps):
    count = lax.axis_size(axis)
    first, last_one = (max(0, -steps), min(count, count - steps))
    return lax.ppermute(value, axis, [(source, source + steps) for source in range(first, last_one)])


def turned(value, axis, size, stride, steps):
    pairs = []
    for source in range(lax.axis_size(axis)):
        position = (source // stride) % size
        target = source + ((position + steps) % size - position) * stride
        pairs.append((source, target))
    return lax.ppermute(value, axis, pairs)


along_z = lambda value, steps: turned(value, "cells", 8, 8, steps)
along_y = lambda value, steps: turned(value, "cells", 4, 2, steps)
along_core = lambda value, steps: turned(value, "cells", 2, 1, steps)
along_x = lambda value, steps: turned(value, "sub", 4, 1, steps)


def tie(*values):
    return lax.optimization_barrier(values)


def body(
    leaf_multipoles,
    occupancy,
    upward_maps,
    transfer_maps,
    downward_maps,
    sources_seven,
    classes_seven,
    sources_six,
    classes_six,
    sources_five,
    classes_five,
    sources_four,
    classes_four,
):
    leaves = leaf_multipoles.T
    up, maps = upward_maps.T, transfer_maps.T
    lo, hi, six, five = rise(leaves, occupancy.reshape(8, 128), up)
    below = shifted(hi, ("cells", "sub"), 1)
    above = shifted(lo, ("cells", "sub"), -1)

    cells, sub = lax.axis_index("cells"), lax.axis_index("sub")
    place = cells * 4 + sub
    src_seven = sources_seven.T - (place * 1024 - 512)
    cls_seven = classes_seven.T
    rel_six = sources_six.T - (place * 128 - 64)
    src_six = jnp.where(rel_six < 64, rel_six + 128, jnp.where(rel_six < 192, rel_six - 64, rel_six))

    down = flip(downward_maps)
    minus, plus = along_z(five, 1), along_z(five, -1)
    three = jnp.stack([minus, five, plus])
    three, near_lo = tie(three, lo)
    upper = along_z(three, -3)
    lower = along_z(three[1:], 3)
    seven_0 = near(0, 1, below, near_lo, hi, src_seven, cls_seven, maps)
    column = jnp.concatenate([lower, three, upper], axis=0).reshape(128, F).T
    column, seven_0, near_lo = tie(column, seven_0, near_lo)
    sides = along_y(column, -1), along_y(column, 2), along_y(column, 1)
    seven_1 = near(1, 1, below, near_lo, hi, src_seven, cls_seven, maps)
    plane = jnp.concatenate([column, *sides], axis=1)
    plane, seven_1, near_lo, near_up = tie(plane, seven_1, near_lo, up)
    tables = [plane, along_x(plane, -1), along_x(plane, 2), along_x(plane, 1)]
    halo = halo_six(below, above, near_up)
    seven_2 = near(2, 2, near_lo, hi, above, src_seven, cls_seven, maps)
    *tables, seven_2, halo = tie(*tables, seven_2, halo)
    tables = tables + [along_core(table, 1) for table in tables]
    sevens = [seven_0, seven_1, seven_2]

    def where_held(cell):
        device = cell // 16
        there = (device // 4, device % 4)
        dz = (there[0] // 8 - cells // 8 + 3) % 8
        dy = (there[0] // 2 - cells // 2) % 4
        dc = (there[0] - cells) % 2
        dx = (there[1] - sub) % 4
        return (dc * 4 + dx) * 512 + dy * 128 + dz * 16 + cell % 16

    entries_five = sources_five.T.reshape(1, 128)
    entries_four = sources_four.T.reshape(1, 16)
    octants = jnp.arange(8, dtype=jnp.int32)[:, None]
    children = (8 * entries_four + octants).reshape(1, 128)
    index = where_held(jnp.concatenate([entries_five, children], axis=1))
    cls_low = jnp.concatenate(
        [classes_five.T, classes_four.T, jnp.full((LIST, 110), KINDS, jnp.int32), classes_six.T], axis=1
    )
    return last(tables, index, six, halo, src_six, cls_low, up, down, sevens, maps).T


def solution(mesh):
    in_specs = (
        P(("cells", "sub"), None),
        P(("cells", "sub")),
        P(),
        P(),
        P(),
        P(("cells", "sub"), None),
        P(("cells", "sub"), None),
        P(("cells", "sub"), None),
        P(("cells", "sub"), None),
        P(("cells", "sub"), None),
        P(("cells", "sub"), None),
        P(("cells", "sub"), None),
        P(("cells", "sub"), None),
    )
    out_specs = P(("cells", "sub"), None)
    return jax.shard_map(body, mesh=mesh, in_specs=in_specs, out_specs=out_specs, check_vma=False)
```

time: 122 us -> 89.3 us (0.73); the launches traced: 120 us -> 89.1 us
  Pallas kernels: 66.4 us -> 45.6 us
  local copies, waits for them, and re-layouts: 17.1 us -> 6.39 us
  waiting for transfers between devices: 2.16 us -> 7.49 us
  other arithmetic: 3.12 us -> 0.23 us
  starting transfers between devices: 31 us -> 29 us
    pallas_call x6, Pallas kernels: 51.9 us -> 30.9 us  [the longest x3 25.8 us: near(): pl.pallas_call(functools.partial(near_body, block, count), out_shape=jax....]
    reshape x3 -> x0, local copies, waits for them, and re-layouts: 12.4 us -> none  [body(): down = downward_maps.reshape(F, 8, F).transpose(2, 1, 0).reshape(F, 8 * F)]
    ppermute x14, waiting for transfers between devices: 2.16 us -> 6.11 us  [turned(): return lax.ppermute(value, axis, pairs)]
    unnamed x34, local copies, waits for them, and re-layouts: 3.53 us -> 5.85 us
    ppermute x14, starting transfers between devices: 23.9 us -> 21.8 us  [turned(): return lax.ppermute(value, axis, pairs)]
    ppermute x2, waiting for transfers between devices: 0.01 us -> 1.38 us  [shifted(): lax.ppermute(value, axis, [(source, source + steps) for source in range(f...]
  transfers between devices with their start and end apart: 16 -> 16, of which waited for: 2 -> 5; matrix products, arithmetic and copies ran while one was open for 12% -> 1% of each run, Pallas kernels for 41% -> 31%
where the time goes in v2:
time: 89.3 us; the launch traced here: 89.1 us
  Pallas kernels  45.6 us (51%)
  starting transfers between devices  29 us (32%)
  waiting for transfers between devices  7.49 us (8%)
  local copies, waits for them, and re-layouts  6.39 us (7%)
    pallas_call x3, Pallas kernels, near(): pl.pallas_call(functools.partial(near_body, block, count), out_shape=jax....  25.8 us
    ppermute x14, starting transfers between devices, turned(): return lax.ppermute(value, axis, pairs)  21.8 us
    pallas_call x1, Pallas kernels, last(): pl.pallas_call(last_body, out_shape=jax.ShapeDtypeStruct((F, 1024), BF),...  14.7 us
    ppermute x2, starting transfers between devices, shifted(): lax.ppermute(value, axis, [(source, source + steps) for source in range(f...  7.14 us
    ppermute x14, waiting for transfers between devices, turned(): return lax.ppermute(value, axis, pairs)  6.11 us
    unnamed x34, local copies, waits for them, and re-layouts  5.85 us
    pallas_call x1, Pallas kernels, rise(): pl.pallas_call(rise_body, out_shape=(jax.ShapeDtypeStruct((F, 512), BF),...  3.01 us
  transfers between devices with their start and end apart: 16, of which 5 were waited for; matrix products, arithmetic and copies ran while one was open for 1% of the time, Pallas kernels for 31%

profile of v2, /device:TPU:1, one launch (start us, length us, event | category | flops | bytes accessed | tf_op | source)
XLA Modules:
  0.0 89.1 jit_solution(2528304250741755984)
XLA Ops:
  0.0 1.4 %copy-done.2 = bf16[2368,296]{0,1:T(8,128)(2,1)S(1)} copy-done((bf16[2368,296]{0,1:T(8,128)(2,1)S(1)}, bf16[2368,296]{0,1:T(8,128)(2,1)}, u32[]{:S(2)}) %copy-start.2) | copy-done | bytes 1401880
  1.4 1.1 %copy-done.4 = bf16[1024,296]{0,1:T(8,128)(2,1)S(1)} copy-done((bf16[1024,296]{0,1:T(8,128)(2,1)S(1)}, bf16[1024,296]{0,1:T(8,128)(2,1)}, u32[]{:S(2)}) %copy-start.4) | copy-done | bytes 606232
  2.4 0.7 copy-done.6
  3.2 3.0 %rise.1 = (bf16[296,512]{1,0:T(8,128)(2,1)S(1)}, bf16[296,512]{1,0:T(8,128)(2,1)S(1)}, bf16[296,128]{1,0:T(8,128)(2,1)S(1)}, bf16[16,296]{1,0:T(8,128)(2,1)S(1)}) custom-call(bf16[296,1024]{1,0:T(8,128)(2,1)S(1)} %bitcast.37, s32[8,128]{1,0:T(8,128)S(1)} %bitcast.41, bf16[296,2368]{1,0:T(8,128)(2,1)S(1)} %bitcast.34), custom_call_target="tpu_custom_call" | custom-call | flops 2000000000 | bytes 3000000 | tf_op jit(solution)/shard_map/rise/pallas_call | solution.py:57
  6.2 6.4 %collective-permute-start.1 = (bf16[16,296]{1,0:T(8,128)(2,1)S(1)}, bf16[16,296]{1,0:T(8,128)(2,1)S(1)}, u32[]{:S(2)}, u32[]{:S(2)}) collective-permute-start(bf16[16,296]{1,0:T(8,128)(2,1)S(1)} %get-tuple-element.24), channel_id=1, source_target_pairs={{0,224},{4,228},{8,232},{12,236},{16,240},{20,244},{24,248},{28,25... | collective-permute-start | bytes 28424 | tf_op jit(solution)/shard_map/ppermute | solution.py:307
  12.6 0.0 collective-permute-start
  12.6 5.2 %collective-permute-start.11 = (bf16[296,512]{1,0:T(8,128)(2,1)S(1)}, bf16[296,512]{1,0:T(8,128)(2,1)S(1)}, u32[]{:S(2)}, u32[]{:S(2)}) collective-permute-start(bf16[296,512]{1,0:T(8,128)(2,1)S(1)} %get-tuple-element.32.b_ref.a_ref), channel_id=1, source_target_pairs={{1,0},{2,1},{3,2},{4,3},{5,4},{6,5},{7,6},{8,7},{9,8},{10,9},{11,1... | collective-permute-start | bytes 909320 | tf_op jit(solution)/shard_map/ppermute | solution.py:298
  17.8 1.9 %collective-permute-start.4 = (bf16[296,512]{1,0:T(8,128)(2,1)S(1)}, bf16[296,512]{1,0:T(8,128)(2,1)S(1)}, u32[]{:S(2)}, u32[]{:S(2)}) collective-permute-start(bf16[296,512]{1,0:T(8,128)(2,1)S(1)} %get-tuple-element.27.c_ref.b_ref), channel_id=1, source_target_pairs={{0,1},{1,2},{2,3},{3,4},{4,5},{5,6},{6,7},{7,8},{8,9},{9,10},{10,1... | collective-permute-start | bytes 909320 | tf_op jit(solution)/shard_map/ppermute | solution.py:298
  19.8 0.1 concatenate.64
  19.9 0.1 copy.18
  19.9 0.1 mul.79
  20.0 0.1 concatenate.65
  20.2 0.0 collective-permute-done
  20.2 2.7 %collective-permute-start.3 = (bf16[3,16,296]{2,1,0:T(8,128)(2,1)S(1)}, bf16[3,16,296]{2,1,0:T(8,128)(2,1)S(1)}, u32[]{:S(2)}, u32[]{:S(2)}) collective-permute-start(bf16[3,16,296]{2,1,0:T(8,128)(2,1)S(1)} %pad_maximum_fusion.2), channel_id=1, source_target_pairs={{0,160},{4,164},{8,168},{12,172},{16,176},{20,180},{24,184},{28,18... | collective-permute-start | bytes 85256 | tf_op jit(solution)/shard_map/ppermute | solution.py:307
  23.0 0.6 collective-permute-start.2
  23.6 0.1 fusion.2.index_ref
  23.6 0.1 pad.2.clone
  23.7 0.1 copy.19
  23.8 4.8 %collective-permute-done.2 = bf16[2,16,296]{2,1,0:T(8,128)(2,1)S(1)} collective-permute-done((bf16[2,16,296]{2,1,0:T(8,128)(2,1)S(1)}, bf16[2,16,296]{2,1,0:T(8,128)(2,1)S(1)}, u32[]{:S(2)}, u32[]{:S(2)}) %collective-permute-start.2) | collective-permute-done | bytes 18976 | tf_op jit(solution)/shard_map/ppermute | solution.py:307
  28.7 0.1 copy.17
  28.8 1.4 %collective-permute-done.4.a_ref.below_ref = bf16[296,512]{1,0:T(8,128)(2,1)S(1)} collective-permute-done((bf16[296,512]{1,0:T(8,128)(2,1)S(1)}, bf16[296,512]{1,0:T(8,128)(2,1)S(1)}, u32[]{:S(2)}, u32[]{:S(2)}) %collective-permute-start.4) | collective-permute-done | bytes 303136 | tf_op jit(solution)/shard_map/ppermute | solution.py:298
  30.2 2.6 %copy-done = bf16[9472,296]{0,1:T(8,128)(2,1)S(1)} copy-done((bf16[9472,296]{0,1:T(8,128)(2,1)S(1)}, bf16[9472,296]{0,1:T(8,128)(2,1)}, u32[]{:S(2)}) %copy-start) | copy-done | bytes 5607448
  32.8 6.5 %near0.1.s0 = f32[1,296,256]{2,1,0:T(8,128)S(1)} custom-call(bf16[296,512]{1,0:T(8,128)(2,1)S(1)} %collective-permute-done.4.a_ref.below_ref, bf16[296,512]{1,0:T(8,128)(2,1)S(1)} %get-tuple-element.32.b_ref.a_ref, bf16[296,512]{1,0:T(8,128)(2,1)S(1)} %get-tuple-element.27.c_ref.b_ref, s32[8,1024]{1,0:T(8,128)S(1)} %subtract_bitcast_fusion.src_ref, ...), custom_call_target="tpu_custom_call" | custom-call | flops 6000000000 | bytes 6000000 | tf_op jit(solution)/shard_map/near0/pallas_call | solution.py:147
  39.2 0.0 slice-start
  39.3 1.4 %collective-permute-start.7 = (bf16[296,128]{1,0:T(8,128)(2,1)S(1)}, bf16[296,128]{1,0:T(8,128)(2,1)S(1)}, u32[]{:S(2)}, u32[]{:S(2)}) collective-permute-start(bf16[296,128]{1,0:T(8,128)(2,1)S(1)} %bitcast.43), channel_id=1, source_target_pairs={{0,8},{4,12},{8,16},{12,20},{16,24},{20,28},{24,0},{28,4},{32,40},... | collective-permute-start | bytes 227336 | tf_op jit(solution)/shard_map/ppermute | solution.py:307
  40.6 1.7 %collective-permute-start.6 = (bf16[296,128]{1,0:T(8,128)(2,1)S(1)}, bf16[296,128]{1,0:T(8,128)(2,1)S(1)}, u32[]{:S(2)}, u32[]{:S(2)}) collective-permute-start(bf16[296,128]{1,0:T(8,128)(2,1)S(1)} %bitcast.44), channel_id=1, source_target_pairs={{0,16},{4,20},{8,24},{12,28},{16,0},{20,4},{24,8},{28,12},{32,48},... | collective-permute-start | bytes 227336 | tf_op jit(solution)/shard_map/ppermute | solution.py:307
  42.3 2.0 %collective-permute-start.5 = (bf16[296,128]{1,0:T(8,128)(2,1)S(1)}, bf16[296,128]{1,0:T(8,128)(2,1)S(1)}, u32[]{:S(2)}, u32[]{:S(2)}) collective-permute-start(bf16[296,128]{1,0:T(8,128)(2,1)S(1)} %bitcast.45), channel_id=1, source_target_pairs={{0,24},{4,28},{8,0},{12,4},{16,8},{20,12},{24,16},{28,20},{32,56},... | collective-permute-start | bytes 227336 | tf_op jit(solution)/shard_map/ppermute | solution.py:307
  44.3 6.4 %near1.1.s1 = f32[1,296,256]{2,1,0:T(8,128)S(1)} custom-call(bf16[296,512]{1,0:T(8,128)(2,1)S(1)} %collective-permute-done.4.a_ref.below_ref, bf16[296,512]{1,0:T(8,128)(2,1)S(1)} %get-tuple-element.32.b_ref.a_ref, bf16[296,512]{1,0:T(8,128)(2,1)S(1)} %get-tuple-element.27.c_ref.b_ref, s32[8,1024]{1,0:T(8,128)S(1)} %subtract_bitcast_fusion.src_ref, ...), custom_call_target="tpu_custom_call" | custom-call | flops 6000000000 | bytes 6000000 | tf_op jit(solution)/shard_map/near1/pallas_call | solution.py:147
  50.8 0.0 collective-permute-done.6
  50.8 0.0 collective-permute-done.5
  50.8 0.0 copy-start.3
  50.9 0.1 collective-permute-start.10
  50.9 3.6 %collective-permute-start.9 = (bf16[296,512]{1,0:T(8,128)(2,1)S(1)}, bf16[296,512]{1,0:T(8,128)(2,1)S(1)}, u32[]{:S(2)}, u32[]{:S(2)}) collective-permute-start(bf16[296,512]{1,0:T(8,128)(2,1)S(1)} %pad_maximum_fusion.t0), channel_id=1, source_target_pairs={{0,2},{1,3},{2,0},{3,1},{4,6},{5,7},{6,4},{7,5},{8,10},{9,11},{10,... | collective-permute-start | bytes 909320 | tf_op jit(solution)/shard_map/ppermute | solution.py:307
  54.6 12.9 %near2.1.s2 = f32[2,296,256]{2,1,0:T(8,128)S(1)} custom-call(bf16[296,512]{1,0:T(8,128)(2,1)S(1)} %get-tuple-element.32.b_ref.a_ref, bf16[296,512]{1,0:T(8,128)(2,1)S(1)} %get-tuple-element.27.c_ref.b_ref, bf16[296,512]{1,0:T(8,128)(2,1)S(1)} %collective-permute-done.11.c_ref.above_ref, s32[8,1024]{1,0:T(8,128)S(1)} %subtract_bitcast_fusion.src_ref, ...), custom_call_target="tpu_custom_call" | custom-call | flops 12000000000 | bytes 6000000 | tf_op jit(solution)/shard_map/near2/pallas_call | solution.py:147
  67.4 0.0 copy-start.1
  67.5 1.6 %halo.1.halo_ref = bf16[296,128]{1,0:T(8,128)(2,1)S(1)} custom-call(bf16[296,512]{1,0:T(8,128)(2,1)S(1)} %collective-permute-done.4.a_ref.below_ref, bf16[296,512]{1,0:T(8,128)(2,1)S(1)} %collective-permute-done.11.c_ref.above_ref, bf16[296,2368]{1,0:T(8,128)(2,1)S(1)} %bitcast.35), custom_call_target="tpu_custom_call" | custom-call | flops 2000000000 | bytes 3000000 | tf_op jit(solution)/shard_map/halo/pallas_call | solution.py:170
  69.0 0.0 copy-start.10
  69.0 0.0 copy-start.11
  69.1 2.7 %collective-permute-start.12 = (bf16[296,512]{1,0:T(8,128)(2,1)S(1)}, bf16[296,512]{1,0:T(8,128)(2,1)S(1)}, u32[]{:S(2)}, u32[]{:S(2)}) collective-permute-start(bf16[296,512]{1,0:T(8,128)(2,1)S(1)} %pad_maximum_fusion.t0), channel_id=1, source_target_pairs={{0,4},{4,0},{8,12},{12,8},{16,20},{20,16},{24,28},{28,24},{32,36},... | collective-permute-start | bytes 909320 | tf_op jit(solution)/shard_map/ppermute | solution.py:307
  71.8 0.1 collective-permute-start.13
  71.9 0.4 collective-permute-start.14
  72.3 0.1 collective-permute-start.15
  72.4 0.5 flip.1.down_ref
  73.0 0.1 pad_add_fusion.cls_ref
  73.1 0.4 collective-permute-done.13.t5
  73.5 0.4 collective-permute-done.14.t6
  73.9 0.4 collective-permute-done.15.t7
  74.3 14.7 %last.1 = bf16[296,1024]{1,0:T(8,128)(2,1)} custom-call(bf16[296,512]{1,0:T(8,128)(2,1)S(1)} %pad_maximum_fusion.t0, bf16[296,512]{1,0:T(8,128)(2,1)S(1)} %collective-permute-done.8.t1, bf16[296,512]{1,0:T(8,128)(2,1)S(1)} %collective-permute-done.9.t2, bf16[296,512]{1,0:T(8,128)(2,1)S(1)} %collective-permute-done.10.t3, ...), custom_call_target="tpu_custom_call" | custom-call | flops 8000000000 | bytes 12000000 | tf_op jit(solution)/shard_map/last/pallas_call | solution.py:273
  (44 shorter events, 0.2 us)
Async XLA Ops:
  0.0 1.4 %copy-start.2 = (bf16[2368,296]{0,1:T(8,128)(2,1)S(1)}, bf16[2368,296]{0,1:T(8,128)(2,1)}, u32[]{:S(2)}) copy-start(bf16[2368,296]{0,1:T(8,128)(2,1)} %param.15) | copy-start | bytes 4205572
  1.4 1.1 %copy-start.4 = (bf16[1024,296]{0,1:T(8,128)(2,1)S(1)}, bf16[1024,296]{0,1:T(8,128)(2,1)}, u32[]{:S(2)}) copy-start(bf16[1024,296]{0,1:T(8,128)(2,1)} %param.13) | copy-start | bytes 1818628
  2.4 0.7 copy-start.6
  3.1 16.6 %copy-start.8 = (s32[16,8]{0,1:T(8,128)S(1)}, s32[16,8]{0,1:T(8,128)}, u32[]{:S(2)}) copy-start(s32[16,8]{0,1:T(8,128)} %param.22) | copy-start | bytes 1540
  3.1 16.7 %copy-start.13 = (s32[2,8]{1,0:T(2,128)S(1)}, s32[2,8]{1,0:T(2,128)}, u32[]{:S(2)}) copy-start(s32[2,8]{1,0:T(2,128)} %param.24) | copy-start | bytes 196
  3.1 17.0 %copy-start.9 = (s32[128,8]{0,1:T(8,128)S(1)}, s32[128,8]{0,1:T(8,128)}, u32[]{:S(2)}) copy-start(s32[128,8]{0,1:T(8,128)} %param.20) | copy-start | bytes 12292
  3.1 17.0 %copy-start.7 = (s32[1024,8]{0,1:T(8,128)S(1)}, s32[1024,8]{0,1:T(8,128)}, u32[]{:S(2)}) copy-start(s32[1024,8]{0,1:T(8,128)} %param.18) | copy-start | bytes 98308
  3.1 20.6 %copy-start.12 = (s32[2,8]{1,0:T(2,128)S(1)}, s32[2,8]{1,0:T(2,128)}, u32[]{:S(2)}) copy-start(s32[2,8]{1,0:T(2,128)} %param.25) | copy-start | bytes 196
  3.1 27.0 %copy-start.5 = (s32[1024,8]{0,1:T(8,128)S(1)}, s32[1024,8]{0,1:T(8,128)}, u32[]{:S(2)}) copy-start(s32[1024,8]{0,1:T(8,128)} %param.19) | copy-start | bytes 98308
  6.2 14.0 %collective-permute-start.1 = (bf16[16,296]{1,0:T(8,128)(2,1)S(1)}, bf16[16,296]{1,0:T(8,128)(2,1)S(1)}, u32[]{:S(2)}, u32[]{:S(2)}) collective-permute-start(bf16[16,296]{1,0:T(8,128)(2,1)S(1)} %get-tuple-element.24), channel_id=1, source_target_pairs={{0,224},{4,228},{8,232},{12,236},{16,240},{20,244},{24,248},{28,25... | collective-permute-start | bytes 28424 | tf_op jit(solution)/shard_map/ppermute | solution.py:307
  12.6 7.6 %collective-permute-start = (bf16[16,296]{1,0:T(8,128)(2,1)S(1)}, bf16[16,296]{1,0:T(8,128)(2,1)S(1)}, u32[]{:S(2)}, u32[]{:S(2)}) collective-permute-start(bf16[16,296]{1,0:T(8,128)(2,1)S(1)} %get-tuple-element.24), channel_id=1, source_target_pairs={{0,32},{4,36},{8,40},{12,44},{16,48},{20,52},{24,56},{28,60},{32,6... | collective-permute-start | bytes 28424 | tf_op jit(solution)/shard_map/ppermute | solution.py:307
  12.6 41.9 %collective-permute-start.11 = (bf16[296,512]{1,0:T(8,128)(2,1)S(1)}, bf16[296,512]{1,0:T(8,128)(2,1)S(1)}, u32[]{:S(2)}, u32[]{:S(2)}) collective-permute-start(bf16[296,512]{1,0:T(8,128)(2,1)S(1)} %get-tuple-element.32.b_ref.a_ref), channel_id=1, source_target_pairs={{1,0},{2,1},{3,2},{4,3},{5,4},{6,5},{7,6},{8,7},{9,8},{10,9},{11,1... | collective-permute-start | bytes 909320 | tf_op jit(solution)/shard_map/ppermute | solution.py:298
  17.8 12.4 %collective-permute-start.4 = (bf16[296,512]{1,0:T(8,128)(2,1)S(1)}, bf16[296,512]{1,0:T(8,128)(2,1)S(1)}, u32[]{:S(2)}, u32[]{:S(2)}) collective-permute-start(bf16[296,512]{1,0:T(8,128)(2,1)S(1)} %get-tuple-element.27.c_ref.b_ref), channel_id=1, source_target_pairs={{0,1},{1,2},{2,3},{3,4},{4,5},{5,6},{6,7},{7,8},{8,9},{9,10},{10,1... | collective-permute-start | bytes 909320 | tf_op jit(solution)/shard_map/ppermute | solution.py:298
  20.2 8.4 %collective-permute-start.3 = (bf16[3,16,296]{2,1,0:T(8,128)(2,1)S(1)}, bf16[3,16,296]{2,1,0:T(8,128)(2,1)S(1)}, u32[]{:S(2)}, u32[]{:S(2)}) collective-permute-start(bf16[3,16,296]{2,1,0:T(8,128)(2,1)S(1)} %pad_maximum_fusion.2), channel_id=1, source_target_pairs={{0,160},{4,164},{8,168},{12,172},{16,176},{20,180},{24,184},{28,18... | collective-permute-start | bytes 85256 | tf_op jit(solution)/shard_map/ppermute | solution.py:307
  23.0 5.7 %collective-permute-start.2 = (bf16[2,16,296]{2,1,0:T(8,128)(2,1)S(1)}, bf16[2,16,296]{2,1,0:T(8,128)(2,1)S(1)}, u32[]{:S(2)}, u32[]{:S(2)}) collective-permute-start(bf16[2,16,296]{2,1,0:T(8,128)(2,1)S(1)} %slice.3), channel_id=1, source_target_pairs={{0,96},{4,100},{8,104},{12,108},{16,112},{20,116},{24,120},{28,124... | collective-permute-start | bytes 56840 | tf_op jit(solution)/shard_map/ppermute | solution.py:307
  30.2 2.6 %copy-start = (bf16[9472,296]{0,1:T(8,128)(2,1)S(1)}, bf16[9472,296]{0,1:T(8,128)(2,1)}, u32[]{:S(2)}) copy-start(bf16[9472,296]{0,1:T(8,128)(2,1)} %param.16) | copy-start | bytes 16822276
  39.2 15.3 %slice-start = ((s8[5607424]{0:T(1024)(128)(4,1)}), s8[4194304]{0:T(1024)(128)(4,1)S(1)}, s32[]{:S(2)}) async-start(s8[5607424]{0:T(1024)(128)(4,1)} %bitcast.30), calls=%async_computation | async-start | bytes 8388608
  39.2 15.3 %slice-start.1 = ((s8[5607424]{0:T(1024)(128)(4,1)}), s8[1413120]{0:T(1024)(128)(4,1)S(1)}, s32[]{:S(2)}) async-start(s8[5607424]{0:T(1024)(128)(4,1)} %bitcast.30), calls=%async_computation.1 | async-start | bytes 2826240
  39.3 11.5 %collective-permute-start.7 = (bf16[296,128]{1,0:T(8,128)(2,1)S(1)}, bf16[296,128]{1,0:T(8,128)(2,1)S(1)}, u32[]{:S(2)}, u32[]{:S(2)}) collective-permute-start(bf16[296,128]{1,0:T(8,128)(2,1)S(1)} %bitcast.43), channel_id=1, source_target_pairs={{0,8},{4,12},{8,16},{12,20},{16,24},{20,28},{24,0},{28,4},{32,40},... | collective-permute-start | bytes 227336 | tf_op jit(solution)/shard_map/ppermute | solution.py:307
  40.6 10.2 %collective-permute-start.6 = (bf16[296,128]{1,0:T(8,128)(2,1)S(1)}, bf16[296,128]{1,0:T(8,128)(2,1)S(1)}, u32[]{:S(2)}, u32[]{:S(2)}) collective-permute-start(bf16[296,128]{1,0:T(8,128)(2,1)S(1)} %bitcast.44), channel_id=1, source_target_pairs={{0,16},{4,20},{8,24},{12,28},{16,0},{20,4},{24,8},{28,12},{32,48},... | collective-permute-start | bytes 227336 | tf_op jit(solution)/shard_map/ppermute | solution.py:307
  42.3 8.5 %collective-permute-start.5 = (bf16[296,128]{1,0:T(8,128)(2,1)S(1)}, bf16[296,128]{1,0:T(8,128)(2,1)S(1)}, u32[]{:S(2)}, u32[]{:S(2)}) collective-permute-start(bf16[296,128]{1,0:T(8,128)(2,1)S(1)} %bitcast.45), channel_id=1, source_target_pairs={{0,24},{4,28},{8,0},{12,4},{16,8},{20,12},{24,16},{28,20},{32,56},... | collective-permute-start | bytes 227336 | tf_op jit(solution)/shard_map/ppermute | solution.py:307
  50.8 16.6 %copy-start.3 = (bf16[2368,296]{0,1:T(8,128)(2,1)S(1)}, bf16[2368,296]{0,1:T(8,128)(2,1)}, u32[]{:S(2)}) copy-start(bf16[2368,296]{0,1:T(8,128)(2,1)} %param.15) | copy-start | bytes 4205572
  50.9 18.2 %collective-permute-start.10 = (bf16[296,512]{1,0:T(8,128)(2,1)S(1)}, bf16[296,512]{1,0:T(8,128)(2,1)S(1)}, u32[]{:S(2)}, u32[]{:S(2)}) collective-permute-start(bf16[296,512]{1,0:T(8,128)(2,1)S(1)} %pad_maximum_fusion.t0), channel_id=1, source_target_pairs={{0,1},{1,2},{2,3},{3,0},{4,5},{5,6},{6,7},{7,4},{8,9},{9,10},{10,1... | collective-permute-start | bytes 909320 | tf_op jit(solution)/shard_map/ppermute | solution.py:307
  50.9 18.1 %collective-permute-start.9 = (bf16[296,512]{1,0:T(8,128)(2,1)S(1)}, bf16[296,512]{1,0:T(8,128)(2,1)S(1)}, u32[]{:S(2)}, u32[]{:S(2)}) collective-permute-start(bf16[296,512]{1,0:T(8,128)(2,1)S(1)} %pad_maximum_fusion.t0), channel_id=1, source_target_pairs={{0,2},{1,3},{2,0},{3,1},{4,6},{5,7},{6,4},{7,5},{8,10},{9,11},{10,... | collective-permute-start | bytes 909320 | tf_op jit(solution)/shard_map/ppermute | solution.py:307
  54.5 14.6 %collective-permute-start.8 = (bf16[296,512]{1,0:T(8,128)(2,1)S(1)}, bf16[296,512]{1,0:T(8,128)(2,1)S(1)}, u32[]{:S(2)}, u32[]{:S(2)}) collective-permute-start(bf16[296,512]{1,0:T(8,128)(2,1)S(1)} %pad_maximum_fusion.t0), channel_id=1, source_target_pairs={{0,3},{1,0},{2,1},{3,2},{4,7},{5,4},{6,5},{7,6},{8,11},{9,8},{10,9... | collective-permute-start | bytes 909320 | tf_op jit(solution)/shard_map/ppermute | solution.py:307
  67.4 5.0 %copy-start.1 = (bf16[296,2368]{1,0:T(8,128)(2,1)S(1)}, bf16[296,2368]{1,0:T(8,128)(2,1)}, u32[]{:S(2)}) copy-start(bf16[296,2368]{1,0:T(8,128)(2,1)} %down_ref.1) | copy-start | bytes 4205572
  69.0 3.9 %copy-start.10 = (s32[128,8]{0,1:T(8,128)S(1)}, s32[128,8]{0,1:T(8,128)}, u32[]{:S(2)}) copy-start(s32[128,8]{0,1:T(8,128)} %param.21) | copy-start | bytes 12292
  69.0 3.9 %copy-start.11 = (s32[16,8]{0,1:T(8,128)S(1)}, s32[16,8]{0,1:T(8,128)}, u32[]{:S(2)}) copy-start(s32[16,8]{0,1:T(8,128)} %param.23) | copy-start | bytes 1540
  69.1 4.0 %collective-permute-start.12 = (bf16[296,512]{1,0:T(8,128)(2,1)S(1)}, bf16[296,512]{1,0:T(8,128)(2,1)S(1)}, u32[]{:S(2)}, u32[]{:S(2)}) collective-permute-start(bf16[296,512]{1,0:T(8,128)(2,1)S(1)} %pad_maximum_fusion.t0), channel_id=1, source_target_pairs={{0,4},{4,0},{8,12},{12,8},{16,20},{20,16},{24,28},{28,24},{32,36},... | collective-permute-start | bytes 909320 | tf_op jit(solution)/shard_map/ppermute | solution.py:307
  71.8 1.7 %collective-permute-start.13 = (bf16[296,512]{1,0:T(8,128)(2,1)S(1)}, bf16[296,512]{1,0:T(8,128)(2,1)S(1)}, u32[]{:S(2)}, u32[]{:S(2)}) collective-permute-start(bf16[296,512]{1,0:T(8,128)(2,1)S(1)} %collective-permute-done.8.t1), channel_id=1, source_target_pairs={{0,4},{4,0},{8,12},{12,8},{16,20},{20,16},{24,28},{28,24},{32,36},... | collective-permute-start | bytes 909320 | tf_op jit(solution)/shard_map/ppermute | solution.py:307
  71.9 2.0 %collective-permute-start.14 = (bf16[296,512]{1,0:T(8,128)(2,1)S(1)}, bf16[296,512]{1,0:T(8,128)(2,1)S(1)}, u32[]{:S(2)}, u32[]{:S(2)}) collective-permute-start(bf16[296,512]{1,0:T(8,128)(2,1)S(1)} %collective-permute-done.9.t2), channel_id=1, source_target_pairs={{0,4},{4,0},{8,12},{12,8},{16,20},{20,16},{24,28},{28,24},{32,36},... | collective-permute-start | bytes 909320 | tf_op jit(solution)/shard_map/ppermute | solution.py:307
  72.3 2.0 %collective-permute-start.15 = (bf16[296,512]{1,0:T(8,128)(2,1)S(1)}, bf16[296,512]{1,0:T(8,128)(2,1)S(1)}, u32[]{:S(2)}, u32[]{:S(2)}) collective-permute-start(bf16[296,512]{1,0:T(8,128)(2,1)S(1)} %collective-permute-done.10.t3), channel_id=1, source_target_pairs={{0,4},{4,0},{8,12},{12,8},{16,20},{20,16},{24,28},{28,24},{32,36},... | collective-permute-start | bytes 909320 | tf_op jit(solution)/shard_map/ppermute | solution.py:307

commit v3 on v2

--- a/solution.py
+++ b/solution.py
@@ -42,33 +42,28 @@
     return dot(up_ref[...], stack[...].astype(BF))
 
 
-def rise_body(leaf_ref, held_ref, up_ref, lo_ref, hi_ref, six_ref, five_ref, stack):
-    held = jnp.concatenate([held_ref[r : r + 1, :] for r in range(8)], axis=1)
-    children = leaf_ref[...] * jnp.where(held > 0, 1.0, 0.0).astype(BF)
-    lo_ref[...] = children[:, :512]
-    hi_ref[...] = children[:, 512:]
+def rise_body(lo_ref, hi_ref, up_ref, six_ref, five_ref, stack):
+    children = jnp.concatenate([lo_ref[...], hi_ref[...]], axis=1)
     six = ascend(children, up_ref, stack).astype(BF)
     six_ref[...] = six
     five = ascend(six, up_ref, stack)
     five_ref[...] = five.T[:16, :].astype(BF)
 
 
-def rise(leaves, held, up):
+def rise(lo, hi, up):
     return pl.pallas_call(
         rise_body,
         out_shape=(
-            jax.ShapeDtypeStruct((F, 512), BF),
-            jax.ShapeDtypeStruct((F, 512), BF),
             jax.ShapeDtypeStruct((F, 128), BF),
             jax.ShapeDtypeStruct((16, F), BF),
         ),
         in_specs=[VM] * 3,
-        out_specs=(VM,) * 4,
+        out_specs=(VM,) * 2,
         scratch_shapes=[pltpu.VMEM((8 * F, 128), F32)],
         compiler_params=pltpu.CompilerParams(vmem_limit_bytes=16 * 2**20),
-        cost_estimate=pl.CostEstimate(flops=2 * 10**9, bytes_accessed=3 * 10**6, transcendentals=0),
+        cost_estimate=pl.CostEstimate(flops=8 * 10**9, bytes_accessed=3 * 10**6, transcendentals=0),
         name="rise",
-    )(leaves, held, up)
+    )(lo, hi, up)
 
 
 def spread(value, even, odd, slot, lanes):
@@ -334,9 +329,11 @@
 ):
     leaves = leaf_multipoles.T
     up, maps = upward_maps.T, transfer_maps.T
-    lo, hi, six, five = rise(leaves, occupancy.reshape(8, 128), up)
+    masked = leaves * occupancy.astype(BF)[None, :]
+    lo, hi = masked[:, :512], masked[:, 512:]
     below = shifted(hi, ("cells", "sub"), 1)
     above = shifted(lo, ("cells", "sub"), -1)
+    six, five = rise(lo, hi, up)
 
     cells, sub = lax.axis_index("cells"), lax.axis_index("sub")
     place = cells * 4 + sub
@@ -352,10 +349,12 @@
     upper = along_z(three, -3)
     lower = along_z(three[1:], 3)
     seven_0 = near(0, 1, below, near_lo, hi, src_seven, cls_seven, maps)
+    lower, upper, seven_0 = tie(lower, upper, seven_0)
     column = jnp.concatenate([lower, three, upper], axis=0).reshape(128, F).T
     column, seven_0, near_lo = tie(column, seven_0, near_lo)
     sides = along_y(column, -1), along_y(column, 2), along_y(column, 1)
     seven_1 = near(1, 1, below, near_lo, hi, src_seven, cls_seven, maps)
+    *sides, seven_1 = tie(*sides, seven_1)
     plane = jnp.concatenate([column, *sides], axis=1)
     plane, seven_1, near_lo, near_up = tie(plane, seven_1, near_lo, up)
     tables = [plane, along_x(plane, -1), along_x(plane, 2), along_x(plane, 1)]

time: 89.3 us -> 91.7 us (1.027)
  local copies, waits for them, and re-layouts: 6.39 us -> 8.5 us
  other arithmetic: 0.23 us -> 2.14 us
  starting transfers between devices: 29 us -> 27.2 us
    ppermute x2, waiting for transfers between devices: 1.38 us -> 6.38 us  [shifted(): lax.ppermute(value, axis, [(source, source + steps) for source in range(f...]
    ppermute x14, waiting for transfers between devices: 6.11 us -> 1.28 us  [turned(): return lax.ppermute(value, axis, pairs)]
    unnamed x34 -> x30, local copies, waits for them, and re-layouts: 5.85 us -> 7.92 us
    ppermute x14, starting transfers between devices: 21.8 us -> 20 us  [turned(): return lax.ppermute(value, axis, pairs)]
    mul x0 -> x1, other arithmetic: none -> 1.11 us  [body(): masked = leaves * occupancy.astype(BF)[None, :]]
  transfers between devices with their start and end apart: 16 -> 16, of which waited for: 5 -> 4; matrix products, arithmetic and copies ran while one was open for 1% -> 1% of each run, Pallas kernels for 31% -> 30%
where the time goes in v3:
time: 91.7 us; the launch traced here: 91.4 us
  Pallas kernels  45.6 us (50%)
  starting transfers between devices  27.2 us (30%)
  local copies, waits for them, and re-layouts  8.5 us (9%)
  waiting for transfers between devices  7.66 us (8%)
  other arithmetic  2.14 us (2%)
    pallas_call x3, Pallas kernels, near(): pl.pallas_call(functools.partial(near_body, block, count), out_shape=jax....  25.7 us
    ppermute x14, starting transfers between devices, turned(): return lax.ppermute(value, axis, pairs)  20 us
    pallas_call x1, Pallas kernels, last(): pl.pallas_call(last_body, out_shape=jax.ShapeDtypeStruct((F, 1024), BF),...  14.7 us
    unnamed x30, local copies, waits for them, and re-layouts  7.92 us
    ppermute x2, starting transfers between devices, shifted(): lax.ppermute(value, axis, [(source, source + steps) for source in range(f...  7.14 us
    ppermute x2, waiting for transfers between devices, shifted(): lax.ppermute(value, axis, [(source, source + steps) for source in range(f...  6.38 us
    pallas_call x1, Pallas kernels, rise(): pl.pallas_call(rise_body, out_shape=(jax.ShapeDtypeStruct((F, 128), BF),...  3 us
  transfers between devices with their start and end apart: 16, of which 4 were waited for; matrix products, arithmetic and copies ran while one was open for 1% of the time, Pallas kernels for 30%

profile of v3, /device:TPU:1, one launch (start us, length us, event | category | flops | bytes accessed | tf_op | source)
XLA Modules:
  0.0 91.4 jit_solution(6612216624081743385)
XLA Ops:
  0.0 0.8 convert_element_type.3
  0.8 1.1 %multiply_bitcast_fusion = bf16[296,1024]{1,0:T(8,128)(2,1)S(1)} fusion(bf16[1024,296]{0,1:T(8,128)(2,1)} %param.13, bf16[1024]{0:T(1024)(128)(2,1)S(1)} %convert_element_type.3), kind=kLoop, calls=%fused_computation | loop fusion | flops 303104 | bytes 1214464 | tf_op jit(solution)/shard_map/mul | solution.py:332
  2.0 0.0 copy-start.8
  2.0 0.0 copy-start.13
  2.0 0.0 copy-start.9
  2.0 0.0 copy-start.7
  2.0 0.0 copy-start.12
  2.0 0.0 copy-start.6
  2.1 3.0 %rise.1 = (bf16[296,128]{1,0:T(8,128)(2,1)S(1)}, bf16[16,296]{1,0:T(8,128)(2,1)S(1)}) custom-call(bf16[296,512]{1,0:T(8,128)(2,1)S(1)} %get-tuple-element.42.lo_ref.b_ref.a_ref, bf16[296,512]{1,0:T(8,128)(2,1)S(1)} %get-tuple-element.53.hi_ref.c_ref.b_ref, bf16[296,2368]{1,0:T(8,128)(2,1)S(1)} %bitcast.32), custom_call_target="tpu_custom_call" | custom-call | flops 8000000000 | bytes 3000000 | tf_op jit(solution)/shard_map/rise/pallas_call | solution.py:54
  5.1 6.4 %collective-permute-start.1 = (bf16[16,296]{1,0:T(8,128)(2,1)S(1)}, bf16[16,296]{1,0:T(8,128)(2,1)S(1)}, u32[]{:S(2)}, u32[]{:S(2)}) collective-permute-start(bf16[16,296]{1,0:T(8,128)(2,1)S(1)} %get-tuple-element.29), channel_id=1, source_target_pairs={{0,224},{4,228},{8,232},{12,236},{16,240},{20,244},{24,248},{28,25... | collective-permute-start | bytes 28424 | tf_op jit(solution)/shard_map/ppermute | solution.py:302
  11.5 5.2 %collective-permute-start.11 = (bf16[296,512]{1,0:T(8,128)(2,1)S(1)}, bf16[296,512]{1,0:T(8,128)(2,1)S(1)}, u32[]{:S(2)}, u32[]{:S(2)}) collective-permute-start(bf16[296,512]{1,0:T(8,128)(2,1)S(1)} %get-tuple-element.42.lo_ref.b_ref.a_ref), channel_id=1, source_target_pairs={{1,0},{2,1},{3,2},{4,3},{5,4},{6,5},{7,6},{8,7},{9,8},{10,9},{11,1... | collective-permute-start | bytes 909320 | tf_op jit(solution)/shard_map/ppermute | solution.py:293
  16.7 1.9 %collective-permute-start.4 = (bf16[296,512]{1,0:T(8,128)(2,1)S(1)}, bf16[296,512]{1,0:T(8,128)(2,1)S(1)}, u32[]{:S(2)}, u32[]{:S(2)}) collective-permute-start(bf16[296,512]{1,0:T(8,128)(2,1)S(1)} %get-tuple-element.53.hi_ref.c_ref.b_ref), channel_id=1, source_target_pairs={{0,1},{1,2},{2,3},{3,4},{4,5},{5,6},{6,7},{7,8},{8,9},{9,10},{10,1... | collective-permute-start | bytes 909320 | tf_op jit(solution)/shard_map/ppermute | solution.py:293
  18.7 0.1 concatenate.64
  18.8 0.1 copy.18
  18.9 0.1 mul.93
  18.9 0.1 concatenate.65
  19.1 0.1 fusion.2.index_ref
  19.2 0.1 pad.2.clone
  19.2 0.1 copy.19
  19.3 2.7 %collective-permute-start.3 = (bf16[3,16,296]{2,1,0:T(8,128)(2,1)S(1)}, bf16[3,16,296]{2,1,0:T(8,128)(2,1)S(1)}, u32[]{:S(2)}, u32[]{:S(2)}) collective-permute-start(bf16[3,16,296]{2,1,0:T(8,128)(2,1)S(1)} %pad_maximum_fusion.2), channel_id=1, source_target_pairs={{0,160},{4,164},{8,168},{12,172},{16,176},{20,180},{24,184},{28,18... | collective-permute-start | bytes 85256 | tf_op jit(solution)/shard_map/ppermute | solution.py:302
  22.1 0.6 collective-permute-start.2
  22.7 6.4 %collective-permute-done.4.a_ref.below_ref = bf16[296,512]{1,0:T(8,128)(2,1)S(1)} collective-permute-done((bf16[296,512]{1,0:T(8,128)(2,1)S(1)}, bf16[296,512]{1,0:T(8,128)(2,1)S(1)}, u32[]{:S(2)}, u32[]{:S(2)}) %collective-permute-start.4) | collective-permute-done | bytes 303136 | tf_op jit(solution)/shard_map/ppermute | solution.py:293
  29.1 2.6 %copy-done = bf16[9472,296]{0,1:T(8,128)(2,1)S(1)} copy-done((bf16[9472,296]{0,1:T(8,128)(2,1)S(1)}, bf16[9472,296]{0,1:T(8,128)(2,1)}, u32[]{:S(2)}) %copy-start) | copy-done | bytes 5607448
  31.7 6.4 %near0.1.s0 = f32[1,296,256]{2,1,0:T(8,128)S(1)} custom-call(bf16[296,512]{1,0:T(8,128)(2,1)S(1)} %collective-permute-done.4.a_ref.below_ref, bf16[296,512]{1,0:T(8,128)(2,1)S(1)} %get-tuple-element.42.lo_ref.b_ref.a_ref, bf16[296,512]{1,0:T(8,128)(2,1)S(1)} %get-tuple-element.53.hi_ref.c_ref.b_ref, s32[8,1024]{1,0:T(8,128)S(1)} %subtract_bitcast_fusion.src_ref, ...), custom_call_target="tpu_custom_call" | custom-call | flops 6000000000 | bytes 6000000 | tf_op jit(solution)/shard_map/near0/pallas_call | solution.py:142
  38.2 0.1 copy.17
  38.3 1.4 %collective-permute-start.7 = (bf16[296,128]{1,0:T(8,128)(2,1)S(1)}, bf16[296,128]{1,0:T(8,128)(2,1)S(1)}, u32[]{:S(2)}, u32[]{:S(2)}) collective-permute-start(bf16[296,128]{1,0:T(8,128)(2,1)S(1)} %bitcast.39), channel_id=1, source_target_pairs={{0,8},{4,12},{8,16},{12,20},{16,24},{20,28},{24,0},{28,4},{32,40},... | collective-permute-start | bytes 227336 | tf_op jit(solution)/shard_map/ppermute | solution.py:302
  39.7 1.7 %collective-permute-start.6 = (bf16[296,128]{1,0:T(8,128)(2,1)S(1)}, bf16[296,128]{1,0:T(8,128)(2,1)S(1)}, u32[]{:S(2)}, u32[]{:S(2)}) collective-permute-start(bf16[296,128]{1,0:T(8,128)(2,1)S(1)} %bitcast.40), channel_id=1, source_target_pairs={{0,16},{4,20},{8,24},{12,28},{16,0},{20,4},{24,8},{28,12},{32,48},... | collective-permute-start | bytes 227336 | tf_op jit(solution)/shard_map/ppermute | solution.py:302
  41.4 2.0 %collective-permute-start.5 = (bf16[296,128]{1,0:T(8,128)(2,1)S(1)}, bf16[296,128]{1,0:T(8,128)(2,1)S(1)}, u32[]{:S(2)}, u32[]{:S(2)}) collective-permute-start(bf16[296,128]{1,0:T(8,128)(2,1)S(1)} %bitcast.41), channel_id=1, source_target_pairs={{0,24},{4,28},{8,0},{12,4},{16,8},{20,12},{24,16},{28,20},{32,56},... | collective-permute-start | bytes 227336 | tf_op jit(solution)/shard_map/ppermute | solution.py:302
  43.4 2.6 %copy-done.1 = bf16[9472,296]{0,1:T(8,128)(2,1)S(1)} copy-done((bf16[9472,296]{0,1:T(8,128)(2,1)S(1)}, bf16[9472,296]{0,1:T(8,128)(2,1)}, u32[]{:S(2)}) %copy-start.1) | copy-done | bytes 5607448
  45.9 6.4 %near1.1.s1 = f32[1,296,256]{2,1,0:T(8,128)S(1)} custom-call(bf16[296,512]{1,0:T(8,128)(2,1)S(1)} %collective-permute-done.4.a_ref.below_ref, bf16[296,512]{1,0:T(8,128)(2,1)S(1)} %get-tuple-element.42.lo_ref.b_ref.a_ref, bf16[296,512]{1,0:T(8,128)(2,1)S(1)} %get-tuple-element.53.hi_ref.c_ref.b_ref, s32[8,1024]{1,0:T(8,128)S(1)} %subtract_bitcast_fusion.src_ref, ...), custom_call_target="tpu_custom_call" | custom-call | flops 6000000000 | bytes 6000000 | tf_op jit(solution)/shard_map/near1/pallas_call | solution.py:142
  52.5 0.1 collective-permute-start.10
  52.6 0.5 collective-permute-start.9
  53.1 2.2 %collective-permute-start.8 = (bf16[296,512]{1,0:T(8,128)(2,1)S(1)}, bf16[296,512]{1,0:T(8,128)(2,1)S(1)}, u32[]{:S(2)}, u32[]{:S(2)}) collective-permute-start(bf16[296,512]{1,0:T(8,128)(2,1)S(1)} %pad_maximum_fusion.t0), channel_id=1, source_target_pairs={{0,3},{1,0},{2,1},{3,2},{4,7},{5,4},{6,5},{7,6},{8,11},{9,8},{10,9... | collective-permute-start | bytes 909320 | tf_op jit(solution)/shard_map/ppermute | solution.py:302
  55.2 2.6 %copy-done.2 = bf16[9472,296]{0,1:T(8,128)(2,1)S(1)} copy-done((bf16[9472,296]{0,1:T(8,128)(2,1)S(1)}, bf16[9472,296]{0,1:T(8,128)(2,1)}, u32[]{:S(2)}) %copy-start.2) | copy-done | bytes 5607448
  57.8 12.9 %near2.1.s2 = f32[2,296,256]{2,1,0:T(8,128)S(1)} custom-call(bf16[296,512]{1,0:T(8,128)(2,1)S(1)} %get-tuple-element.42.lo_ref.b_ref.a_ref, bf16[296,512]{1,0:T(8,128)(2,1)S(1)} %get-tuple-element.53.hi_ref.c_ref.b_ref, bf16[296,512]{1,0:T(8,128)(2,1)S(1)} %collective-permute-done.11.c_ref.above_ref, s32[8,1024]{1,0:T(8,128)S(1)} %subtract_bitcast_fusion.src_ref, ...), custom_call_target="tpu_custom_call" | custom-call | flops 12000000000 | bytes 6000000 | tf_op jit(solution)/shard_map/near2/pallas_call | solution.py:142
  70.7 0.0 copy-start.3
  70.7 1.6 %halo.1.halo_ref = bf16[296,128]{1,0:T(8,128)(2,1)S(1)} custom-call(bf16[296,512]{1,0:T(8,128)(2,1)S(1)} %collective-permute-done.4.a_ref.below_ref, bf16[296,512]{1,0:T(8,128)(2,1)S(1)} %collective-permute-done.11.c_ref.above_ref, bf16[296,2368]{1,0:T(8,128)(2,1)S(1)} %bitcast.33), custom_call_target="tpu_custom_call" | custom-call | flops 2000000000 | bytes 3000000 | tf_op jit(solution)/shard_map/halo/pallas_call | solution.py:165
  72.3 0.0 copy-start.11
  72.3 1.8 %collective-permute-start.12 = (bf16[296,512]{1,0:T(8,128)(2,1)S(1)}, bf16[296,512]{1,0:T(8,128)(2,1)S(1)}, u32[]{:S(2)}, u32[]{:S(2)}) collective-permute-start(bf16[296,512]{1,0:T(8,128)(2,1)S(1)} %pad_maximum_fusion.t0), channel_id=1, source_target_pairs={{0,4},{4,0},{8,12},{12,8},{16,20},{20,16},{24,28},{28,24},{32,36},... | collective-permute-start | bytes 909320 | tf_op jit(solution)/shard_map/ppermute | solution.py:302
  74.2 0.1 collective-permute-start.13
  74.3 0.4 collective-permute-start.14
  74.7 0.1 collective-permute-start.15
  74.8 0.5 flip.1.down_ref
  75.4 0.1 pad_add_fusion.cls_ref
  75.5 0.4 collective-permute-done.13.t5
  75.8 0.4 collective-permute-done.14.t6
  76.3 0.4 collective-permute-done.15.t7
  76.7 14.7 %last.1 = bf16[296,1024]{1,0:T(8,128)(2,1)} custom-call(bf16[296,512]{1,0:T(8,128)(2,1)S(1)} %pad_maximum_fusion.t0, bf16[296,512]{1,0:T(8,128)(2,1)S(1)} %collective-permute-done.8.t1, bf16[296,512]{1,0:T(8,128)(2,1)S(1)} %collective-permute-done.9.t2, bf16[296,512]{1,0:T(8,128)(2,1)S(1)} %collective-permute-done.10.t3, ...), custom_call_target="tpu_custom_call" | custom-call | flops 8000000000 | bytes 12000000 | tf_op jit(solution)/shard_map/last/pallas_call | solution.py:268
  (42 shorter events, 0.2 us)
Async XLA Ops:
  0.0 2.0 %copy-start.5 = (bf16[2368,296]{0,1:T(8,128)(2,1)S(1)}, bf16[2368,296]{0,1:T(8,128)(2,1)}, u32[]{:S(2)}) copy-start(bf16[2368,296]{0,1:T(8,128)(2,1)} %param.15) | copy-start | bytes 4205572
  2.0 16.7 %copy-start.8 = (s32[16,8]{0,1:T(8,128)S(1)}, s32[16,8]{0,1:T(8,128)}, u32[]{:S(2)}) copy-start(s32[16,8]{0,1:T(8,128)} %param.22) | copy-start | bytes 1540
  2.0 16.8 %copy-start.13 = (s32[2,8]{1,0:T(2,128)S(1)}, s32[2,8]{1,0:T(2,128)}, u32[]{:S(2)}) copy-start(s32[2,8]{1,0:T(2,128)} %param.24) | copy-start | bytes 196
  2.0 17.0 %copy-start.9 = (s32[128,8]{0,1:T(8,128)S(1)}, s32[128,8]{0,1:T(8,128)}, u32[]{:S(2)}) copy-start(s32[128,8]{0,1:T(8,128)} %param.20) | copy-start | bytes 12292
  2.0 17.0 %copy-start.7 = (s32[1024,8]{0,1:T(8,128)S(1)}, s32[1024,8]{0,1:T(8,128)}, u32[]{:S(2)}) copy-start(s32[1024,8]{0,1:T(8,128)} %param.18) | copy-start | bytes 98308
  2.0 17.2 %copy-start.12 = (s32[2,8]{1,0:T(2,128)S(1)}, s32[2,8]{1,0:T(2,128)}, u32[]{:S(2)}) copy-start(s32[2,8]{1,0:T(2,128)} %param.25) | copy-start | bytes 196
  2.0 27.0 %copy-start.6 = (s32[1024,8]{0,1:T(8,128)S(1)}, s32[1024,8]{0,1:T(8,128)}, u32[]{:S(2)}) copy-start(s32[1024,8]{0,1:T(8,128)} %param.19) | copy-start | bytes 98308
  5.1 14.3 %collective-permute-start.1 = (bf16[16,296]{1,0:T(8,128)(2,1)S(1)}, bf16[16,296]{1,0:T(8,128)(2,1)S(1)}, u32[]{:S(2)}, u32[]{:S(2)}) collective-permute-start(bf16[16,296]{1,0:T(8,128)(2,1)S(1)} %get-tuple-element.29), channel_id=1, source_target_pairs={{0,224},{4,228},{8,232},{12,236},{16,240},{20,244},{24,248},{28,25... | collective-permute-start | bytes 28424 | tf_op jit(solution)/shard_map/ppermute | solution.py:302
  11.5 7.8 %collective-permute-start = (bf16[16,296]{1,0:T(8,128)(2,1)S(1)}, bf16[16,296]{1,0:T(8,128)(2,1)S(1)}, u32[]{:S(2)}, u32[]{:S(2)}) collective-permute-start(bf16[16,296]{1,0:T(8,128)(2,1)S(1)} %get-tuple-element.29), channel_id=1, source_target_pairs={{0,32},{4,36},{8,40},{12,44},{16,48},{20,52},{24,56},{28,60},{32,6... | collective-permute-start | bytes 28424 | tf_op jit(solution)/shard_map/ppermute | solution.py:302
  11.5 43.7 %collective-permute-start.11 = (bf16[296,512]{1,0:T(8,128)(2,1)S(1)}, bf16[296,512]{1,0:T(8,128)(2,1)S(1)}, u32[]{:S(2)}, u32[]{:S(2)}) collective-permute-start(bf16[296,512]{1,0:T(8,128)(2,1)S(1)} %get-tuple-element.42.lo_ref.b_ref.a_ref), channel_id=1, source_target_pairs={{1,0},{2,1},{3,2},{4,3},{5,4},{6,5},{7,6},{8,7},{9,8},{10,9},{11,1... | collective-permute-start | bytes 909320 | tf_op jit(solution)/shard_map/ppermute | solution.py:293
  16.7 12.4 %collective-permute-start.4 = (bf16[296,512]{1,0:T(8,128)(2,1)S(1)}, bf16[296,512]{1,0:T(8,128)(2,1)S(1)}, u32[]{:S(2)}, u32[]{:S(2)}) collective-permute-start(bf16[296,512]{1,0:T(8,128)(2,1)S(1)} %get-tuple-element.53.hi_ref.c_ref.b_ref), channel_id=1, source_target_pairs={{0,1},{1,2},{2,3},{3,4},{4,5},{5,6},{6,7},{7,8},{8,9},{9,10},{10,1... | collective-permute-start | bytes 909320 | tf_op jit(solution)/shard_map/ppermute | solution.py:293
  19.3 18.8 %collective-permute-start.3 = (bf16[3,16,296]{2,1,0:T(8,128)(2,1)S(1)}, bf16[3,16,296]{2,1,0:T(8,128)(2,1)S(1)}, u32[]{:S(2)}, u32[]{:S(2)}) collective-permute-start(bf16[3,16,296]{2,1,0:T(8,128)(2,1)S(1)} %pad_maximum_fusion.2), channel_id=1, source_target_pairs={{0,160},{4,164},{8,168},{12,172},{16,176},{20,180},{24,184},{28,18... | collective-permute-start | bytes 85256 | tf_op jit(solution)/shard_map/ppermute | solution.py:302
  22.1 16.1 %collective-permute-start.2 = (bf16[2,16,296]{2,1,0:T(8,128)(2,1)S(1)}, bf16[2,16,296]{2,1,0:T(8,128)(2,1)S(1)}, u32[]{:S(2)}, u32[]{:S(2)}) collective-permute-start(bf16[2,16,296]{2,1,0:T(8,128)(2,1)S(1)} %slice.11), channel_id=1, source_target_pairs={{0,96},{4,100},{8,104},{12,108},{16,112},{20,116},{24,120},{28,124... | collective-permute-start | bytes 56840 | tf_op jit(solution)/shard_map/ppermute | solution.py:302
  29.1 2.6 %copy-start = (bf16[9472,296]{0,1:T(8,128)(2,1)S(1)}, bf16[9472,296]{0,1:T(8,128)(2,1)}, u32[]{:S(2)}) copy-start(bf16[9472,296]{0,1:T(8,128)(2,1)} %param.16) | copy-start | bytes 16822276
  38.3 14.1 %collective-permute-start.7 = (bf16[296,128]{1,0:T(8,128)(2,1)S(1)}, bf16[296,128]{1,0:T(8,128)(2,1)S(1)}, u32[]{:S(2)}, u32[]{:S(2)}) collective-permute-start(bf16[296,128]{1,0:T(8,128)(2,1)S(1)} %bitcast.39), channel_id=1, source_target_pairs={{0,8},{4,12},{8,16},{12,20},{16,24},{20,28},{24,0},{28,4},{32,40},... | collective-permute-start | bytes 227336 | tf_op jit(solution)/shard_map/ppermute | solution.py:302
  39.7 12.7 %collective-permute-start.6 = (bf16[296,128]{1,0:T(8,128)(2,1)S(1)}, bf16[296,128]{1,0:T(8,128)(2,1)S(1)}, u32[]{:S(2)}, u32[]{:S(2)}) collective-permute-start(bf16[296,128]{1,0:T(8,128)(2,1)S(1)} %bitcast.40), channel_id=1, source_target_pairs={{0,16},{4,20},{8,24},{12,28},{16,0},{20,4},{24,8},{28,12},{32,48},... | collective-permute-start | bytes 227336 | tf_op jit(solution)/shard_map/ppermute | solution.py:302
  41.4 11.0 %collective-permute-start.5 = (bf16[296,128]{1,0:T(8,128)(2,1)S(1)}, bf16[296,128]{1,0:T(8,128)(2,1)S(1)}, u32[]{:S(2)}, u32[]{:S(2)}) collective-permute-start(bf16[296,128]{1,0:T(8,128)(2,1)S(1)} %bitcast.41), channel_id=1, source_target_pairs={{0,24},{4,28},{8,0},{12,4},{16,8},{20,12},{24,16},{28,20},{32,56},... | collective-permute-start | bytes 227336 | tf_op jit(solution)/shard_map/ppermute | solution.py:302
  43.4 2.6 %copy-start.1 = (bf16[9472,296]{0,1:T(8,128)(2,1)S(1)}, bf16[9472,296]{0,1:T(8,128)(2,1)}, u32[]{:S(2)}) copy-start(bf16[9472,296]{0,1:T(8,128)(2,1)} %param.16) | copy-start | bytes 16822276
  52.5 19.8 %collective-permute-start.10 = (bf16[296,512]{1,0:T(8,128)(2,1)S(1)}, bf16[296,512]{1,0:T(8,128)(2,1)S(1)}, u32[]{:S(2)}, u32[]{:S(2)}) collective-permute-start(bf16[296,512]{1,0:T(8,128)(2,1)S(1)} %pad_maximum_fusion.t0), channel_id=1, source_target_pairs={{0,1},{1,2},{2,3},{3,0},{4,5},{5,6},{6,7},{7,4},{8,9},{9,10},{10,1... | collective-permute-start | bytes 909320 | tf_op jit(solution)/shard_map/ppermute | solution.py:302
  52.6 19.8 %collective-permute-start.9 = (bf16[296,512]{1,0:T(8,128)(2,1)S(1)}, bf16[296,512]{1,0:T(8,128)(2,1)S(1)}, u32[]{:S(2)}, u32[]{:S(2)}) collective-permute-start(bf16[296,512]{1,0:T(8,128)(2,1)S(1)} %pad_maximum_fusion.t0), channel_id=1, source_target_pairs={{0,2},{1,3},{2,0},{3,1},{4,6},{5,7},{6,4},{7,5},{8,10},{9,11},{10,... | collective-permute-start | bytes 909320 | tf_op jit(solution)/shard_map/ppermute | solution.py:302
  53.1 19.3 %collective-permute-start.8 = (bf16[296,512]{1,0:T(8,128)(2,1)S(1)}, bf16[296,512]{1,0:T(8,128)(2,1)S(1)}, u32[]{:S(2)}, u32[]{:S(2)}) collective-permute-start(bf16[296,512]{1,0:T(8,128)(2,1)S(1)} %pad_maximum_fusion.t0), channel_id=1, source_target_pairs={{0,3},{1,0},{2,1},{3,2},{4,7},{5,4},{6,5},{7,6},{8,11},{9,8},{10,9... | collective-permute-start | bytes 909320 | tf_op jit(solution)/shard_map/ppermute | solution.py:302
  55.2 2.6 %copy-start.2 = (bf16[9472,296]{0,1:T(8,128)(2,1)S(1)}, bf16[9472,296]{0,1:T(8,128)(2,1)}, u32[]{:S(2)}) copy-start(bf16[9472,296]{0,1:T(8,128)(2,1)} %param.16) | copy-start | bytes 16822276
  70.7 4.1 %copy-start.4 = (bf16[296,2368]{1,0:T(8,128)(2,1)S(1)}, bf16[296,2368]{1,0:T(8,128)(2,1)}, u32[]{:S(2)}) copy-start(bf16[296,2368]{1,0:T(8,128)(2,1)} %down_ref.1) | copy-start | bytes 4205572
  70.7 6.0 %copy-start.3 = (bf16[9472,296]{0,1:T(8,128)(2,1)S(1)}, bf16[9472,296]{0,1:T(8,128)(2,1)}, u32[]{:S(2)}) copy-start(bf16[9472,296]{0,1:T(8,128)(2,1)} %param.16) | copy-start | bytes 16822276
  72.3 3.1 %copy-start.10 = (s32[128,8]{0,1:T(8,128)S(1)}, s32[128,8]{0,1:T(8,128)}, u32[]{:S(2)}) copy-start(s32[128,8]{0,1:T(8,128)} %param.21) | copy-start | bytes 12292
  72.3 3.1 %copy-start.11 = (s32[16,8]{0,1:T(8,128)S(1)}, s32[16,8]{0,1:T(8,128)}, u32[]{:S(2)}) copy-start(s32[16,8]{0,1:T(8,128)} %param.23) | copy-start | bytes 1540
  72.3 3.1 %collective-permute-start.12 = (bf16[296,512]{1,0:T(8,128)(2,1)S(1)}, bf16[296,512]{1,0:T(8,128)(2,1)S(1)}, u32[]{:S(2)}, u32[]{:S(2)}) collective-permute-start(bf16[296,512]{1,0:T(8,128)(2,1)S(1)} %pad_maximum_fusion.t0), channel_id=1, source_target_pairs={{0,4},{4,0},{8,12},{12,8},{16,20},{20,16},{24,28},{28,24},{32,36},... | collective-permute-start | bytes 909320 | tf_op jit(solution)/shard_map/ppermute | solution.py:302
  74.2 1.7 %collective-permute-start.13 = (bf16[296,512]{1,0:T(8,128)(2,1)S(1)}, bf16[296,512]{1,0:T(8,128)(2,1)S(1)}, u32[]{:S(2)}, u32[]{:S(2)}) collective-permute-start(bf16[296,512]{1,0:T(8,128)(2,1)S(1)} %collective-permute-done.8.t1), channel_id=1, source_target_pairs={{0,4},{4,0},{8,12},{12,8},{16,20},{20,16},{24,28},{28,24},{32,36},... | collective-permute-start | bytes 909320 | tf_op jit(solution)/shard_map/ppermute | solution.py:302
  74.3 2.0 %collective-permute-start.14 = (bf16[296,512]{1,0:T(8,128)(2,1)S(1)}, bf16[296,512]{1,0:T(8,128)(2,1)S(1)}, u32[]{:S(2)}, u32[]{:S(2)}) collective-permute-start(bf16[296,512]{1,0:T(8,128)(2,1)S(1)} %collective-permute-done.9.t2), channel_id=1, source_target_pairs={{0,4},{4,0},{8,12},{12,8},{16,20},{20,16},{24,28},{28,24},{32,36},... | collective-permute-start | bytes 909320 | tf_op jit(solution)/shard_map/ppermute | solution.py:302
  74.7 2.0 %collective-permute-start.15 = (bf16[296,512]{1,0:T(8,128)(2,1)S(1)}, bf16[296,512]{1,0:T(8,128)(2,1)S(1)}, u32[]{:S(2)}, u32[]{:S(2)}) collective-permute-start(bf16[296,512]{1,0:T(8,128)(2,1)S(1)} %collective-permute-done.10.t3), channel_id=1, source_target_pairs={{0,4},{4,0},{8,12},{12,8},{16,20},{20,16},{24,28},{28,24},{32,36},... | collective-permute-start | bytes 909320 | tf_op jit(solution)/shard_map/ppermute | solution.py:302

commit v4 on v3

--- a/solution.py
+++ b/solution.py
@@ -13,6 +13,10 @@
 BF = jnp.bfloat16
 F32 = jnp.float32
 VM = pl.BlockSpec(memory_space=pltpu.VMEM)
+
+
+def place():
+    return lax.axis_index("cells") * 4 + lax.axis_index("sub")
 
 
 def dot(a, b):
@@ -113,7 +117,7 @@
         local, four = i // 2, i % 2
         base = pl.multiple_of(local * 256, 256)
         lanes = pl.ds(pl.multiple_of((block + local) * 256, 256), 256)
-        start = (block + local) * 256
+        start = place() * 1024 - 512 + (block + local) * 256
         wanted = [onehot(src_ref[pl.ds(4 * four + q, 1), lanes] - start, 1280) for q in range(4)]
         value = dot(window[:, pl.ds(base, 1280)], jnp.concatenate(wanted, axis=1))
         for q in range(4):
@@ -156,6 +160,23 @@
     )(a, b, c, src, cls, maps)
 
 
+def turn_body(lower_ref, middle_ref, upper_ref, out_ref):
+    parts = [ref[k].astype(F32) for ref in (lower_ref, middle_ref, upper_ref) for k in range(ref.shape[0])]
+    out_ref[...] = jnp.concatenate(parts, axis=0).T.astype(BF)
+
+
+def turn(lower, three, upper):
+    return pl.pallas_call(
+        turn_body,
+        out_shape=jax.ShapeDtypeStruct((F, 128), BF),
+        in_specs=[VM] * 3,
+        out_specs=VM,
+        compiler_params=pltpu.CompilerParams(vmem_limit_bytes=8 * 2**20),
+        cost_estimate=pl.CostEstimate(flops=10**8, bytes_accessed=10**5, transcendentals=0),
+        name="turn",
+    )(lower, three, upper)
+
+
 def halo_body(below_ref, above_ref, up_ref, out_ref, stack):
     children = jnp.concatenate([below_ref[...], above_ref[...]], axis=1)
     out_ref[...] = ascend(children, up_ref, stack).astype(BF)
@@ -190,12 +211,34 @@
     )(down)
 
 
+def where_held(cell):
+    cells, sub = lax.axis_index("cells"), lax.axis_index("sub")
+    there = cell >> 6
+    dz = ((there >> 3) - (cells >> 3) + 3) & 7
+    dy = ((there >> 1) - (cells >> 1)) & 3
+    dc = (there - cells) & 1
+    dx = ((cell >> 4) - sub) & 3
+    return (dc * 4 + dx) * 512 + dy * 128 + dz * 16 + (cell & 15)
+
+
 def last_body(
-    t0, t1, t2, t3, t4, t5, t6, t7, index_ref, six_ref, halo_ref, src_ref, cls_ref, up_ref, down_ref,
+    t0, t1, t2, t3, t4, t5, t6, t7, six_ref, halo_ref, src6_ref, cls6_ref, src5_ref, cls5_ref, src4_ref, cls4_ref,
+    up_ref, down_ref,
     s0, s1, s2, maps_ref, out_ref,
-    even, odd, grouped, stack, coarse, both, weave, fars, local,
+    even, odd, grouped, stack, coarse, both, weave, fars, local, src_ref, cls_ref,
 ):
     window = jnp.concatenate([six_ref[...], halo_ref[...]], axis=1)
+    rel = src6_ref[...] - (place() * 128 - 64)
+    src_ref[...] = jnp.where(rel < 64, rel + 128, jnp.where(rel < 192, rel - 64, rel))
+    entry = lax.broadcasted_iota(jnp.int32, (8, 8), 0)
+    column = lax.broadcasted_iota(jnp.int32, (8, 8), 1)
+    four_labels = [
+        jnp.sum(jnp.where(entry == column, cls4_ref[t : t + 1, :], 0).astype(F32), axis=1, keepdims=True)
+        for t in range(2)
+    ]
+    unused = jnp.full((8, 110), KINDS, jnp.int32)
+    cls_ref[:, :128] = jnp.concatenate([cls5_ref[...], *(x.astype(jnp.int32) for x in four_labels), unused], axis=1)
+    cls_ref[:, 128:] = cls6_ref[...]
 
     def pick(i, carry):
         wanted = jnp.concatenate([src_ref[pl.ds(2 * i, 1), :], src_ref[pl.ds(2 * i + 1, 1), :]], axis=1)
@@ -206,7 +249,11 @@
 
     lax.fori_loop(0, LIST // 2, pick, 0)
 
-    wanted = index_ref[...]
+    entries_four = jnp.concatenate([src4_ref[0:1, :], src4_ref[1:2, :]], axis=1)
+    wanted = jnp.concatenate(
+        [src5_ref[j : j + 1, :] for j in range(LIST)] + [8 * entries_four + o for o in range(8)], axis=1
+    )
+    wanted = where_held(wanted)
     picked = jnp.zeros((F, 256), F32)
     for k, table in enumerate((t0, t1, t2, t3, t4, t5, t6, t7)):
         picked += dot(table[...], onehot(wanted - 512 * k, 512))
@@ -216,7 +263,7 @@
     four = dot(up_ref[...], stack[...].astype(BF)).astype(BF).astype(F32)
     blank = jnp.zeros((F, 110), F32)
     for j in range(LIST):
-        value = jnp.concatenate([picked[:, 16 * j : 16 * j + 16], four[:, 2 * j : 2 * j + 2], blank], axis=1)
+        value = jnp.concatenate([picked[:, 16 * j : 16 * j + 16], four[:, j : j + 1], four[:, 8 + j : 9 + j], blank], axis=1)
         spread(value, even, odd, j, slice(0, 128))
 
     def sums(p, carry):
@@ -264,11 +311,11 @@
         out_ref[:, lanes] = (woven(lanes) + seven[...]).astype(BF)
 
 
-def last(tables, index, six, halo, src, cls, up, down, sevens, maps):
+def last(tables, six, halo, lists, up, down, sevens, maps):
     return pl.pallas_call(
         last_body,
         out_shape=jax.ShapeDtypeStruct((F, 1024), BF),
-        in_specs=[VM] * 19,
+        in_specs=[VM] * 22,
         out_specs=VM,
         scratch_shapes=[
             pltpu.VMEM((LIST, F + 8, 256), BF),
@@ -280,11 +327,13 @@
             pltpu.VMEM((1024, 1024), BF),
             pltpu.VMEM((2, F, 128), F32),
             pltpu.VMEM((F, 128), BF),
+            pltpu.VMEM((LIST, 128), jnp.int32),
+            pltpu.VMEM((LIST, 256), jnp.int32),
         ],
         compiler_params=pltpu.CompilerParams(vmem_limit_bytes=24 * 2**20),
         cost_estimate=pl.CostEstimate(flops=8 * 10**9, bytes_accessed=12 * 10**6, transcendentals=0),
         name="last",
-    )(*tables, index, six, halo, src, cls, up, down, *sevens, maps)
+    )(*tables, six, halo, *lists, up, down, *sevens, maps)
 
 
 def shifted(value, axis, steps):
@@ -335,12 +384,7 @@
     above = shifted(lo, ("cells", "sub"), -1)
     six, five = rise(lo, hi, up)
 
-    cells, sub = lax.axis_index("cells"), lax.axis_index("sub")
-    place = cells * 4 + sub
-    src_seven = sources_seven.T - (place * 1024 - 512)
-    cls_seven = classes_seven.T
-    rel_six = sources_six.T - (place * 128 - 64)
-    src_six = jnp.where(rel_six < 64, rel_six + 128, jnp.where(rel_six < 192, rel_six - 64, rel_six))
+    src_seven, cls_seven = sources_seven.T, classes_seven.T
 
     down = flip(downward_maps)
     minus, plus = along_z(five, 1), along_z(five, -1)
@@ -350,7 +394,7 @@
     lower = along_z(three[1:], 3)
     seven_0 = near(0, 1, below, near_lo, hi, src_seven, cls_seven, maps)
     lower, upper, seven_0 = tie(lower, upper, seven_0)
-    column = jnp.concatenate([lower, three, upper], axis=0).reshape(128, F).T
+    column = turn(lower, three, upper)
     column, seven_0, near_lo = tie(column, seven_0, near_lo)
     sides = along_y(column, -1), along_y(column, 2), along_y(column, 1)
     seven_1 = near(1, 1, below, near_lo, hi, src_seven, cls_seven, maps)
@@ -364,24 +408,15 @@
     tables = tables + [along_core(table, 1) for table in tables]
     sevens = [seven_0, seven_1, seven_2]
 
-    def where_held(cell):
-        device = cell // 16
-        there = (device // 4, device % 4)
-        dz = (there[0] // 8 - cells // 8 + 3) % 8
-        dy = (there[0] // 2 - cells // 2) % 4
-        dc = (there[0] - cells) % 2
-        dx = (there[1] - sub) % 4
-        return (dc * 4 + dx) * 512 + dy * 128 + dz * 16 + cell % 16
-
-    entries_five = sources_five.T.reshape(1, 128)
-    entries_four = sources_four.T.reshape(1, 16)
-    octants = jnp.arange(8, dtype=jnp.int32)[:, None]
-    children = (8 * entries_four + octants).reshape(1, 128)
-    index = where_held(jnp.concatenate([entries_five, children], axis=1))
-    cls_low = jnp.concatenate(
-        [classes_five.T, classes_four.T, jnp.full((LIST, 110), KINDS, jnp.int32), classes_six.T], axis=1
+    lists = (
+        sources_six.T,
+        classes_six.T,
+        sources_five.T,
+        classes_five.T,
+        sources_four,
+        classes_four,
     )
-    return last(tables, index, six, halo, src_six, cls_low, up, down, sevens, maps).T
+    return last(tables, six, halo, lists, up, down, sevens, maps).T
 
 
 def solution(mesh):

time: 91.7 us -> 82.2 us (0.90)
  local copies, waits for them, and re-layouts: 8.5 us -> 0.12 us
  waiting for transfers between devices: 7.66 us -> 1.39 us
  starting transfers between devices: 27.2 us -> 32 us
    unnamed x30 -> x24, local copies, waits for them, and re-layouts: 7.92 us -> 0.08 us
    ppermute x2, waiting for transfers between devices: 6.38 us -> 0.01 us  [shifted(): lax.ppermute(value, axis, [(source, source + steps) for source in range(f...]
    ppermute x14, starting transfers between devices: 20 us -> 23.8 us  [turned(): return lax.ppermute(value, axis, pairs)]
    ppermute x2, starting transfers between devices: 7.14 us -> 8.23 us  [shifted(): lax.ppermute(value, axis, [(source, source + steps) for source in range(f...]
  transfers between devices with their start and end apart: 16 -> 16, of which waited for: 4 -> 4; matrix products, arithmetic and copies ran while one was open for 1% -> 0% of each run, Pallas kernels for 30% -> 38%
where the time goes in v4:
time: 82.2 us; the launch traced here: 82 us
  Pallas kernels  46.2 us (56%)
  starting transfers between devices  32 us (39%)
  other arithmetic  1.97 us (2%)
  waiting for transfers between devices  1.39 us (2%)
    pallas_call x3, Pallas kernels, near(): pl.pallas_call(functools.partial(near_body, block, count), out_shape=jax....  25.9 us
    ppermute x14, starting transfers between devices, turned(): return lax.ppermute(value, axis, pairs)  23.8 us
    pallas_call x1, Pallas kernels, last(): pl.pallas_call(last_body, out_shape=jax.ShapeDtypeStruct((F, 1024), BF),...  15.1 us
    ppermute x2, starting transfers between devices, shifted(): lax.ppermute(value, axis, [(source, source + steps) for source in range(f...  8.23 us
    pallas_call x1, Pallas kernels, rise(): pl.pallas_call(rise_body, out_shape=(jax.ShapeDtypeStruct((F, 128), BF),...  3.01 us
  transfers between devices with their start and end apart: 16, of which 4 were waited for; matrix products, arithmetic and copies ran while one was open for 0% of the time, Pallas kernels for 38%

profile of v4, /device:TPU:1, one launch (start us, length us, event | category | flops | bytes accessed | tf_op | source)
XLA Modules:
  0.0 82.0 jit_solution(14005987809046498467)
XLA Ops:
  0.0 0.8 convert_element_type.3
  0.8 1.1 %multiply_bitcast_fusion = bf16[296,1024]{1,0:T(8,128)(2,1)S(1)} fusion(bf16[1024,296]{0,1:T(8,128)(2,1)} %param.13, bf16[1024]{0:T(1024)(128)(2,1)S(1)} %convert_element_type.3), kind=kLoop, calls=%fused_computation | loop fusion | flops 303104 | bytes 1214464 | tf_op jit(solution)/shard_map/mul | solution.py:381
  1.9 0.0 slice-start
  2.0 4.2 %collective-permute-start.4 = (bf16[296,512]{1,0:T(8,128)(2,1)S(1)}, bf16[296,512]{1,0:T(8,128)(2,1)S(1)}, u32[]{:S(2)}, u32[]{:S(2)}) collective-permute-start(bf16[296,512]{1,0:T(8,128)(2,1)S(1)} %get-tuple-element.53.hi_ref.c_ref.b_ref), channel_id=1, source_target_pairs={{0,1},{1,2},{2,3},{3,4},{4,5},{5,6},{6,7},{7,8},{8,9},{9,10},{10,1... | collective-permute-start | bytes 909320 | tf_op jit(solution)/shard_map/ppermute | solution.py:342
  6.2 0.0 slice-start.1
  6.2 0.0 copy-start.2
  6.2 0.0 copy-start.3
  6.2 3.0 %rise.1 = (bf16[296,128]{1,0:T(8,128)(2,1)S(1)}, bf16[16,296]{1,0:T(8,128)(2,1)S(1)}) custom-call(bf16[296,512]{1,0:T(8,128)(2,1)S(1)} %get-tuple-element.42.lo_ref.b_ref.a_ref, bf16[296,512]{1,0:T(8,128)(2,1)S(1)} %get-tuple-element.53.hi_ref.c_ref.b_ref, bf16[296,2368]{1,0:T(8,128)(2,1)S(1)} %bitcast.21), custom_call_target="tpu_custom_call" | custom-call | flops 8000000000 | bytes 3000000 | tf_op jit(solution)/shard_map/rise/pallas_call | solution.py:58
  9.3 5.6 %collective-permute-start.1 = (bf16[16,296]{1,0:T(8,128)(2,1)S(1)}, bf16[16,296]{1,0:T(8,128)(2,1)S(1)}, u32[]{:S(2)}, u32[]{:S(2)}) collective-permute-start(bf16[16,296]{1,0:T(8,128)(2,1)S(1)} %get-tuple-element.29), channel_id=1, source_target_pairs={{0,224},{4,228},{8,232},{12,236},{16,240},{20,244},{24,248},{28,25... | collective-permute-start | bytes 28424 | tf_op jit(solution)/shard_map/ppermute | solution.py:351
  14.9 0.0 collective-permute-start
  14.9 4.0 %collective-permute-start.11 = (bf16[296,512]{1,0:T(8,128)(2,1)S(1)}, bf16[296,512]{1,0:T(8,128)(2,1)S(1)}, u32[]{:S(2)}, u32[]{:S(2)}) collective-permute-start(bf16[296,512]{1,0:T(8,128)(2,1)S(1)} %get-tuple-element.42.lo_ref.b_ref.a_ref), channel_id=1, source_target_pairs={{1,0},{2,1},{3,2},{4,3},{5,4},{6,5},{7,6},{8,7},{9,8},{10,9},{11,1... | collective-permute-start | bytes 909320 | tf_op jit(solution)/shard_map/ppermute | solution.py:342
  18.9 0.0 collective-permute-done.1
  18.9 0.0 collective-permute-done
  18.9 2.7 %collective-permute-start.3 = (bf16[3,16,296]{2,1,0:T(8,128)(2,1)S(1)}, bf16[3,16,296]{2,1,0:T(8,128)(2,1)S(1)}, u32[]{:S(2)}, u32[]{:S(2)}) collective-permute-start(bf16[3,16,296]{2,1,0:T(8,128)(2,1)S(1)} %pad_maximum_fusion.1.middle_ref), channel_id=1, source_target_pairs={{0,160},{4,164},{8,168},{12,172},{16,176},{20,180},{24,184},{28,18... | collective-permute-start | bytes 85256 | tf_op jit(solution)/shard_map/ppermute | solution.py:351
  21.7 0.6 collective-permute-start.2
  22.3 6.5 %near0.1.s0 = f32[1,296,256]{2,1,0:T(8,128)S(1)} custom-call(bf16[296,512]{1,0:T(8,128)(2,1)S(1)} %collective-permute-done.4.a_ref.below_ref, bf16[296,512]{1,0:T(8,128)(2,1)S(1)} %get-tuple-element.42.lo_ref.b_ref.a_ref, bf16[296,512]{1,0:T(8,128)(2,1)S(1)} %get-tuple-element.53.hi_ref.c_ref.b_ref, s32[8,1024]{1,0:T(8,128)S(1)} %bitcast.24, ...), custom_call_target="tpu_custom_call" | custom-call | flops 6000000000 | bytes 6000000 | tf_op jit(solution)/shard_map/near0/pallas_call | solution.py:146
  28.8 0.0 collective-permute-done.2.lower_ref
  28.8 0.0 collective-permute-done.3.upper_ref
  28.8 0.1 turn.1
  28.9 1.4 %collective-permute-start.7 = (bf16[296,128]{1,0:T(8,128)(2,1)S(1)}, bf16[296,128]{1,0:T(8,128)(2,1)S(1)}, u32[]{:S(2)}, u32[]{:S(2)}) collective-permute-start(bf16[296,128]{1,0:T(8,128)(2,1)S(1)} %turn.1), channel_id=1, source_target_pairs={{0,8},{4,12},{8,16},{12,20},{16,24},{20,28},{24,0},{28,4},{32,40},... | collective-permute-start | bytes 227336 | tf_op jit(solution)/shard_map/ppermute | solution.py:351
  30.3 2.6 %collective-permute-start.6 = (bf16[296,128]{1,0:T(8,128)(2,1)S(1)}, bf16[296,128]{1,0:T(8,128)(2,1)S(1)}, u32[]{:S(2)}, u32[]{:S(2)}) collective-permute-start(bf16[296,128]{1,0:T(8,128)(2,1)S(1)} %turn.1), channel_id=1, source_target_pairs={{0,16},{4,20},{8,24},{12,28},{16,0},{20,4},{24,8},{28,12},{32,48},... | collective-permute-start | bytes 227336 | tf_op jit(solution)/shard_map/ppermute | solution.py:351
  32.9 1.1 %collective-permute-start.5 = (bf16[296,128]{1,0:T(8,128)(2,1)S(1)}, bf16[296,128]{1,0:T(8,128)(2,1)S(1)}, u32[]{:S(2)}, u32[]{:S(2)}) collective-permute-start(bf16[296,128]{1,0:T(8,128)(2,1)S(1)} %turn.1), channel_id=1, source_target_pairs={{0,24},{4,28},{8,0},{12,4},{16,8},{20,12},{24,16},{28,20},{32,56},... | collective-permute-start | bytes 227336 | tf_op jit(solution)/shard_map/ppermute | solution.py:351
  34.0 6.5 %near1.1.s1 = f32[1,296,256]{2,1,0:T(8,128)S(1)} custom-call(bf16[296,512]{1,0:T(8,128)(2,1)S(1)} %collective-permute-done.4.a_ref.below_ref, bf16[296,512]{1,0:T(8,128)(2,1)S(1)} %get-tuple-element.42.lo_ref.b_ref.a_ref, bf16[296,512]{1,0:T(8,128)(2,1)S(1)} %get-tuple-element.53.hi_ref.c_ref.b_ref, s32[8,1024]{1,0:T(8,128)S(1)} %bitcast.25, ...), custom_call_target="tpu_custom_call" | custom-call | flops 6000000000 | bytes 6000000 | tf_op jit(solution)/shard_map/near1/pallas_call | solution.py:146
  40.5 0.0 collective-permute-done.5
  40.6 1.2 %collective-permute-start.10 = (bf16[296,512]{1,0:T(8,128)(2,1)S(1)}, bf16[296,512]{1,0:T(8,128)(2,1)S(1)}, u32[]{:S(2)}, u32[]{:S(2)}) collective-permute-start(bf16[296,512]{1,0:T(8,128)(2,1)S(1)} %pad_maximum_fusion.t0), channel_id=1, source_target_pairs={{0,1},{1,2},{2,3},{3,0},{4,5},{5,6},{6,7},{7,4},{8,9},{9,10},{10,1... | collective-permute-start | bytes 909320 | tf_op jit(solution)/shard_map/ppermute | solution.py:351
  41.7 3.0 %collective-permute-start.9 = (bf16[296,512]{1,0:T(8,128)(2,1)S(1)}, bf16[296,512]{1,0:T(8,128)(2,1)S(1)}, u32[]{:S(2)}, u32[]{:S(2)}) collective-permute-start(bf16[296,512]{1,0:T(8,128)(2,1)S(1)} %pad_maximum_fusion.t0), channel_id=1, source_target_pairs={{0,2},{1,3},{2,0},{3,1},{4,6},{5,7},{6,4},{7,5},{8,10},{9,11},{10,... | collective-permute-start | bytes 909320 | tf_op jit(solution)/shard_map/ppermute | solution.py:351
  44.8 0.3 collective-permute-start.8
  45.1 12.9 %near2.1.s2 = f32[2,296,256]{2,1,0:T(8,128)S(1)} custom-call(bf16[296,512]{1,0:T(8,128)(2,1)S(1)} %get-tuple-element.42.lo_ref.b_ref.a_ref, bf16[296,512]{1,0:T(8,128)(2,1)S(1)} %get-tuple-element.53.hi_ref.c_ref.b_ref, bf16[296,512]{1,0:T(8,128)(2,1)S(1)} %collective-permute-done.11.c_ref.above_ref, s32[8,1024]{1,0:T(8,128)S(1)} %bitcast.26, ...), custom_call_target="tpu_custom_call" | custom-call | flops 12000000000 | bytes 6000000 | tf_op jit(solution)/shard_map/near2/pallas_call | solution.py:146
  58.0 0.0 copy-start
  58.0 1.6 %halo.1.halo_ref = bf16[296,128]{1,0:T(8,128)(2,1)S(1)} custom-call(bf16[296,512]{1,0:T(8,128)(2,1)S(1)} %collective-permute-done.4.a_ref.below_ref, bf16[296,512]{1,0:T(8,128)(2,1)S(1)} %collective-permute-done.11.c_ref.above_ref, bf16[296,2368]{1,0:T(8,128)(2,1)S(1)} %bitcast.22), custom_call_target="tpu_custom_call" | custom-call | flops 2000000000 | bytes 3000000 | tf_op jit(solution)/shard_map/halo/pallas_call | solution.py:186
  59.6 0.0 copy-start.4
  59.6 0.0 copy-start.5
  59.6 0.0 copy-start.6
  59.6 0.0 copy-start.7
  59.6 0.0 copy-start.8
  59.7 0.0 copy-start.9
  59.7 0.0 collective-permute-done.9.t2
  59.7 0.0 collective-permute-done.8.t1
  59.7 4.7 %collective-permute-start.12 = (bf16[296,512]{1,0:T(8,128)(2,1)S(1)}, bf16[296,512]{1,0:T(8,128)(2,1)S(1)}, u32[]{:S(2)}, u32[]{:S(2)}) collective-permute-start(bf16[296,512]{1,0:T(8,128)(2,1)S(1)} %pad_maximum_fusion.t0), channel_id=1, source_target_pairs={{0,4},{4,0},{8,12},{12,8},{16,20},{20,16},{24,28},{28,24},{32,36},... | collective-permute-start | bytes 909320 | tf_op jit(solution)/shard_map/ppermute | solution.py:351
  64.4 0.1 collective-permute-start.13
  64.5 0.4 collective-permute-start.14
  64.9 0.1 collective-permute-start.15
  65.0 0.5 flip.1.down_ref
  65.6 0.1 collective-permute-done.12.t4
  65.6 0.4 collective-permute-done.13.t5
  66.1 0.4 collective-permute-done.14.t6
  66.5 0.4 collective-permute-done.15.t7
  67.0 15.1 %last.1 = bf16[296,1024]{1,0:T(8,128)(2,1)} custom-call(bf16[296,512]{1,0:T(8,128)(2,1)S(1)} %pad_maximum_fusion.t0, bf16[296,512]{1,0:T(8,128)(2,1)S(1)} %collective-permute-done.8.t1, bf16[296,512]{1,0:T(8,128)(2,1)S(1)} %collective-permute-done.9.t2, bf16[296,512]{1,0:T(8,128)(2,1)S(1)} %collective-permute-done.10.t3, ...), custom_call_target="tpu_custom_call" | custom-call | flops 8000000000 | bytes 12000000 | tf_op jit(solution)/shard_map/last/pallas_call | solution.py:315
  (23 shorter events, 0.1 us)
Async XLA Ops:
  0.0 6.2 %copy-start.1 = (bf16[2368,296]{0,1:T(8,128)(2,1)S(1)}, bf16[2368,296]{0,1:T(8,128)(2,1)}, u32[]{:S(2)}) copy-start(bf16[2368,296]{0,1:T(8,128)(2,1)} %param.15) | copy-start | bytes 4205572
  1.9 20.4 %slice-start = ((s8[5607424]{0:T(1024)(128)(4,1)}), s8[4194304]{0:T(1024)(128)(4,1)S(1)}, s32[]{:S(2)}) async-start(s8[5607424]{0:T(1024)(128)(4,1)} %bitcast.15), calls=%async_computation | async-start | bytes 8388608
  2.0 20.3 %collective-permute-start.4 = (bf16[296,512]{1,0:T(8,128)(2,1)S(1)}, bf16[296,512]{1,0:T(8,128)(2,1)S(1)}, u32[]{:S(2)}, u32[]{:S(2)}) collective-permute-start(bf16[296,512]{1,0:T(8,128)(2,1)S(1)} %get-tuple-element.53.hi_ref.c_ref.b_ref), channel_id=1, source_target_pairs={{0,1},{1,2},{2,3},{3,4},{4,5},{5,6},{6,7},{7,8},{8,9},{9,10},{10,1... | collective-permute-start | bytes 909320 | tf_op jit(solution)/shard_map/ppermute | solution.py:342
  6.2 16.1 %slice-start.1 = ((s8[5607424]{0:T(1024)(128)(4,1)}), s8[1413120]{0:T(1024)(128)(4,1)S(1)}, s32[]{:S(2)}) async-start(s8[5607424]{0:T(1024)(128)(4,1)} %bitcast.15), calls=%async_computation.1 | async-start | bytes 2826240
  6.2 16.1 %copy-start.2 = (s32[1024,8]{0,1:T(8,128)S(1)}, s32[1024,8]{0,1:T(8,128)}, u32[]{:S(2)}) copy-start(s32[1024,8]{0,1:T(8,128)} %param.18) | copy-start | bytes 98308
  6.2 16.1 %copy-start.3 = (s32[1024,8]{0,1:T(8,128)S(1)}, s32[1024,8]{0,1:T(8,128)}, u32[]{:S(2)}) copy-start(s32[1024,8]{0,1:T(8,128)} %param.19) | copy-start | bytes 98308
  9.3 9.6 %collective-permute-start.1 = (bf16[16,296]{1,0:T(8,128)(2,1)S(1)}, bf16[16,296]{1,0:T(8,128)(2,1)S(1)}, u32[]{:S(2)}, u32[]{:S(2)}) collective-permute-start(bf16[16,296]{1,0:T(8,128)(2,1)S(1)} %get-tuple-element.29), channel_id=1, source_target_pairs={{0,224},{4,228},{8,232},{12,236},{16,240},{20,244},{24,248},{28,25... | collective-permute-start | bytes 28424 | tf_op jit(solution)/shard_map/ppermute | solution.py:351
  14.9 4.0 %collective-permute-start = (bf16[16,296]{1,0:T(8,128)(2,1)S(1)}, bf16[16,296]{1,0:T(8,128)(2,1)S(1)}, u32[]{:S(2)}, u32[]{:S(2)}) collective-permute-start(bf16[16,296]{1,0:T(8,128)(2,1)S(1)} %get-tuple-element.29), channel_id=1, source_target_pairs={{0,32},{4,36},{8,40},{12,44},{16,48},{20,52},{24,56},{28,60},{32,6... | collective-permute-start | bytes 28424 | tf_op jit(solution)/shard_map/ppermute | solution.py:351
  14.9 30.2 %collective-permute-start.11 = (bf16[296,512]{1,0:T(8,128)(2,1)S(1)}, bf16[296,512]{1,0:T(8,128)(2,1)S(1)}, u32[]{:S(2)}, u32[]{:S(2)}) collective-permute-start(bf16[296,512]{1,0:T(8,128)(2,1)S(1)} %get-tuple-element.42.lo_ref.b_ref.a_ref), channel_id=1, source_target_pairs={{1,0},{2,1},{3,2},{4,3},{5,4},{6,5},{7,6},{8,7},{9,8},{10,9},{11,1... | collective-permute-start | bytes 909320 | tf_op jit(solution)/shard_map/ppermute | solution.py:342
  18.9 9.9 %collective-permute-start.3 = (bf16[3,16,296]{2,1,0:T(8,128)(2,1)S(1)}, bf16[3,16,296]{2,1,0:T(8,128)(2,1)S(1)}, u32[]{:S(2)}, u32[]{:S(2)}) collective-permute-start(bf16[3,16,296]{2,1,0:T(8,128)(2,1)S(1)} %pad_maximum_fusion.1.middle_ref), channel_id=1, source_target_pairs={{0,160},{4,164},{8,168},{12,172},{16,176},{20,180},{24,184},{28,18... | collective-permute-start | bytes 85256 | tf_op jit(solution)/shard_map/ppermute | solution.py:351
  21.7 7.1 %collective-permute-start.2 = (bf16[2,16,296]{2,1,0:T(8,128)(2,1)S(1)}, bf16[2,16,296]{2,1,0:T(8,128)(2,1)S(1)}, u32[]{:S(2)}, u32[]{:S(2)}) collective-permute-start(bf16[2,16,296]{2,1,0:T(8,128)(2,1)S(1)} %slice.11), channel_id=1, source_target_pairs={{0,96},{4,100},{8,104},{12,108},{16,112},{20,116},{24,120},{28,124... | collective-permute-start | bytes 56840 | tf_op jit(solution)/shard_map/ppermute | solution.py:351
  28.9 11.6 %collective-permute-start.7 = (bf16[296,128]{1,0:T(8,128)(2,1)S(1)}, bf16[296,128]{1,0:T(8,128)(2,1)S(1)}, u32[]{:S(2)}, u32[]{:S(2)}) collective-permute-start(bf16[296,128]{1,0:T(8,128)(2,1)S(1)} %turn.1), channel_id=1, source_target_pairs={{0,8},{4,12},{8,16},{12,20},{16,24},{20,28},{24,0},{28,4},{32,40},... | collective-permute-start | bytes 227336 | tf_op jit(solution)/shard_map/ppermute | solution.py:351
  30.3 10.2 %collective-permute-start.6 = (bf16[296,128]{1,0:T(8,128)(2,1)S(1)}, bf16[296,128]{1,0:T(8,128)(2,1)S(1)}, u32[]{:S(2)}, u32[]{:S(2)}) collective-permute-start(bf16[296,128]{1,0:T(8,128)(2,1)S(1)} %turn.1), channel_id=1, source_target_pairs={{0,16},{4,20},{8,24},{12,28},{16,0},{20,4},{24,8},{28,12},{32,48},... | collective-permute-start | bytes 227336 | tf_op jit(solution)/shard_map/ppermute | solution.py:351
  32.9 7.6 %collective-permute-start.5 = (bf16[296,128]{1,0:T(8,128)(2,1)S(1)}, bf16[296,128]{1,0:T(8,128)(2,1)S(1)}, u32[]{:S(2)}, u32[]{:S(2)}) collective-permute-start(bf16[296,128]{1,0:T(8,128)(2,1)S(1)} %turn.1), channel_id=1, source_target_pairs={{0,24},{4,28},{8,0},{12,4},{16,8},{20,12},{24,16},{28,20},{32,56},... | collective-permute-start | bytes 227336 | tf_op jit(solution)/shard_map/ppermute | solution.py:351
  40.6 19.1 %collective-permute-start.10 = (bf16[296,512]{1,0:T(8,128)(2,1)S(1)}, bf16[296,512]{1,0:T(8,128)(2,1)S(1)}, u32[]{:S(2)}, u32[]{:S(2)}) collective-permute-start(bf16[296,512]{1,0:T(8,128)(2,1)S(1)} %pad_maximum_fusion.t0), channel_id=1, source_target_pairs={{0,1},{1,2},{2,3},{3,0},{4,5},{5,6},{6,7},{7,4},{8,9},{9,10},{10,1... | collective-permute-start | bytes 909320 | tf_op jit(solution)/shard_map/ppermute | solution.py:351
  41.7 18.0 %collective-permute-start.9 = (bf16[296,512]{1,0:T(8,128)(2,1)S(1)}, bf16[296,512]{1,0:T(8,128)(2,1)S(1)}, u32[]{:S(2)}, u32[]{:S(2)}) collective-permute-start(bf16[296,512]{1,0:T(8,128)(2,1)S(1)} %pad_maximum_fusion.t0), channel_id=1, source_target_pairs={{0,2},{1,3},{2,0},{3,1},{4,6},{5,7},{6,4},{7,5},{8,10},{9,11},{10,... | collective-permute-start | bytes 909320 | tf_op jit(solution)/shard_map/ppermute | solution.py:351
  44.8 14.9 %collective-permute-start.8 = (bf16[296,512]{1,0:T(8,128)(2,1)S(1)}, bf16[296,512]{1,0:T(8,128)(2,1)S(1)}, u32[]{:S(2)}, u32[]{:S(2)}) collective-permute-start(bf16[296,512]{1,0:T(8,128)(2,1)S(1)} %pad_maximum_fusion.t0), channel_id=1, source_target_pairs={{0,3},{1,0},{2,1},{3,2},{4,7},{5,4},{6,5},{7,6},{8,11},{9,8},{10,9... | collective-permute-start | bytes 909320 | tf_op jit(solution)/shard_map/ppermute | solution.py:351
  58.0 7.0 %copy-start = (bf16[296,2368]{1,0:T(8,128)(2,1)S(1)}, bf16[296,2368]{1,0:T(8,128)(2,1)}, u32[]{:S(2)}) copy-start(bf16[296,2368]{1,0:T(8,128)(2,1)} %down_ref.1) | copy-start | bytes 4205572
  59.6 7.3 %copy-start.4 = (s32[128,8]{0,1:T(8,128)S(1)}, s32[128,8]{0,1:T(8,128)}, u32[]{:S(2)}) copy-start(s32[128,8]{0,1:T(8,128)} %param.20) | copy-start | bytes 12292
  59.6 7.3 %copy-start.5 = (s32[128,8]{0,1:T(8,128)S(1)}, s32[128,8]{0,1:T(8,128)}, u32[]{:S(2)}) copy-start(s32[128,8]{0,1:T(8,128)} %param.21) | copy-start | bytes 12292
  59.6 7.3 %copy-start.6 = (s32[16,8]{0,1:T(8,128)S(1)}, s32[16,8]{0,1:T(8,128)}, u32[]{:S(2)}) copy-start(s32[16,8]{0,1:T(8,128)} %param.22) | copy-start | bytes 1540
  59.6 7.3 %copy-start.7 = (s32[16,8]{0,1:T(8,128)S(1)}, s32[16,8]{0,1:T(8,128)}, u32[]{:S(2)}) copy-start(s32[16,8]{0,1:T(8,128)} %param.23) | copy-start | bytes 1540
  59.6 7.3 %copy-start.8 = (s32[2,8]{1,0:T(2,128)S(1)}, s32[2,8]{1,0:T(2,128)}, u32[]{:S(2)}) copy-start(s32[2,8]{1,0:T(2,128)} %src4_ref.1) | copy-start | bytes 196
  59.7 7.3 %copy-start.9 = (s32[2,8]{1,0:T(2,128)S(1)}, s32[2,8]{1,0:T(2,128)}, u32[]{:S(2)}) copy-start(s32[2,8]{1,0:T(2,128)} %cls4_ref.1) | copy-start | bytes 196
  59.7 5.9 %collective-permute-start.12 = (bf16[296,512]{1,0:T(8,128)(2,1)S(1)}, bf16[296,512]{1,0:T(8,128)(2,1)S(1)}, u32[]{:S(2)}, u32[]{:S(2)}) collective-permute-start(bf16[296,512]{1,0:T(8,128)(2,1)S(1)} %pad_maximum_fusion.t0), channel_id=1, source_target_pairs={{0,4},{4,0},{8,12},{12,8},{16,20},{20,16},{24,28},{28,24},{32,36},... | collective-permute-start | bytes 909320 | tf_op jit(solution)/shard_map/ppermute | solution.py:351
  64.4 1.7 %collective-permute-start.13 = (bf16[296,512]{1,0:T(8,128)(2,1)S(1)}, bf16[296,512]{1,0:T(8,128)(2,1)S(1)}, u32[]{:S(2)}, u32[]{:S(2)}) collective-permute-start(bf16[296,512]{1,0:T(8,128)(2,1)S(1)} %collective-permute-done.8.t1), channel_id=1, source_target_pairs={{0,4},{4,0},{8,12},{12,8},{16,20},{20,16},{24,28},{28,24},{32,36},... | collective-permute-start | bytes 909320 | tf_op jit(solution)/shard_map/ppermute | solution.py:351
  64.5 2.0 %collective-permute-start.14 = (bf16[296,512]{1,0:T(8,128)(2,1)S(1)}, bf16[296,512]{1,0:T(8,128)(2,1)S(1)}, u32[]{:S(2)}, u32[]{:S(2)}) collective-permute-start(bf16[296,512]{1,0:T(8,128)(2,1)S(1)} %collective-permute-done.9.t2), channel_id=1, source_target_pairs={{0,4},{4,0},{8,12},{12,8},{16,20},{20,16},{24,28},{28,24},{32,36},... | collective-permute-start | bytes 909320 | tf_op jit(solution)/shard_map/ppermute | solution.py:351
  64.9 2.0 %collective-permute-start.15 = (bf16[296,512]{1,0:T(8,128)(2,1)S(1)}, bf16[296,512]{1,0:T(8,128)(2,1)S(1)}, u32[]{:S(2)}, u32[]{:S(2)}) collective-permute-start(bf16[296,512]{1,0:T(8,128)(2,1)S(1)} %collective-permute-done.10.t3), channel_id=1, source_target_pairs={{0,4},{4,0},{8,12},{12,8},{16,20},{20,16},{24,28},{28,24},{32,36},... | collective-permute-start | bytes 909320 | tf_op jit(solution)/shard_map/ppermute | solution.py:351

commit v5 on v4

--- a/solution.py
+++ b/solution.py
@@ -32,9 +32,9 @@
 def split_octants(children, first, width):
     count = children.shape[1]
     source = lax.broadcasted_iota(jnp.int32, (count, 2 * width), 0)
-    place = lax.broadcasted_iota(jnp.int32, (count, 2 * width), 1)
-    second = (place >= width).astype(jnp.int32)
-    wanted = 8 * (place - width * second) + first + second
+    place_in = lax.broadcasted_iota(jnp.int32, (1, 2 * width), 1)
+    second = (place_in >= width).astype(jnp.int32)
+    wanted = 8 * (place_in - width * second) + first + second
     return dot(children, jnp.where(source == wanted, 1.0, 0.0).astype(BF))
 
 
@@ -84,19 +84,29 @@
         grouped[pl.ds(row + 288 + 16 * i, 16), lanes] = odd_tile(i)
 
 
-def group(labels, even, odd, grouped, p):
-    wide = [jnp.broadcast_to(label, (16, 256)) for label in labels]
-
+def prepare(labels, wide):
+    for j in range(LIST):
+        wide[j] = jnp.broadcast_to(labels[j : j + 1, :].astype(F32), (16, 256)).astype(BF)
+
+
+def group(wide, even, odd, grouped, p, few=0):
     def masks(kind):
-        return [jnp.where(label == kind, 1.0, 0.0).astype(BF) for label in wide]
+        wanted = jnp.full((16, 256), kind, F32).astype(BF)
+        return [jnp.where(wide[j] == wanted, jnp.ones((), BF), jnp.zeros((), BF)) for j in range(LIST)]
 
     first, second = masks(2 * p), masks(2 * p + 1)
 
-    def total(ref, mask, i):
-        terms = [ref[j, 16 * i : 16 * i + 16, :] * mask[j] for j in range(LIST)]
+    def part(ref, mask, i, count, lanes):
+        terms = [ref[j, 16 * i : 16 * i + 16, lanes] * mask[j][:, lanes] for j in range(count)]
         while len(terms) > 1:
             terms = [terms[q] + terms[q + 1] for q in range(0, len(terms), 2)]
         return terms[0]
+
+    def total(ref, mask, i):
+        if not few:
+            return part(ref, mask, i, LIST, slice(None))
+        low = part(ref, mask, i, few, slice(0, 128))
+        return jnp.concatenate([low, part(ref, mask, i, LIST, slice(128, 256))], axis=1)
 
     stack_pair(
         grouped,
@@ -107,7 +117,7 @@
     )
 
 
-def near_body(block, count, a_ref, b_ref, c_ref, src_ref, cls_ref, maps_ref, out_ref, window, even, odd, grouped):
+def near_body(block, count, a_ref, b_ref, c_ref, src_ref, cls_ref, maps_ref, out_ref, window, even, odd, grouped, wide):
     side = block % 2
     for k in range(4 + count):
         half = k + side
@@ -129,8 +139,8 @@
     def sums(i, carry):
         local, p = i // 16, i % 16
         lanes = pl.ds(pl.multiple_of((block + local) * 256, 256), 256)
-        labels = [cls_ref[j : j + 1, lanes] for j in range(LIST)]
-        group(labels, even.at[local], odd.at[local], grouped.at[local], p)
+        pl.when(p == 0)(lambda: prepare(cls_ref[:, lanes], wide))
+        group(wide, even.at[local], odd.at[local], grouped.at[local], p)
         return carry
 
     lax.fori_loop(0, 16 * count, sums, 0)
@@ -153,6 +163,7 @@
             pltpu.VMEM((count, LIST, F + 8, 256), BF),
             pltpu.VMEM((count, LIST, F + 8, 256), BF),
             pltpu.VMEM((count, KINDS * F, 256), BF),
+            pltpu.VMEM((LIST, 16, 256), BF),
         ],
         compiler_params=pltpu.CompilerParams(vmem_limit_bytes=(22 if count > 1 else 16) * 2**20),
         cost_estimate=pl.CostEstimate(flops=count * 6 * 10**9, bytes_accessed=6 * 10**6, transcendentals=0),
@@ -225,19 +236,16 @@
     t0, t1, t2, t3, t4, t5, t6, t7, six_ref, halo_ref, src6_ref, cls6_ref, src5_ref, cls5_ref, src4_ref, cls4_ref,
     up_ref, down_ref,
     s0, s1, s2, maps_ref, out_ref,
-    even, odd, grouped, stack, coarse, both, weave, fars, local, src_ref, cls_ref,
+    even, odd, grouped, stack, coarse, both, weave, fars, local, src_ref, cls_ref, wide,
 ):
     window = jnp.concatenate([six_ref[...], halo_ref[...]], axis=1)
     rel = src6_ref[...] - (place() * 128 - 64)
     src_ref[...] = jnp.where(rel < 64, rel + 128, jnp.where(rel < 192, rel - 64, rel))
-    entry = lax.broadcasted_iota(jnp.int32, (8, 8), 0)
-    column = lax.broadcasted_iota(jnp.int32, (8, 8), 1)
-    four_labels = [
-        jnp.sum(jnp.where(entry == column, cls4_ref[t : t + 1, :], 0).astype(F32), axis=1, keepdims=True)
-        for t in range(2)
-    ]
-    unused = jnp.full((8, 110), KINDS, jnp.int32)
-    cls_ref[:, :128] = jnp.concatenate([cls5_ref[...], *(x.astype(jnp.int32) for x in four_labels), unused], axis=1)
+    cls_ref[...] = jnp.full((LIST, 256), KINDS, jnp.int32)
+    for r in range(2):
+        row = [cls5_ref[4 * r + j : 4 * r + j + 1, :] for j in range(4)]
+        cls_ref[r : r + 1, :64] = jnp.concatenate(row, axis=1)
+    cls_ref[0:1, 64:80] = jnp.concatenate([cls4_ref[0:1, :], cls4_ref[1:2, :]], axis=1)
     cls_ref[:, 128:] = cls6_ref[...]
 
     def pick(i, carry):
@@ -261,31 +269,32 @@
     for o in range(8):
         stack[o * F : (o + 1) * F, :16] = picked[:, 128 + 16 * o : 144 + 16 * o]
     four = dot(up_ref[...], stack[...].astype(BF)).astype(BF).astype(F32)
-    blank = jnp.zeros((F, 110), F32)
-    for j in range(LIST):
-        value = jnp.concatenate([picked[:, 16 * j : 16 * j + 16], four[:, j : j + 1], four[:, 8 + j : 9 + j], blank], axis=1)
-        spread(value, even, odd, j, slice(0, 128))
+    low = slice(0, 128)
+    spread(jnp.concatenate([picked[:, :64], four[:, :16], jnp.zeros((F, 48), F32)], axis=1), even, odd, 0, low)
+    spread(jnp.concatenate([picked[:, 64:128], jnp.zeros((F, 64), F32)], axis=1), even, odd, 1, low)
+    prepare(cls_ref[...], wide)
 
     def sums(p, carry):
-        group([cls_ref[j : j + 1, :] for j in range(LIST)], even, odd, grouped, p)
+        group(wide, even, odd, grouped, p, few=2)
         return carry
 
     lax.fori_loop(0, KINDS // 2, sums, 0)
     coarse[...] = dot(maps_ref[...], grouped[...])
 
     def fill(o, carry):
-        row = lax.broadcasted_iota(jnp.int32, (128, 1024), 0)
-        cell = lax.broadcasted_iota(jnp.int32, (128, 1024), 1)
-        weave[pl.ds(pl.multiple_of(o * 128, 128), 128), :] = jnp.where(cell == 8 * row + o, 1.0, 0.0).astype(BF)
+        parent = lax.broadcasted_iota(jnp.int32, (128, 1024), 0)
+        cell = lax.broadcasted_iota(jnp.int32, (1, 1024), 1) - o
+        cell = jnp.where((cell & 7) == 0, cell >> 3, -1)
+        weave[pl.ds(pl.multiple_of(o * 128, 128), 128), :] = jnp.where(parent == cell, 1.0, 0.0).astype(BF)
         return carry
 
     lax.fori_loop(0, 8, fill, 0)
     both[...] = jnp.zeros(both.shape, BF)
-    lane = lax.broadcasted_iota(jnp.int32, (F, 128), 1)
-    fars[0] = jnp.where(lane < 16, coarse[:, :128], 0.0)
+    five = coarse[:, :16] + coarse[:, 16:32] + coarse[:, 32:48] + coarse[:, 48:64]
+    fars[0] = jnp.concatenate([five, jnp.zeros((F, 112), F32)], axis=1)
     fars[1] = coarse[:, 128:]
-    take = lax.broadcasted_iota(jnp.int32, (128, 128), 0) == lax.broadcasted_iota(jnp.int32, (128, 128), 1) + 16
-    local[...] = dot(coarse[:, :128].astype(BF), jnp.where(take, 1.0, 0.0).astype(BF)).astype(BF)
+    four = [jnp.sum(coarse[:, 64 + 8 * t : 72 + 8 * t], axis=1, keepdims=True) for t in range(2)]
+    local[...] = jnp.concatenate([*four, jnp.zeros((F, 126), F32)], axis=1).astype(BF)
 
     def woven(lanes):
         pieces = dot(both[...], weave[:, lanes])
@@ -329,6 +338,7 @@
             pltpu.VMEM((F, 128), BF),
             pltpu.VMEM((LIST, 128), jnp.int32),
             pltpu.VMEM((LIST, 256), jnp.int32),
+            pltpu.VMEM((LIST, 16, 256), BF),
         ],
         compiler_params=pltpu.CompilerParams(vmem_limit_bytes=24 * 2**20),
         cost_estimate=pl.CostEstimate(flops=8 * 10**9, bytes_accessed=12 * 10**6, transcendentals=0),

time: 82.2 us -> 84.7 us (1.030)
  Pallas kernels: 46.2 us -> 48.7 us
    pallas_call x3, Pallas kernels: 25.9 us -> 27.4 us  [near(): pl.pallas_call(functools.partial(near_body, block, count), out_shape=jax....]
    pallas_call x1, Pallas kernels: 15.1 us -> 16.1 us  [last(): pl.pallas_call(last_body, out_shape=jax.ShapeDtypeStruct((F, 1024), BF),...]
  transfers between devices with their start and end apart: 16 -> 16, of which waited for: 4 -> 4; matrix products, arithmetic and copies ran while one was open for 0% -> 0% of each run, Pallas kernels for 38% -> 39%
where the time goes in v5:
time: 84.7 us; the launch traced here: 84.6 us
  Pallas kernels  48.7 us (57%)
  starting transfers between devices  32 us (38%)
  other arithmetic  1.97 us (2%)
  waiting for transfers between devices  1.39 us (2%)
    pallas_call x3, Pallas kernels, near(): pl.pallas_call(functools.partial(near_body, block, count), out_shape=jax....  27.4 us
    ppermute x14, starting transfers between devices, turned(): return lax.ppermute(value, axis, pairs)  23.8 us
    pallas_call x1, Pallas kernels, last(): pl.pallas_call(last_body, out_shape=jax.ShapeDtypeStruct((F, 1024), BF),...  16.1 us
    ppermute x2, starting transfers between devices, shifted(): lax.ppermute(value, axis, [(source, source + steps) for source in range(f...  8.23 us
    pallas_call x1, Pallas kernels, rise(): pl.pallas_call(rise_body, out_shape=(jax.ShapeDtypeStruct((F, 128), BF),...  3.01 us
  transfers between devices with their start and end apart: 16, of which 4 were waited for; matrix products, arithmetic and copies ran while one was open for 0% of the time, Pallas kernels for 39%

profile of v5, /device:TPU:1, one launch (start us, length us, event | category | flops | bytes accessed | tf_op | source)
XLA Modules:
  0.0 84.6 jit_solution(16431985048195947785)
XLA Ops:
  0.0 0.8 convert_element_type.3
  0.8 1.1 %multiply_bitcast_fusion = bf16[296,1024]{1,0:T(8,128)(2,1)S(1)} fusion(bf16[1024,296]{0,1:T(8,128)(2,1)} %param.13, bf16[1024]{0:T(1024)(128)(2,1)S(1)} %convert_element_type.3), kind=kLoop, calls=%fused_computation | loop fusion | flops 303104 | bytes 1214464 | tf_op jit(solution)/shard_map/mul | solution.py:391
  1.9 0.0 slice-start
  2.0 4.2 %collective-permute-start.4 = (bf16[296,512]{1,0:T(8,128)(2,1)S(1)}, bf16[296,512]{1,0:T(8,128)(2,1)S(1)}, u32[]{:S(2)}, u32[]{:S(2)}) collective-permute-start(bf16[296,512]{1,0:T(8,128)(2,1)S(1)} %get-tuple-element.53.hi_ref.c_ref.b_ref), channel_id=1, source_target_pairs={{0,1},{1,2},{2,3},{3,4},{4,5},{5,6},{6,7},{7,8},{8,9},{9,10},{10,1... | collective-permute-start | bytes 909320 | tf_op jit(solution)/shard_map/ppermute | solution.py:352
  6.2 0.0 slice-start.1
  6.2 0.0 copy-start.2
  6.2 0.0 copy-start.3
  6.2 3.0 %rise.1 = (bf16[296,128]{1,0:T(8,128)(2,1)S(1)}, bf16[16,296]{1,0:T(8,128)(2,1)S(1)}) custom-call(bf16[296,512]{1,0:T(8,128)(2,1)S(1)} %get-tuple-element.42.lo_ref.b_ref.a_ref, bf16[296,512]{1,0:T(8,128)(2,1)S(1)} %get-tuple-element.53.hi_ref.c_ref.b_ref, bf16[296,2368]{1,0:T(8,128)(2,1)S(1)} %bitcast.21), custom_call_target="tpu_custom_call" | custom-call | flops 8000000000 | bytes 3000000 | tf_op jit(solution)/shard_map/rise/pallas_call | solution.py:58
  9.3 5.6 %collective-permute-start.1 = (bf16[16,296]{1,0:T(8,128)(2,1)S(1)}, bf16[16,296]{1,0:T(8,128)(2,1)S(1)}, u32[]{:S(2)}, u32[]{:S(2)}) collective-permute-start(bf16[16,296]{1,0:T(8,128)(2,1)S(1)} %get-tuple-element.29), channel_id=1, source_target_pairs={{0,224},{4,228},{8,232},{12,236},{16,240},{20,244},{24,248},{28,25... | collective-permute-start | bytes 28424 | tf_op jit(solution)/shard_map/ppermute | solution.py:361
  14.9 0.0 collective-permute-start
  14.9 4.0 %collective-permute-start.11 = (bf16[296,512]{1,0:T(8,128)(2,1)S(1)}, bf16[296,512]{1,0:T(8,128)(2,1)S(1)}, u32[]{:S(2)}, u32[]{:S(2)}) collective-permute-start(bf16[296,512]{1,0:T(8,128)(2,1)S(1)} %get-tuple-element.42.lo_ref.b_ref.a_ref), channel_id=1, source_target_pairs={{1,0},{2,1},{3,2},{4,3},{5,4},{6,5},{7,6},{8,7},{9,8},{10,9},{11,1... | collective-permute-start | bytes 909320 | tf_op jit(solution)/shard_map/ppermute | solution.py:352
  18.9 0.0 collective-permute-done.1
  18.9 2.7 %collective-permute-start.3 = (bf16[3,16,296]{2,1,0:T(8,128)(2,1)S(1)}, bf16[3,16,296]{2,1,0:T(8,128)(2,1)S(1)}, u32[]{:S(2)}, u32[]{:S(2)}) collective-permute-start(bf16[3,16,296]{2,1,0:T(8,128)(2,1)S(1)} %pad_maximum_fusion.1.middle_ref), channel_id=1, source_target_pairs={{0,160},{4,164},{8,168},{12,172},{16,176},{20,180},{24,184},{28,18... | collective-permute-start | bytes 85256 | tf_op jit(solution)/shard_map/ppermute | solution.py:361
  21.7 0.6 collective-permute-start.2
  22.3 0.0 collective-permute-done.4.a_ref.below_ref
  22.3 6.8 %near0.1.s0 = f32[1,296,256]{2,1,0:T(8,128)S(1)} custom-call(bf16[296,512]{1,0:T(8,128)(2,1)S(1)} %collective-permute-done.4.a_ref.below_ref, bf16[296,512]{1,0:T(8,128)(2,1)S(1)} %get-tuple-element.42.lo_ref.b_ref.a_ref, bf16[296,512]{1,0:T(8,128)(2,1)S(1)} %get-tuple-element.53.hi_ref.c_ref.b_ref, s32[8,1024]{1,0:T(8,128)S(1)} %bitcast.24, ...), custom_call_target="tpu_custom_call" | custom-call | flops 6000000000 | bytes 6000000 | tf_op jit(solution)/shard_map/near0/pallas_call | solution.py:156
  29.2 0.0 collective-permute-done.3.upper_ref
  29.2 0.1 turn.1
  29.3 1.4 %collective-permute-start.7 = (bf16[296,128]{1,0:T(8,128)(2,1)S(1)}, bf16[296,128]{1,0:T(8,128)(2,1)S(1)}, u32[]{:S(2)}, u32[]{:S(2)}) collective-permute-start(bf16[296,128]{1,0:T(8,128)(2,1)S(1)} %turn.1), channel_id=1, source_target_pairs={{0,8},{4,12},{8,16},{12,20},{16,24},{20,28},{24,0},{28,4},{32,40},... | collective-permute-start | bytes 227336 | tf_op jit(solution)/shard_map/ppermute | solution.py:361
  30.7 2.6 %collective-permute-start.6 = (bf16[296,128]{1,0:T(8,128)(2,1)S(1)}, bf16[296,128]{1,0:T(8,128)(2,1)S(1)}, u32[]{:S(2)}, u32[]{:S(2)}) collective-permute-start(bf16[296,128]{1,0:T(8,128)(2,1)S(1)} %turn.1), channel_id=1, source_target_pairs={{0,16},{4,20},{8,24},{12,28},{16,0},{20,4},{24,8},{28,12},{32,48},... | collective-permute-start | bytes 227336 | tf_op jit(solution)/shard_map/ppermute | solution.py:361
  33.3 1.1 %collective-permute-start.5 = (bf16[296,128]{1,0:T(8,128)(2,1)S(1)}, bf16[296,128]{1,0:T(8,128)(2,1)S(1)}, u32[]{:S(2)}, u32[]{:S(2)}) collective-permute-start(bf16[296,128]{1,0:T(8,128)(2,1)S(1)} %turn.1), channel_id=1, source_target_pairs={{0,24},{4,28},{8,0},{12,4},{16,8},{20,12},{24,16},{28,20},{32,56},... | collective-permute-start | bytes 227336 | tf_op jit(solution)/shard_map/ppermute | solution.py:361
  34.4 6.9 %near1.1.s1 = f32[1,296,256]{2,1,0:T(8,128)S(1)} custom-call(bf16[296,512]{1,0:T(8,128)(2,1)S(1)} %collective-permute-done.4.a_ref.below_ref, bf16[296,512]{1,0:T(8,128)(2,1)S(1)} %get-tuple-element.42.lo_ref.b_ref.a_ref, bf16[296,512]{1,0:T(8,128)(2,1)S(1)} %get-tuple-element.53.hi_ref.c_ref.b_ref, s32[8,1024]{1,0:T(8,128)S(1)} %bitcast.25, ...), custom_call_target="tpu_custom_call" | custom-call | flops 6000000000 | bytes 6000000 | tf_op jit(solution)/shard_map/near1/pallas_call | solution.py:156
  41.2 0.0 collective-permute-done.6
  41.3 0.0 collective-permute-done.5
  41.3 1.2 %collective-permute-start.10 = (bf16[296,512]{1,0:T(8,128)(2,1)S(1)}, bf16[296,512]{1,0:T(8,128)(2,1)S(1)}, u32[]{:S(2)}, u32[]{:S(2)}) collective-permute-start(bf16[296,512]{1,0:T(8,128)(2,1)S(1)} %pad_maximum_fusion.t0), channel_id=1, source_target_pairs={{0,1},{1,2},{2,3},{3,0},{4,5},{5,6},{6,7},{7,4},{8,9},{9,10},{10,1... | collective-permute-start | bytes 909320 | tf_op jit(solution)/shard_map/ppermute | solution.py:361
  42.5 3.0 %collective-permute-start.9 = (bf16[296,512]{1,0:T(8,128)(2,1)S(1)}, bf16[296,512]{1,0:T(8,128)(2,1)S(1)}, u32[]{:S(2)}, u32[]{:S(2)}) collective-permute-start(bf16[296,512]{1,0:T(8,128)(2,1)S(1)} %pad_maximum_fusion.t0), channel_id=1, source_target_pairs={{0,2},{1,3},{2,0},{3,1},{4,6},{5,7},{6,4},{7,5},{8,10},{9,11},{10,... | collective-permute-start | bytes 909320 | tf_op jit(solution)/shard_map/ppermute | solution.py:361
  45.5 0.3 collective-permute-start.8
  45.8 0.0 collective-permute-done.11.c_ref.above_ref
  45.8 13.7 %near2.1.s2 = f32[2,296,256]{2,1,0:T(8,128)S(1)} custom-call(bf16[296,512]{1,0:T(8,128)(2,1)S(1)} %get-tuple-element.42.lo_ref.b_ref.a_ref, bf16[296,512]{1,0:T(8,128)(2,1)S(1)} %get-tuple-element.53.hi_ref.c_ref.b_ref, bf16[296,512]{1,0:T(8,128)(2,1)S(1)} %collective-permute-done.11.c_ref.above_ref, s32[8,1024]{1,0:T(8,128)S(1)} %bitcast.26, ...), custom_call_target="tpu_custom_call" | custom-call | flops 12000000000 | bytes 6000000 | tf_op jit(solution)/shard_map/near2/pallas_call | solution.py:156
  59.5 0.0 copy-start
  59.5 1.6 %halo.1.halo_ref = bf16[296,128]{1,0:T(8,128)(2,1)S(1)} custom-call(bf16[296,512]{1,0:T(8,128)(2,1)S(1)} %collective-permute-done.4.a_ref.below_ref, bf16[296,512]{1,0:T(8,128)(2,1)S(1)} %collective-permute-done.11.c_ref.above_ref, bf16[296,2368]{1,0:T(8,128)(2,1)S(1)} %bitcast.22), custom_call_target="tpu_custom_call" | custom-call | flops 2000000000 | bytes 3000000 | tf_op jit(solution)/shard_map/halo/pallas_call | solution.py:197
  61.1 0.0 copy-start.4
  61.1 0.0 copy-start.5
  61.1 0.0 copy-start.6
  61.1 0.0 copy-start.7
  61.2 0.0 copy-start.8
  61.2 0.0 copy-start.9
  61.2 0.0 collective-permute-done.9.t2
  61.2 4.7 %collective-permute-start.12 = (bf16[296,512]{1,0:T(8,128)(2,1)S(1)}, bf16[296,512]{1,0:T(8,128)(2,1)S(1)}, u32[]{:S(2)}, u32[]{:S(2)}) collective-permute-start(bf16[296,512]{1,0:T(8,128)(2,1)S(1)} %pad_maximum_fusion.t0), channel_id=1, source_target_pairs={{0,4},{4,0},{8,12},{12,8},{16,20},{20,16},{24,28},{28,24},{32,36},... | collective-permute-start | bytes 909320 | tf_op jit(solution)/shard_map/ppermute | solution.py:361
  65.9 0.1 collective-permute-start.13
  66.0 0.4 collective-permute-start.14
  66.4 0.1 collective-permute-start.15
  66.5 0.5 flip.1.down_ref
  67.1 0.1 collective-permute-done.12.t4
  67.1 0.4 collective-permute-done.13.t5
  67.6 0.4 collective-permute-done.14.t6
  68.0 0.4 collective-permute-done.15.t7
  68.5 16.1 %last.1 = bf16[296,1024]{1,0:T(8,128)(2,1)} custom-call(bf16[296,512]{1,0:T(8,128)(2,1)S(1)} %pad_maximum_fusion.t0, bf16[296,512]{1,0:T(8,128)(2,1)S(1)} %collective-permute-done.8.t1, bf16[296,512]{1,0:T(8,128)(2,1)S(1)} %collective-permute-done.9.t2, bf16[296,512]{1,0:T(8,128)(2,1)S(1)} %collective-permute-done.10.t3, ...), custom_call_target="tpu_custom_call" | custom-call | flops 8000000000 | bytes 12000000 | tf_op jit(solution)/shard_map/last/pallas_call | solution.py:324
  (23 shorter events, 0.1 us)
Async XLA Ops:
  0.0 6.2 %copy-start.1 = (bf16[2368,296]{0,1:T(8,128)(2,1)S(1)}, bf16[2368,296]{0,1:T(8,128)(2,1)}, u32[]{:S(2)}) copy-start(bf16[2368,296]{0,1:T(8,128)(2,1)} %param.15) | copy-start | bytes 4205572
  1.9 20.4 %slice-start = ((s8[5607424]{0:T(1024)(128)(4,1)}), s8[4194304]{0:T(1024)(128)(4,1)S(1)}, s32[]{:S(2)}) async-start(s8[5607424]{0:T(1024)(128)(4,1)} %bitcast.15), calls=%async_computation | async-start | bytes 8388608
  2.0 20.3 %collective-permute-start.4 = (bf16[296,512]{1,0:T(8,128)(2,1)S(1)}, bf16[296,512]{1,0:T(8,128)(2,1)S(1)}, u32[]{:S(2)}, u32[]{:S(2)}) collective-permute-start(bf16[296,512]{1,0:T(8,128)(2,1)S(1)} %get-tuple-element.53.hi_ref.c_ref.b_ref), channel_id=1, source_target_pairs={{0,1},{1,2},{2,3},{3,4},{4,5},{5,6},{6,7},{7,8},{8,9},{9,10},{10,1... | collective-permute-start | bytes 909320 | tf_op jit(solution)/shard_map/ppermute | solution.py:352
  6.2 16.1 %slice-start.1 = ((s8[5607424]{0:T(1024)(128)(4,1)}), s8[1413120]{0:T(1024)(128)(4,1)S(1)}, s32[]{:S(2)}) async-start(s8[5607424]{0:T(1024)(128)(4,1)} %bitcast.15), calls=%async_computation.1 | async-start | bytes 2826240
  6.2 16.1 %copy-start.2 = (s32[1024,8]{0,1:T(8,128)S(1)}, s32[1024,8]{0,1:T(8,128)}, u32[]{:S(2)}) copy-start(s32[1024,8]{0,1:T(8,128)} %param.18) | copy-start | bytes 98308
  6.2 16.1 %copy-start.3 = (s32[1024,8]{0,1:T(8,128)S(1)}, s32[1024,8]{0,1:T(8,128)}, u32[]{:S(2)}) copy-start(s32[1024,8]{0,1:T(8,128)} %param.19) | copy-start | bytes 98308
  9.3 9.6 %collective-permute-start.1 = (bf16[16,296]{1,0:T(8,128)(2,1)S(1)}, bf16[16,296]{1,0:T(8,128)(2,1)S(1)}, u32[]{:S(2)}, u32[]{:S(2)}) collective-permute-start(bf16[16,296]{1,0:T(8,128)(2,1)S(1)} %get-tuple-element.29), channel_id=1, source_target_pairs={{0,224},{4,228},{8,232},{12,236},{16,240},{20,244},{24,248},{28,25... | collective-permute-start | bytes 28424 | tf_op jit(solution)/shard_map/ppermute | solution.py:361
  14.9 4.0 %collective-permute-start = (bf16[16,296]{1,0:T(8,128)(2,1)S(1)}, bf16[16,296]{1,0:T(8,128)(2,1)S(1)}, u32[]{:S(2)}, u32[]{:S(2)}) collective-permute-start(bf16[16,296]{1,0:T(8,128)(2,1)S(1)} %get-tuple-element.29), channel_id=1, source_target_pairs={{0,32},{4,36},{8,40},{12,44},{16,48},{20,52},{24,56},{28,60},{32,6... | collective-permute-start | bytes 28424 | tf_op jit(solution)/shard_map/ppermute | solution.py:361
  14.9 30.9 %collective-permute-start.11 = (bf16[296,512]{1,0:T(8,128)(2,1)S(1)}, bf16[296,512]{1,0:T(8,128)(2,1)S(1)}, u32[]{:S(2)}, u32[]{:S(2)}) collective-permute-start(bf16[296,512]{1,0:T(8,128)(2,1)S(1)} %get-tuple-element.42.lo_ref.b_ref.a_ref), channel_id=1, source_target_pairs={{1,0},{2,1},{3,2},{4,3},{5,4},{6,5},{7,6},{8,7},{9,8},{10,9},{11,1... | collective-permute-start | bytes 909320 | tf_op jit(solution)/shard_map/ppermute | solution.py:352
  18.9 10.3 %collective-permute-start.3 = (bf16[3,16,296]{2,1,0:T(8,128)(2,1)S(1)}, bf16[3,16,296]{2,1,0:T(8,128)(2,1)S(1)}, u32[]{:S(2)}, u32[]{:S(2)}) collective-permute-start(bf16[3,16,296]{2,1,0:T(8,128)(2,1)S(1)} %pad_maximum_fusion.1.middle_ref), channel_id=1, source_target_pairs={{0,160},{4,164},{8,168},{12,172},{16,176},{20,180},{24,184},{28,18... | collective-permute-start | bytes 85256 | tf_op jit(solution)/shard_map/ppermute | solution.py:361
  21.7 7.5 %collective-permute-start.2 = (bf16[2,16,296]{2,1,0:T(8,128)(2,1)S(1)}, bf16[2,16,296]{2,1,0:T(8,128)(2,1)S(1)}, u32[]{:S(2)}, u32[]{:S(2)}) collective-permute-start(bf16[2,16,296]{2,1,0:T(8,128)(2,1)S(1)} %slice.11), channel_id=1, source_target_pairs={{0,96},{4,100},{8,104},{12,108},{16,112},{20,116},{24,120},{28,124... | collective-permute-start | bytes 56840 | tf_op jit(solution)/shard_map/ppermute | solution.py:361
  29.3 11.9 %collective-permute-start.7 = (bf16[296,128]{1,0:T(8,128)(2,1)S(1)}, bf16[296,128]{1,0:T(8,128)(2,1)S(1)}, u32[]{:S(2)}, u32[]{:S(2)}) collective-permute-start(bf16[296,128]{1,0:T(8,128)(2,1)S(1)} %turn.1), channel_id=1, source_target_pairs={{0,8},{4,12},{8,16},{12,20},{16,24},{20,28},{24,0},{28,4},{32,40},... | collective-permute-start | bytes 227336 | tf_op jit(solution)/shard_map/ppermute | solution.py:361
  30.7 10.6 %collective-permute-start.6 = (bf16[296,128]{1,0:T(8,128)(2,1)S(1)}, bf16[296,128]{1,0:T(8,128)(2,1)S(1)}, u32[]{:S(2)}, u32[]{:S(2)}) collective-permute-start(bf16[296,128]{1,0:T(8,128)(2,1)S(1)} %turn.1), channel_id=1, source_target_pairs={{0,16},{4,20},{8,24},{12,28},{16,0},{20,4},{24,8},{28,12},{32,48},... | collective-permute-start | bytes 227336 | tf_op jit(solution)/shard_map/ppermute | solution.py:361
  33.3 8.0 %collective-permute-start.5 = (bf16[296,128]{1,0:T(8,128)(2,1)S(1)}, bf16[296,128]{1,0:T(8,128)(2,1)S(1)}, u32[]{:S(2)}, u32[]{:S(2)}) collective-permute-start(bf16[296,128]{1,0:T(8,128)(2,1)S(1)} %turn.1), channel_id=1, source_target_pairs={{0,24},{4,28},{8,0},{12,4},{16,8},{20,12},{24,16},{28,20},{32,56},... | collective-permute-start | bytes 227336 | tf_op jit(solution)/shard_map/ppermute | solution.py:361
  41.3 19.9 %collective-permute-start.10 = (bf16[296,512]{1,0:T(8,128)(2,1)S(1)}, bf16[296,512]{1,0:T(8,128)(2,1)S(1)}, u32[]{:S(2)}, u32[]{:S(2)}) collective-permute-start(bf16[296,512]{1,0:T(8,128)(2,1)S(1)} %pad_maximum_fusion.t0), channel_id=1, source_target_pairs={{0,1},{1,2},{2,3},{3,0},{4,5},{5,6},{6,7},{7,4},{8,9},{9,10},{10,1... | collective-permute-start | bytes 909320 | tf_op jit(solution)/shard_map/ppermute | solution.py:361
  42.5 18.7 %collective-permute-start.9 = (bf16[296,512]{1,0:T(8,128)(2,1)S(1)}, bf16[296,512]{1,0:T(8,128)(2,1)S(1)}, u32[]{:S(2)}, u32[]{:S(2)}) collective-permute-start(bf16[296,512]{1,0:T(8,128)(2,1)S(1)} %pad_maximum_fusion.t0), channel_id=1, source_target_pairs={{0,2},{1,3},{2,0},{3,1},{4,6},{5,7},{6,4},{7,5},{8,10},{9,11},{10,... | collective-permute-start | bytes 909320 | tf_op jit(solution)/shard_map/ppermute | solution.py:361
  45.5 15.7 %collective-permute-start.8 = (bf16[296,512]{1,0:T(8,128)(2,1)S(1)}, bf16[296,512]{1,0:T(8,128)(2,1)S(1)}, u32[]{:S(2)}, u32[]{:S(2)}) collective-permute-start(bf16[296,512]{1,0:T(8,128)(2,1)S(1)} %pad_maximum_fusion.t0), channel_id=1, source_target_pairs={{0,3},{1,0},{2,1},{3,2},{4,7},{5,4},{6,5},{7,6},{8,11},{9,8},{10,9... | collective-permute-start | bytes 909320 | tf_op jit(solution)/shard_map/ppermute | solution.py:361
  59.5 7.0 %copy-start = (bf16[296,2368]{1,0:T(8,128)(2,1)S(1)}, bf16[296,2368]{1,0:T(8,128)(2,1)}, u32[]{:S(2)}) copy-start(bf16[296,2368]{1,0:T(8,128)(2,1)} %down_ref.1) | copy-start | bytes 4205572
  61.1 7.3 %copy-start.4 = (s32[128,8]{0,1:T(8,128)S(1)}, s32[128,8]{0,1:T(8,128)}, u32[]{:S(2)}) copy-start(s32[128,8]{0,1:T(8,128)} %param.20) | copy-start | bytes 12292
  61.1 7.3 %copy-start.5 = (s32[128,8]{0,1:T(8,128)S(1)}, s32[128,8]{0,1:T(8,128)}, u32[]{:S(2)}) copy-start(s32[128,8]{0,1:T(8,128)} %param.21) | copy-start | bytes 12292
  61.1 7.3 %copy-start.6 = (s32[16,8]{0,1:T(8,128)S(1)}, s32[16,8]{0,1:T(8,128)}, u32[]{:S(2)}) copy-start(s32[16,8]{0,1:T(8,128)} %param.22) | copy-start | bytes 1540
  61.1 7.3 %copy-start.7 = (s32[16,8]{0,1:T(8,128)S(1)}, s32[16,8]{0,1:T(8,128)}, u32[]{:S(2)}) copy-start(s32[16,8]{0,1:T(8,128)} %param.23) | copy-start | bytes 1540
  61.2 7.3 %copy-start.8 = (s32[2,8]{1,0:T(2,128)S(1)}, s32[2,8]{1,0:T(2,128)}, u32[]{:S(2)}) copy-start(s32[2,8]{1,0:T(2,128)} %src4_ref.1) | copy-start | bytes 196
  61.2 7.3 %copy-start.9 = (s32[2,8]{1,0:T(2,128)S(1)}, s32[2,8]{1,0:T(2,128)}, u32[]{:S(2)}) copy-start(s32[2,8]{1,0:T(2,128)} %cls4_ref.1) | copy-start | bytes 196
  61.2 5.9 %collective-permute-start.12 = (bf16[296,512]{1,0:T(8,128)(2,1)S(1)}, bf16[296,512]{1,0:T(8,128)(2,1)S(1)}, u32[]{:S(2)}, u32[]{:S(2)}) collective-permute-start(bf16[296,512]{1,0:T(8,128)(2,1)S(1)} %pad_maximum_fusion.t0), channel_id=1, source_target_pairs={{0,4},{4,0},{8,12},{12,8},{16,20},{20,16},{24,28},{28,24},{32,36},... | collective-permute-start | bytes 909320 | tf_op jit(solution)/shard_map/ppermute | solution.py:361
  65.9 1.7 %collective-permute-start.13 = (bf16[296,512]{1,0:T(8,128)(2,1)S(1)}, bf16[296,512]{1,0:T(8,128)(2,1)S(1)}, u32[]{:S(2)}, u32[]{:S(2)}) collective-permute-start(bf16[296,512]{1,0:T(8,128)(2,1)S(1)} %collective-permute-done.8.t1), channel_id=1, source_target_pairs={{0,4},{4,0},{8,12},{12,8},{16,20},{20,16},{24,28},{28,24},{32,36},... | collective-permute-start | bytes 909320 | tf_op jit(solution)/shard_map/ppermute | solution.py:361
  66.0 2.0 %collective-permute-start.14 = (bf16[296,512]{1,0:T(8,128)(2,1)S(1)}, bf16[296,512]{1,0:T(8,128)(2,1)S(1)}, u32[]{:S(2)}, u32[]{:S(2)}) collective-permute-start(bf16[296,512]{1,0:T(8,128)(2,1)S(1)} %collective-permute-done.9.t2), channel_id=1, source_target_pairs={{0,4},{4,0},{8,12},{12,8},{16,20},{20,16},{24,28},{28,24},{32,36},... | collective-permute-start | bytes 909320 | tf_op jit(solution)/shard_map/ppermute | solution.py:361
  66.4 2.0 %collective-permute-start.15 = (bf16[296,512]{1,0:T(8,128)(2,1)S(1)}, bf16[296,512]{1,0:T(8,128)(2,1)S(1)}, u32[]{:S(2)}, u32[]{:S(2)}) collective-permute-start(bf16[296,512]{1,0:T(8,128)(2,1)S(1)} %collective-permute-done.10.t3), channel_id=1, source_target_pairs={{0,4},{4,0},{8,12},{12,8},{16,20},{20,16},{24,28},{28,24},{32,36},... | collective-permute-start | bytes 909320 | tf_op jit(solution)/shard_map/ppermute | solution.py:361

commit v6 on v4

--- a/solution.py
+++ b/solution.py
@@ -39,10 +39,12 @@
 
 
 def ascend(children, up_ref, stack):
-    for pair in range(4):
-        both = split_octants(children, 2 * pair, 128)
-        stack[2 * pair * F : (2 * pair + 1) * F, :] = both[:, :128]
-        stack[(2 * pair + 1) * F : (2 * pair + 2) * F, :] = both[:, 128:]
+    count = children.shape[1]
+    source = lax.broadcasted_iota(jnp.int32, (count, 1024), 0)
+    column = lax.broadcasted_iota(jnp.int32, (1, 1024), 1)
+    both = dot(children, jnp.where(source == 8 * (column & 127) + (column >> 7), 1.0, 0.0).astype(BF))
+    for o in range(8):
+        stack[o * F : (o + 1) * F, :] = both[:, 128 * o : 128 * o + 128]
     return dot(up_ref[...], stack[...].astype(BF))
 
 
@@ -50,7 +52,12 @@
     children = jnp.concatenate([lo_ref[...], hi_ref[...]], axis=1)
     six = ascend(children, up_ref, stack).astype(BF)
     six_ref[...] = six
-    five = ascend(six, up_ref, stack)
+    source = lax.broadcasted_iota(jnp.int32, (128, 128), 0)
+    column = lax.broadcasted_iota(jnp.int32, (1, 128), 1)
+    both = dot(six, jnp.where(source == 8 * (column & 15) + (column >> 4), 1.0, 0.0).astype(BF))
+    for o in range(8):
+        stack[o * F : (o + 1) * F, :16] = both[:, 16 * o : 16 * o + 16]
+    five = dot(up_ref[...], stack[...].astype(BF))
     five_ref[...] = five.T[:16, :].astype(BF)
 
 
@@ -400,12 +407,12 @@
     seven_1 = near(1, 1, below, near_lo, hi, src_seven, cls_seven, maps)
     *sides, seven_1 = tie(*sides, seven_1)
     plane = jnp.concatenate([column, *sides], axis=1)
-    plane, seven_1, near_lo, near_up = tie(plane, seven_1, near_lo, up)
+    plane, seven_1, near_lo = tie(plane, seven_1, near_lo)
     tables = [plane, along_x(plane, -1), along_x(plane, 2), along_x(plane, 1)]
-    halo = halo_six(below, above, near_up)
     seven_2 = near(2, 2, near_lo, hi, above, src_seven, cls_seven, maps)
-    *tables, seven_2, halo = tie(*tables, seven_2, halo)
+    *tables, seven_2, late_up = tie(*tables, seven_2, up)
     tables = tables + [along_core(table, 1) for table in tables]
+    halo = halo_six(below, above, late_up)
     sevens = [seven_0, seven_1, seven_2]
 
     lists = (

time: 82.2 us -> 80.7 us (0.982)
  waiting for transfers between devices: 1.39 us -> 0.04 us
    ppermute x14, waiting for transfers between devices: 1.38 us -> 0.04 us  [turned(): return lax.ppermute(value, axis, pairs)]
  transfers between devices with their start and end apart: 16 -> 16, of which waited for: 4 -> 0; matrix products, arithmetic and copies ran while one was open for 0% -> 0% of each run, Pallas kernels for 38% -> 38%
where the time goes in v6:
time: 80.7 us; the launch traced here: 80.5 us
  Pallas kernels  46 us (57%)
  starting transfers between devices  32.1 us (40%)
  other arithmetic  1.97 us (2%)
    pallas_call x3, Pallas kernels, near(): pl.pallas_call(functools.partial(near_body, block, count), out_shape=jax....  25.9 us
    ppermute x14, starting transfers between devices, turned(): return lax.ppermute(value, axis, pairs)  23.8 us
    pallas_call x1, Pallas kernels, last(): pl.pallas_call(last_body, out_shape=jax.ShapeDtypeStruct((F, 1024), BF),...  15.1 us
    ppermute x2, starting transfers between devices, shifted(): lax.ppermute(value, axis, [(source, source + steps) for source in range(f...  8.23 us
    pallas_call x1, Pallas kernels, rise(): pl.pallas_call(rise_body, out_shape=(jax.ShapeDtypeStruct((F, 128), BF),...  2.8 us
  transfers between devices with their start and end apart: 16, of which 0 were waited for; matrix products, arithmetic and copies ran while one was open for 0% of the time, Pallas kernels for 38%

profile of v6, /device:TPU:1, one launch (start us, length us, event | category | flops | bytes accessed | tf_op | source)
XLA Modules:
  0.0 80.5 jit_solution(12265558588521964784)
XLA Ops:
  0.0 0.8 convert_element_type.3
  0.8 1.1 %multiply_bitcast_fusion = bf16[296,1024]{1,0:T(8,128)(2,1)S(1)} fusion(bf16[1024,296]{0,1:T(8,128)(2,1)} %param.13, bf16[1024]{0:T(1024)(128)(2,1)S(1)} %convert_element_type.3), kind=kLoop, calls=%fused_computation | loop fusion | flops 303104 | bytes 1214464 | tf_op jit(solution)/shard_map/mul | solution.py:388
  1.9 0.0 slice-start
  2.0 4.2 %collective-permute-start.4 = (bf16[296,512]{1,0:T(8,128)(2,1)S(1)}, bf16[296,512]{1,0:T(8,128)(2,1)S(1)}, u32[]{:S(2)}, u32[]{:S(2)}) collective-permute-start(bf16[296,512]{1,0:T(8,128)(2,1)S(1)} %get-tuple-element.51.hi_ref.c_ref.b_ref), channel_id=1, source_target_pairs={{0,1},{1,2},{2,3},{3,4},{4,5},{5,6},{6,7},{7,8},{8,9},{9,10},{10,1... | collective-permute-start | bytes 909320 | tf_op jit(solution)/shard_map/ppermute | solution.py:349
  6.2 0.0 slice-start.1
  6.2 0.0 copy-start.2
  6.2 0.0 copy-start.3
  6.2 2.8 %rise.1 = (bf16[296,128]{1,0:T(8,128)(2,1)S(1)}, bf16[16,296]{1,0:T(8,128)(2,1)S(1)}) custom-call(bf16[296,512]{1,0:T(8,128)(2,1)S(1)} %get-tuple-element.41.lo_ref.b_ref.a_ref, bf16[296,512]{1,0:T(8,128)(2,1)S(1)} %get-tuple-element.51.hi_ref.c_ref.b_ref, bf16[296,2368]{1,0:T(8,128)(2,1)S(1)} %bitcast.21), custom_call_target="tpu_custom_call" | custom-call | flops 8000000000 | bytes 3000000 | tf_op jit(solution)/shard_map/rise/pallas_call | solution.py:65
  9.1 5.6 %collective-permute-start.1 = (bf16[16,296]{1,0:T(8,128)(2,1)S(1)}, bf16[16,296]{1,0:T(8,128)(2,1)S(1)}, u32[]{:S(2)}, u32[]{:S(2)}) collective-permute-start(bf16[16,296]{1,0:T(8,128)(2,1)S(1)} %get-tuple-element.28), channel_id=1, source_target_pairs={{0,224},{4,228},{8,232},{12,236},{16,240},{20,244},{24,248},{28,25... | collective-permute-start | bytes 28424 | tf_op jit(solution)/shard_map/ppermute | solution.py:358
  14.7 0.0 collective-permute-start
  14.7 4.0 %collective-permute-start.11 = (bf16[296,512]{1,0:T(8,128)(2,1)S(1)}, bf16[296,512]{1,0:T(8,128)(2,1)S(1)}, u32[]{:S(2)}, u32[]{:S(2)}) collective-permute-start(bf16[296,512]{1,0:T(8,128)(2,1)S(1)} %get-tuple-element.41.lo_ref.b_ref.a_ref), channel_id=1, source_target_pairs={{1,0},{2,1},{3,2},{4,3},{5,4},{6,5},{7,6},{8,7},{9,8},{10,9},{11,1... | collective-permute-start | bytes 909320 | tf_op jit(solution)/shard_map/ppermute | solution.py:349
  18.7 0.0 collective-permute-done.1
  18.7 0.0 collective-permute-done
  18.7 2.7 %collective-permute-start.3 = (bf16[3,16,296]{2,1,0:T(8,128)(2,1)S(1)}, bf16[3,16,296]{2,1,0:T(8,128)(2,1)S(1)}, u32[]{:S(2)}, u32[]{:S(2)}) collective-permute-start(bf16[3,16,296]{2,1,0:T(8,128)(2,1)S(1)} %pad_maximum_fusion.1.middle_ref), channel_id=1, source_target_pairs={{0,160},{4,164},{8,168},{12,172},{16,176},{20,180},{24,184},{28,18... | collective-permute-start | bytes 85256 | tf_op jit(solution)/shard_map/ppermute | solution.py:358
  21.5 0.6 collective-permute-start.2
  22.1 0.0 collective-permute-done.4.a_ref.below_ref
  22.1 6.5 %near0.1.s0 = f32[1,296,256]{2,1,0:T(8,128)S(1)} custom-call(bf16[296,512]{1,0:T(8,128)(2,1)S(1)} %collective-permute-done.4.a_ref.below_ref, bf16[296,512]{1,0:T(8,128)(2,1)S(1)} %get-tuple-element.41.lo_ref.b_ref.a_ref, bf16[296,512]{1,0:T(8,128)(2,1)S(1)} %get-tuple-element.51.hi_ref.c_ref.b_ref, s32[8,1024]{1,0:T(8,128)S(1)} %bitcast.24, ...), custom_call_target="tpu_custom_call" | custom-call | flops 6000000000 | bytes 6000000 | tf_op jit(solution)/shard_map/near0/pallas_call | solution.py:153
  28.6 0.0 collective-permute-done.2.lower_ref
  28.6 0.0 collective-permute-done.3.upper_ref
  28.6 0.1 turn.1
  28.7 1.4 %collective-permute-start.7 = (bf16[296,128]{1,0:T(8,128)(2,1)S(1)}, bf16[296,128]{1,0:T(8,128)(2,1)S(1)}, u32[]{:S(2)}, u32[]{:S(2)}) collective-permute-start(bf16[296,128]{1,0:T(8,128)(2,1)S(1)} %turn.1), channel_id=1, source_target_pairs={{0,8},{4,12},{8,16},{12,20},{16,24},{20,28},{24,0},{28,4},{32,40},... | collective-permute-start | bytes 227336 | tf_op jit(solution)/shard_map/ppermute | solution.py:358
  30.1 2.6 %collective-permute-start.6 = (bf16[296,128]{1,0:T(8,128)(2,1)S(1)}, bf16[296,128]{1,0:T(8,128)(2,1)S(1)}, u32[]{:S(2)}, u32[]{:S(2)}) collective-permute-start(bf16[296,128]{1,0:T(8,128)(2,1)S(1)} %turn.1), channel_id=1, source_target_pairs={{0,16},{4,20},{8,24},{12,28},{16,0},{20,4},{24,8},{28,12},{32,48},... | collective-permute-start | bytes 227336 | tf_op jit(solution)/shard_map/ppermute | solution.py:358
  32.7 1.1 %collective-permute-start.5 = (bf16[296,128]{1,0:T(8,128)(2,1)S(1)}, bf16[296,128]{1,0:T(8,128)(2,1)S(1)}, u32[]{:S(2)}, u32[]{:S(2)}) collective-permute-start(bf16[296,128]{1,0:T(8,128)(2,1)S(1)} %turn.1), channel_id=1, source_target_pairs={{0,24},{4,28},{8,0},{12,4},{16,8},{20,12},{24,16},{28,20},{32,56},... | collective-permute-start | bytes 227336 | tf_op jit(solution)/shard_map/ppermute | solution.py:358
  33.8 6.5 %near1.1.s1 = f32[1,296,256]{2,1,0:T(8,128)S(1)} custom-call(bf16[296,512]{1,0:T(8,128)(2,1)S(1)} %collective-permute-done.4.a_ref.below_ref, bf16[296,512]{1,0:T(8,128)(2,1)S(1)} %get-tuple-element.41.lo_ref.b_ref.a_ref, bf16[296,512]{1,0:T(8,128)(2,1)S(1)} %get-tuple-element.51.hi_ref.c_ref.b_ref, s32[8,1024]{1,0:T(8,128)S(1)} %bitcast.25, ...), custom_call_target="tpu_custom_call" | custom-call | flops 6000000000 | bytes 6000000 | tf_op jit(solution)/shard_map/near1/pallas_call | solution.py:153
  40.3 0.0 collective-permute-done.5
  40.4 0.0 copy-start
  40.4 1.2 %collective-permute-start.10 = (bf16[296,512]{1,0:T(8,128)(2,1)S(1)}, bf16[296,512]{1,0:T(8,128)(2,1)S(1)}, u32[]{:S(2)}, u32[]{:S(2)}) collective-permute-start(bf16[296,512]{1,0:T(8,128)(2,1)S(1)} %pad_maximum_fusion.t0), channel_id=1, source_target_pairs={{0,1},{1,2},{2,3},{3,0},{4,5},{5,6},{6,7},{7,4},{8,9},{9,10},{10,1... | collective-permute-start | bytes 909320 | tf_op jit(solution)/shard_map/ppermute | solution.py:358
  41.5 3.1 %collective-permute-start.9 = (bf16[296,512]{1,0:T(8,128)(2,1)S(1)}, bf16[296,512]{1,0:T(8,128)(2,1)S(1)}, u32[]{:S(2)}, u32[]{:S(2)}) collective-permute-start(bf16[296,512]{1,0:T(8,128)(2,1)S(1)} %pad_maximum_fusion.t0), channel_id=1, source_target_pairs={{0,2},{1,3},{2,0},{3,1},{4,6},{5,7},{6,4},{7,5},{8,10},{9,11},{10,... | collective-permute-start | bytes 909320 | tf_op jit(solution)/shard_map/ppermute | solution.py:358
  44.6 0.3 collective-permute-start.8
  44.8 0.0 collective-permute-done.11.c_ref.above_ref
  44.8 12.9 %near2.1.s2 = f32[2,296,256]{2,1,0:T(8,128)S(1)} custom-call(bf16[296,512]{1,0:T(8,128)(2,1)S(1)} %get-tuple-element.41.lo_ref.b_ref.a_ref, bf16[296,512]{1,0:T(8,128)(2,1)S(1)} %get-tuple-element.51.hi_ref.c_ref.b_ref, bf16[296,512]{1,0:T(8,128)(2,1)S(1)} %collective-permute-done.11.c_ref.above_ref, s32[8,1024]{1,0:T(8,128)S(1)} %bitcast.26, ...), custom_call_target="tpu_custom_call" | custom-call | flops 12000000000 | bytes 6000000 | tf_op jit(solution)/shard_map/near2/pallas_call | solution.py:153
  57.8 0.0 collective-permute-done.9.t2
  57.8 0.0 collective-permute-done.8.t1
  57.8 4.7 %collective-permute-start.12 = (bf16[296,512]{1,0:T(8,128)(2,1)S(1)}, bf16[296,512]{1,0:T(8,128)(2,1)S(1)}, u32[]{:S(2)}, u32[]{:S(2)}) collective-permute-start(bf16[296,512]{1,0:T(8,128)(2,1)S(1)} %pad_maximum_fusion.t0), channel_id=1, source_target_pairs={{0,4},{4,0},{8,12},{12,8},{16,20},{20,16},{24,28},{28,24},{32,36},... | collective-permute-start | bytes 909320 | tf_op jit(solution)/shard_map/ppermute | solution.py:358
  62.5 0.1 collective-permute-start.13
  62.6 0.4 collective-permute-start.14
  63.0 0.1 collective-permute-start.15
  63.2 0.5 flip.1.down_ref
  63.7 0.0 copy-start.4
  63.7 0.0 copy-start.5
  63.7 0.0 copy-start.6
  63.7 0.0 copy-start.7
  63.8 0.0 copy-start.8
  63.8 0.0 copy-start.9
  63.8 1.6 %halo.1.halo_ref = bf16[296,128]{1,0:T(8,128)(2,1)S(1)} custom-call(bf16[296,512]{1,0:T(8,128)(2,1)S(1)} %collective-permute-done.4.a_ref.below_ref, bf16[296,512]{1,0:T(8,128)(2,1)S(1)} %collective-permute-done.11.c_ref.above_ref, bf16[296,2368]{1,0:T(8,128)(2,1)S(1)} %bitcast.22), custom_call_target="tpu_custom_call" | custom-call | flops 2000000000 | bytes 3000000 | tf_op jit(solution)/shard_map/halo/pallas_call | solution.py:193
  65.4 0.0 collective-permute-done.13.t5
  65.4 0.0 collective-permute-done.14.t6
  65.5 15.1 %last.1 = bf16[296,1024]{1,0:T(8,128)(2,1)} custom-call(bf16[296,512]{1,0:T(8,128)(2,1)S(1)} %pad_maximum_fusion.t0, bf16[296,512]{1,0:T(8,128)(2,1)S(1)} %collective-permute-done.8.t1, bf16[296,512]{1,0:T(8,128)(2,1)S(1)} %collective-permute-done.9.t2, bf16[296,512]{1,0:T(8,128)(2,1)S(1)} %collective-permute-done.10.t3, ...), custom_call_target="tpu_custom_call" | custom-call | flops 8000000000 | bytes 12000000 | tf_op jit(solution)/shard_map/last/pallas_call | solution.py:322
  (23 shorter events, 0.1 us)
Async XLA Ops:
  0.0 6.2 %copy-start.1 = (bf16[2368,296]{0,1:T(8,128)(2,1)S(1)}, bf16[2368,296]{0,1:T(8,128)(2,1)}, u32[]{:S(2)}) copy-start(bf16[2368,296]{0,1:T(8,128)(2,1)} %param.15) | copy-start | bytes 4205572
  1.9 20.2 %slice-start = ((s8[5607424]{0:T(1024)(128)(4,1)}), s8[4194304]{0:T(1024)(128)(4,1)S(1)}, s32[]{:S(2)}) async-start(s8[5607424]{0:T(1024)(128)(4,1)} %bitcast.15), calls=%async_computation | async-start | bytes 8388608
  2.0 20.1 %collective-permute-start.4 = (bf16[296,512]{1,0:T(8,128)(2,1)S(1)}, bf16[296,512]{1,0:T(8,128)(2,1)S(1)}, u32[]{:S(2)}, u32[]{:S(2)}) collective-permute-start(bf16[296,512]{1,0:T(8,128)(2,1)S(1)} %get-tuple-element.51.hi_ref.c_ref.b_ref), channel_id=1, source_target_pairs={{0,1},{1,2},{2,3},{3,4},{4,5},{5,6},{6,7},{7,8},{8,9},{9,10},{10,1... | collective-permute-start | bytes 909320 | tf_op jit(solution)/shard_map/ppermute | solution.py:349
  6.2 15.9 %slice-start.1 = ((s8[5607424]{0:T(1024)(128)(4,1)}), s8[1413120]{0:T(1024)(128)(4,1)S(1)}, s32[]{:S(2)}) async-start(s8[5607424]{0:T(1024)(128)(4,1)} %bitcast.15), calls=%async_computation.1 | async-start | bytes 2826240
  6.2 15.9 %copy-start.2 = (s32[1024,8]{0,1:T(8,128)S(1)}, s32[1024,8]{0,1:T(8,128)}, u32[]{:S(2)}) copy-start(s32[1024,8]{0,1:T(8,128)} %param.18) | copy-start | bytes 98308
  6.2 15.9 %copy-start.3 = (s32[1024,8]{0,1:T(8,128)S(1)}, s32[1024,8]{0,1:T(8,128)}, u32[]{:S(2)}) copy-start(s32[1024,8]{0,1:T(8,128)} %param.19) | copy-start | bytes 98308
  9.1 9.6 %collective-permute-start.1 = (bf16[16,296]{1,0:T(8,128)(2,1)S(1)}, bf16[16,296]{1,0:T(8,128)(2,1)S(1)}, u32[]{:S(2)}, u32[]{:S(2)}) collective-permute-start(bf16[16,296]{1,0:T(8,128)(2,1)S(1)} %get-tuple-element.28), channel_id=1, source_target_pairs={{0,224},{4,228},{8,232},{12,236},{16,240},{20,244},{24,248},{28,25... | collective-permute-start | bytes 28424 | tf_op jit(solution)/shard_map/ppermute | solution.py:358
  14.7 4.0 %collective-permute-start = (bf16[16,296]{1,0:T(8,128)(2,1)S(1)}, bf16[16,296]{1,0:T(8,128)(2,1)S(1)}, u32[]{:S(2)}, u32[]{:S(2)}) collective-permute-start(bf16[16,296]{1,0:T(8,128)(2,1)S(1)} %get-tuple-element.28), channel_id=1, source_target_pairs={{0,32},{4,36},{8,40},{12,44},{16,48},{20,52},{24,56},{28,60},{32,6... | collective-permute-start | bytes 28424 | tf_op jit(solution)/shard_map/ppermute | solution.py:358
  14.7 30.2 %collective-permute-start.11 = (bf16[296,512]{1,0:T(8,128)(2,1)S(1)}, bf16[296,512]{1,0:T(8,128)(2,1)S(1)}, u32[]{:S(2)}, u32[]{:S(2)}) collective-permute-start(bf16[296,512]{1,0:T(8,128)(2,1)S(1)} %get-tuple-element.41.lo_ref.b_ref.a_ref), channel_id=1, source_target_pairs={{1,0},{2,1},{3,2},{4,3},{5,4},{6,5},{7,6},{8,7},{9,8},{10,9},{11,1... | collective-permute-start | bytes 909320 | tf_op jit(solution)/shard_map/ppermute | solution.py:349
  18.7 9.9 %collective-permute-start.3 = (bf16[3,16,296]{2,1,0:T(8,128)(2,1)S(1)}, bf16[3,16,296]{2,1,0:T(8,128)(2,1)S(1)}, u32[]{:S(2)}, u32[]{:S(2)}) collective-permute-start(bf16[3,16,296]{2,1,0:T(8,128)(2,1)S(1)} %pad_maximum_fusion.1.middle_ref), channel_id=1, source_target_pairs={{0,160},{4,164},{8,168},{12,172},{16,176},{20,180},{24,184},{28,18... | collective-permute-start | bytes 85256 | tf_op jit(solution)/shard_map/ppermute | solution.py:358
  21.5 7.1 %collective-permute-start.2 = (bf16[2,16,296]{2,1,0:T(8,128)(2,1)S(1)}, bf16[2,16,296]{2,1,0:T(8,128)(2,1)S(1)}, u32[]{:S(2)}, u32[]{:S(2)}) collective-permute-start(bf16[2,16,296]{2,1,0:T(8,128)(2,1)S(1)} %slice.11), channel_id=1, source_target_pairs={{0,96},{4,100},{8,104},{12,108},{16,112},{20,116},{24,120},{28,124... | collective-permute-start | bytes 56840 | tf_op jit(solution)/shard_map/ppermute | solution.py:358
  28.7 11.6 %collective-permute-start.7 = (bf16[296,128]{1,0:T(8,128)(2,1)S(1)}, bf16[296,128]{1,0:T(8,128)(2,1)S(1)}, u32[]{:S(2)}, u32[]{:S(2)}) collective-permute-start(bf16[296,128]{1,0:T(8,128)(2,1)S(1)} %turn.1), channel_id=1, source_target_pairs={{0,8},{4,12},{8,16},{12,20},{16,24},{20,28},{24,0},{28,4},{32,40},... | collective-permute-start | bytes 227336 | tf_op jit(solution)/shard_map/ppermute | solution.py:358
  30.1 10.2 %collective-permute-start.6 = (bf16[296,128]{1,0:T(8,128)(2,1)S(1)}, bf16[296,128]{1,0:T(8,128)(2,1)S(1)}, u32[]{:S(2)}, u32[]{:S(2)}) collective-permute-start(bf16[296,128]{1,0:T(8,128)(2,1)S(1)} %turn.1), channel_id=1, source_target_pairs={{0,16},{4,20},{8,24},{12,28},{16,0},{20,4},{24,8},{28,12},{32,48},... | collective-permute-start | bytes 227336 | tf_op jit(solution)/shard_map/ppermute | solution.py:358
  32.7 7.6 %collective-permute-start.5 = (bf16[296,128]{1,0:T(8,128)(2,1)S(1)}, bf16[296,128]{1,0:T(8,128)(2,1)S(1)}, u32[]{:S(2)}, u32[]{:S(2)}) collective-permute-start(bf16[296,128]{1,0:T(8,128)(2,1)S(1)} %turn.1), channel_id=1, source_target_pairs={{0,24},{4,28},{8,0},{12,4},{16,8},{20,12},{24,16},{28,20},{32,56},... | collective-permute-start | bytes 227336 | tf_op jit(solution)/shard_map/ppermute | solution.py:358
  40.4 22.8 %copy-start = (bf16[296,2368]{1,0:T(8,128)(2,1)S(1)}, bf16[296,2368]{1,0:T(8,128)(2,1)}, u32[]{:S(2)}) copy-start(bf16[296,2368]{1,0:T(8,128)(2,1)} %down_ref.1) | copy-start | bytes 4205572
  40.4 17.4 %collective-permute-start.10 = (bf16[296,512]{1,0:T(8,128)(2,1)S(1)}, bf16[296,512]{1,0:T(8,128)(2,1)S(1)}, u32[]{:S(2)}, u32[]{:S(2)}) collective-permute-start(bf16[296,512]{1,0:T(8,128)(2,1)S(1)} %pad_maximum_fusion.t0), channel_id=1, source_target_pairs={{0,1},{1,2},{2,3},{3,0},{4,5},{5,6},{6,7},{7,4},{8,9},{9,10},{10,1... | collective-permute-start | bytes 909320 | tf_op jit(solution)/shard_map/ppermute | solution.py:358
  41.5 16.3 %collective-permute-start.9 = (bf16[296,512]{1,0:T(8,128)(2,1)S(1)}, bf16[296,512]{1,0:T(8,128)(2,1)S(1)}, u32[]{:S(2)}, u32[]{:S(2)}) collective-permute-start(bf16[296,512]{1,0:T(8,128)(2,1)S(1)} %pad_maximum_fusion.t0), channel_id=1, source_target_pairs={{0,2},{1,3},{2,0},{3,1},{4,6},{5,7},{6,4},{7,5},{8,10},{9,11},{10,... | collective-permute-start | bytes 909320 | tf_op jit(solution)/shard_map/ppermute | solution.py:358
  44.6 13.2 %collective-permute-start.8 = (bf16[296,512]{1,0:T(8,128)(2,1)S(1)}, bf16[296,512]{1,0:T(8,128)(2,1)S(1)}, u32[]{:S(2)}, u32[]{:S(2)}) collective-permute-start(bf16[296,512]{1,0:T(8,128)(2,1)S(1)} %pad_maximum_fusion.t0), channel_id=1, source_target_pairs={{0,3},{1,0},{2,1},{3,2},{4,7},{5,4},{6,5},{7,6},{8,11},{9,8},{10,9... | collective-permute-start | bytes 909320 | tf_op jit(solution)/shard_map/ppermute | solution.py:358
  57.8 7.5 %collective-permute-start.12 = (bf16[296,512]{1,0:T(8,128)(2,1)S(1)}, bf16[296,512]{1,0:T(8,128)(2,1)S(1)}, u32[]{:S(2)}, u32[]{:S(2)}) collective-permute-start(bf16[296,512]{1,0:T(8,128)(2,1)S(1)} %pad_maximum_fusion.t0), channel_id=1, source_target_pairs={{0,4},{4,0},{8,12},{12,8},{16,20},{20,16},{24,28},{28,24},{32,36},... | collective-permute-start | bytes 909320 | tf_op jit(solution)/shard_map/ppermute | solution.py:358
  62.5 2.8 %collective-permute-start.13 = (bf16[296,512]{1,0:T(8,128)(2,1)S(1)}, bf16[296,512]{1,0:T(8,128)(2,1)S(1)}, u32[]{:S(2)}, u32[]{:S(2)}) collective-permute-start(bf16[296,512]{1,0:T(8,128)(2,1)S(1)} %collective-permute-done.8.t1), channel_id=1, source_target_pairs={{0,4},{4,0},{8,12},{12,8},{16,20},{20,16},{24,28},{28,24},{32,36},... | collective-permute-start | bytes 909320 | tf_op jit(solution)/shard_map/ppermute | solution.py:358
  62.6 2.7 %collective-permute-start.14 = (bf16[296,512]{1,0:T(8,128)(2,1)S(1)}, bf16[296,512]{1,0:T(8,128)(2,1)S(1)}, u32[]{:S(2)}, u32[]{:S(2)}) collective-permute-start(bf16[296,512]{1,0:T(8,128)(2,1)S(1)} %collective-permute-done.9.t2), channel_id=1, source_target_pairs={{0,4},{4,0},{8,12},{12,8},{16,20},{20,16},{24,28},{28,24},{32,36},... | collective-permute-start | bytes 909320 | tf_op jit(solution)/shard_map/ppermute | solution.py:358
  63.0 2.3 %collective-permute-start.15 = (bf16[296,512]{1,0:T(8,128)(2,1)S(1)}, bf16[296,512]{1,0:T(8,128)(2,1)S(1)}, u32[]{:S(2)}, u32[]{:S(2)}) collective-permute-start(bf16[296,512]{1,0:T(8,128)(2,1)S(1)} %collective-permute-done.10.t3), channel_id=1, source_target_pairs={{0,4},{4,0},{8,12},{12,8},{16,20},{20,16},{24,28},{28,24},{32,36},... | collective-permute-start | bytes 909320 | tf_op jit(solution)/shard_map/ppermute | solution.py:358
  63.7 1.7 %copy-start.4 = (s32[128,8]{0,1:T(8,128)S(1)}, s32[128,8]{0,1:T(8,128)}, u32[]{:S(2)}) copy-start(s32[128,8]{0,1:T(8,128)} %param.20) | copy-start | bytes 12292
  63.7 1.7 %copy-start.5 = (s32[128,8]{0,1:T(8,128)S(1)}, s32[128,8]{0,1:T(8,128)}, u32[]{:S(2)}) copy-start(s32[128,8]{0,1:T(8,128)} %param.21) | copy-start | bytes 12292
  63.7 1.7 %copy-start.6 = (s32[16,8]{0,1:T(8,128)S(1)}, s32[16,8]{0,1:T(8,128)}, u32[]{:S(2)}) copy-start(s32[16,8]{0,1:T(8,128)} %param.22) | copy-start | bytes 1540
  63.7 1.7 %copy-start.7 = (s32[16,8]{0,1:T(8,128)S(1)}, s32[16,8]{0,1:T(8,128)}, u32[]{:S(2)}) copy-start(s32[16,8]{0,1:T(8,128)} %param.23) | copy-start | bytes 1540
  63.8 1.7 %copy-start.8 = (s32[2,8]{1,0:T(2,128)S(1)}, s32[2,8]{1,0:T(2,128)}, u32[]{:S(2)}) copy-start(s32[2,8]{1,0:T(2,128)} %src4_ref.1) | copy-start | bytes 196
  63.8 1.7 %copy-start.9 = (s32[2,8]{1,0:T(2,128)S(1)}, s32[2,8]{1,0:T(2,128)}, u32[]{:S(2)}) copy-start(s32[2,8]{1,0:T(2,128)} %cls4_ref.1) | copy-start | bytes 196

commit v7 on v6

--- a/solution.py
+++ b/solution.py
@@ -232,7 +232,7 @@
     t0, t1, t2, t3, t4, t5, t6, t7, six_ref, halo_ref, src6_ref, cls6_ref, src5_ref, cls5_ref, src4_ref, cls4_ref,
     up_ref, down_ref,
     s0, s1, s2, maps_ref, out_ref,
-    even, odd, grouped, stack, coarse, both, weave, fars, local, src_ref, cls_ref,
+    even, odd, grouped, stack, coarse, octants, weave, fars, local, src_ref, cls_ref,
 ):
     window = jnp.concatenate([six_ref[...], halo_ref[...]], axis=1)
     rel = src6_ref[...] - (place() * 128 - 64)
@@ -287,7 +287,6 @@
         return carry
 
     lax.fori_loop(0, 8, fill, 0)
-    both[...] = jnp.zeros(both.shape, BF)
     lane = lax.broadcasted_iota(jnp.int32, (F, 128), 1)
     fars[0] = jnp.where(lane < 16, coarse[:, :128], 0.0)
     fars[1] = coarse[:, 128:]
@@ -295,16 +294,12 @@
     local[...] = dot(coarse[:, :128].astype(BF), jnp.where(take, 1.0, 0.0).astype(BF)).astype(BF)
 
     def woven(lanes):
-        pieces = dot(both[...], weave[:, lanes])
-        return pieces[:F, :] + pieces[304 : 304 + F, :]
+        return dot(octants[...], weave[:, lanes])
 
     def fall(level, carry):
         children = dot(down_ref[...], local[...])
         for o in range(8):
-            part = children[o * F : (o + 1) * F, :]
-            high = part.astype(BF)
-            both[:F, 128 * o : 128 * o + 128] = high
-            both[304 : 304 + F, 128 * o : 128 * o + 128] = (part - high.astype(F32)).astype(BF)
+            octants[:, 128 * o : 128 * o + 128] = children[o * F : (o + 1) * F, :].astype(BF)
 
         @pl.when(level < 2)
         def _():
@@ -330,7 +325,7 @@
             pltpu.VMEM((KINDS * F, 256), BF),
             pltpu.VMEM((8 * F, 128), F32),
             pltpu.VMEM((F, 256), F32),
-            pltpu.VMEM((608, 1024), BF),
+            pltpu.VMEM((F, 1024), BF),
             pltpu.VMEM((1024, 1024), BF),
             pltpu.VMEM((2, F, 128), F32),
             pltpu.VMEM((F, 128), BF),

time: 80.7 us -> 79.5 us (0.985)
  Pallas kernels: 46 us -> 44.7 us
    pallas_call x1, Pallas kernels: 15.1 us -> 13.8 us  [last(): pl.pallas_call(last_body, out_shape=jax.ShapeDtypeStruct((F, 1024), BF),...]
  transfers between devices with their start and end apart: 16 -> 16, of which waited for: 0 -> 0; matrix products, arithmetic and copies ran while one was open for 0% -> 0% of each run, Pallas kernels for 38% -> 39%
where the time goes in v7:
time: 79.5 us; the launch traced here: 79.3 us
  Pallas kernels  44.7 us (56%)
  starting transfers between devices  32.1 us (40%)
  other arithmetic  1.97 us (2%)
    pallas_call x3, Pallas kernels, near(): pl.pallas_call(functools.partial(near_body, block, count), out_shape=jax....  25.9 us
    ppermute x14, starting transfers between devices, turned(): return lax.ppermute(value, axis, pairs)  23.8 us
    pallas_call x1, Pallas kernels, last(): pl.pallas_call(last_body, out_shape=jax.ShapeDtypeStruct((F, 1024), BF),...  13.8 us
    ppermute x2, starting transfers between devices, shifted(): lax.ppermute(value, axis, [(source, source + steps) for source in range(f...  8.23 us
    pallas_call x1, Pallas kernels, rise(): pl.pallas_call(rise_body, out_shape=(jax.ShapeDtypeStruct((F, 128), BF),...  2.8 us
  transfers between devices with their start and end apart: 16, of which 0 were waited for; matrix products, arithmetic and copies ran while one was open for 0% of the time, Pallas kernels for 39%

profile of v7, /device:TPU:1, one launch (start us, length us, event | category | flops | bytes accessed | tf_op | source)
XLA Modules:
  0.0 79.3 jit_solution(16519742221406449361)
XLA Ops:
  0.0 0.8 %convert_element_type.3 = bf16[1024]{0:T(1024)(128)(2,1)S(1)} convert(s32[1024]{0:T(1024)} %param.14) | non-fusion elementwise | flops 1024 | bytes 6144 | tf_op jit(solution)/shard_map/convert_element_type | solution.py:383
  0.8 1.1 %multiply_bitcast_fusion = bf16[296,1024]{1,0:T(8,128)(2,1)S(1)} fusion(bf16[1024,296]{0,1:T(8,128)(2,1)} %param.13, bf16[1024]{0:T(1024)(128)(2,1)S(1)} %convert_element_type.3), kind=kLoop, calls=%fused_computation | loop fusion | flops 303104 | bytes 1214464 | tf_op jit(solution)/shard_map/mul | solution.py:383
  1.9 0.0 slice-start
  2.0 4.2 %collective-permute-start.4 = (bf16[296,512]{1,0:T(8,128)(2,1)S(1)}, bf16[296,512]{1,0:T(8,128)(2,1)S(1)}, u32[]{:S(2)}, u32[]{:S(2)}) collective-permute-start(bf16[296,512]{1,0:T(8,128)(2,1)S(1)} %get-tuple-element.51.hi_ref.c_ref.b_ref), channel_id=1, source_target_pairs={{0,1},{1,2},{2,3},{3,4},{4,5},{5,6},{6,7},{7,8},{8,9},{9,10},{10,1... | collective-permute-start | bytes 909320 | tf_op jit(solution)/shard_map/ppermute | solution.py:344
  6.2 0.0 slice-start.1
  6.2 0.0 copy-start.2
  6.2 0.0 copy-start.3
  6.2 2.8 %rise.1 = (bf16[296,128]{1,0:T(8,128)(2,1)S(1)}, bf16[16,296]{1,0:T(8,128)(2,1)S(1)}) custom-call(bf16[296,512]{1,0:T(8,128)(2,1)S(1)} %get-tuple-element.41.lo_ref.b_ref.a_ref, bf16[296,512]{1,0:T(8,128)(2,1)S(1)} %get-tuple-element.51.hi_ref.c_ref.b_ref, bf16[296,2368]{1,0:T(8,128)(2,1)S(1)} %bitcast.21), custom_call_target="tpu_custom_call" | custom-call | flops 8000000000 | bytes 3000000 | tf_op jit(solution)/shard_map/rise/pallas_call | solution.py:65
  9.1 5.6 %collective-permute-start.1 = (bf16[16,296]{1,0:T(8,128)(2,1)S(1)}, bf16[16,296]{1,0:T(8,128)(2,1)S(1)}, u32[]{:S(2)}, u32[]{:S(2)}) collective-permute-start(bf16[16,296]{1,0:T(8,128)(2,1)S(1)} %get-tuple-element.28), channel_id=1, source_target_pairs={{0,224},{4,228},{8,232},{12,236},{16,240},{20,244},{24,248},{28,25... | collective-permute-start | bytes 28424 | tf_op jit(solution)/shard_map/ppermute | solution.py:353
  14.7 0.0 collective-permute-start
  14.7 4.0 %collective-permute-start.11 = (bf16[296,512]{1,0:T(8,128)(2,1)S(1)}, bf16[296,512]{1,0:T(8,128)(2,1)S(1)}, u32[]{:S(2)}, u32[]{:S(2)}) collective-permute-start(bf16[296,512]{1,0:T(8,128)(2,1)S(1)} %get-tuple-element.41.lo_ref.b_ref.a_ref), channel_id=1, source_target_pairs={{1,0},{2,1},{3,2},{4,3},{5,4},{6,5},{7,6},{8,7},{9,8},{10,9},{11,1... | collective-permute-start | bytes 909320 | tf_op jit(solution)/shard_map/ppermute | solution.py:344
  18.7 0.0 collective-permute-done.1
  18.7 0.0 collective-permute-done
  18.7 2.7 %collective-permute-start.3 = (bf16[3,16,296]{2,1,0:T(8,128)(2,1)S(1)}, bf16[3,16,296]{2,1,0:T(8,128)(2,1)S(1)}, u32[]{:S(2)}, u32[]{:S(2)}) collective-permute-start(bf16[3,16,296]{2,1,0:T(8,128)(2,1)S(1)} %pad_maximum_fusion.1.middle_ref), channel_id=1, source_target_pairs={{0,160},{4,164},{8,168},{12,172},{16,176},{20,180},{24,184},{28,18... | collective-permute-start | bytes 85256 | tf_op jit(solution)/shard_map/ppermute | solution.py:353
  21.5 0.6 collective-permute-start.2
  22.1 0.0 collective-permute-done.4.a_ref.below_ref
  22.1 6.5 %near0.1.s0 = f32[1,296,256]{2,1,0:T(8,128)S(1)} custom-call(bf16[296,512]{1,0:T(8,128)(2,1)S(1)} %collective-permute-done.4.a_ref.below_ref, bf16[296,512]{1,0:T(8,128)(2,1)S(1)} %get-tuple-element.41.lo_ref.b_ref.a_ref, bf16[296,512]{1,0:T(8,128)(2,1)S(1)} %get-tuple-element.51.hi_ref.c_ref.b_ref, s32[8,1024]{1,0:T(8,128)S(1)} %bitcast.24, ...), custom_call_target="tpu_custom_call" | custom-call | flops 6000000000 | bytes 6000000 | tf_op jit(solution)/shard_map/near0/pallas_call | solution.py:153
  28.6 0.0 collective-permute-done.2.lower_ref
  28.6 0.0 collective-permute-done.3.upper_ref
  28.6 0.1 turn.1
  28.7 1.4 %collective-permute-start.7 = (bf16[296,128]{1,0:T(8,128)(2,1)S(1)}, bf16[296,128]{1,0:T(8,128)(2,1)S(1)}, u32[]{:S(2)}, u32[]{:S(2)}) collective-permute-start(bf16[296,128]{1,0:T(8,128)(2,1)S(1)} %turn.1), channel_id=1, source_target_pairs={{0,8},{4,12},{8,16},{12,20},{16,24},{20,28},{24,0},{28,4},{32,40},... | collective-permute-start | bytes 227336 | tf_op jit(solution)/shard_map/ppermute | solution.py:353
  30.1 2.6 %collective-permute-start.6 = (bf16[296,128]{1,0:T(8,128)(2,1)S(1)}, bf16[296,128]{1,0:T(8,128)(2,1)S(1)}, u32[]{:S(2)}, u32[]{:S(2)}) collective-permute-start(bf16[296,128]{1,0:T(8,128)(2,1)S(1)} %turn.1), channel_id=1, source_target_pairs={{0,16},{4,20},{8,24},{12,28},{16,0},{20,4},{24,8},{28,12},{32,48},... | collective-permute-start | bytes 227336 | tf_op jit(solution)/shard_map/ppermute | solution.py:353
  32.7 1.1 %collective-permute-start.5 = (bf16[296,128]{1,0:T(8,128)(2,1)S(1)}, bf16[296,128]{1,0:T(8,128)(2,1)S(1)}, u32[]{:S(2)}, u32[]{:S(2)}) collective-permute-start(bf16[296,128]{1,0:T(8,128)(2,1)S(1)} %turn.1), channel_id=1, source_target_pairs={{0,24},{4,28},{8,0},{12,4},{16,8},{20,12},{24,16},{28,20},{32,56},... | collective-permute-start | bytes 227336 | tf_op jit(solution)/shard_map/ppermute | solution.py:353
  33.8 6.5 %near1.1.s1 = f32[1,296,256]{2,1,0:T(8,128)S(1)} custom-call(bf16[296,512]{1,0:T(8,128)(2,1)S(1)} %collective-permute-done.4.a_ref.below_ref, bf16[296,512]{1,0:T(8,128)(2,1)S(1)} %get-tuple-element.41.lo_ref.b_ref.a_ref, bf16[296,512]{1,0:T(8,128)(2,1)S(1)} %get-tuple-element.51.hi_ref.c_ref.b_ref, s32[8,1024]{1,0:T(8,128)S(1)} %bitcast.25, ...), custom_call_target="tpu_custom_call" | custom-call | flops 6000000000 | bytes 6000000 | tf_op jit(solution)/shard_map/near1/pallas_call | solution.py:153
  40.3 0.0 collective-permute-done.5
  40.4 0.0 copy-start
  40.4 1.2 %collective-permute-start.10 = (bf16[296,512]{1,0:T(8,128)(2,1)S(1)}, bf16[296,512]{1,0:T(8,128)(2,1)S(1)}, u32[]{:S(2)}, u32[]{:S(2)}) collective-permute-start(bf16[296,512]{1,0:T(8,128)(2,1)S(1)} %pad_maximum_fusion.t0), channel_id=1, source_target_pairs={{0,1},{1,2},{2,3},{3,0},{4,5},{5,6},{6,7},{7,4},{8,9},{9,10},{10,1... | collective-permute-start | bytes 909320 | tf_op jit(solution)/shard_map/ppermute | solution.py:353
  41.5 3.1 %collective-permute-start.9 = (bf16[296,512]{1,0:T(8,128)(2,1)S(1)}, bf16[296,512]{1,0:T(8,128)(2,1)S(1)}, u32[]{:S(2)}, u32[]{:S(2)}) collective-permute-start(bf16[296,512]{1,0:T(8,128)(2,1)S(1)} %pad_maximum_fusion.t0), channel_id=1, source_target_pairs={{0,2},{1,3},{2,0},{3,1},{4,6},{5,7},{6,4},{7,5},{8,10},{9,11},{10,... | collective-permute-start | bytes 909320 | tf_op jit(solution)/shard_map/ppermute | solution.py:353
  44.6 0.3 collective-permute-start.8
  44.8 0.0 collective-permute-done.11.c_ref.above_ref
  44.8 12.9 %near2.1.s2 = f32[2,296,256]{2,1,0:T(8,128)S(1)} custom-call(bf16[296,512]{1,0:T(8,128)(2,1)S(1)} %get-tuple-element.41.lo_ref.b_ref.a_ref, bf16[296,512]{1,0:T(8,128)(2,1)S(1)} %get-tuple-element.51.hi_ref.c_ref.b_ref, bf16[296,512]{1,0:T(8,128)(2,1)S(1)} %collective-permute-done.11.c_ref.above_ref, s32[8,1024]{1,0:T(8,128)S(1)} %bitcast.26, ...), custom_call_target="tpu_custom_call" | custom-call | flops 12000000000 | bytes 6000000 | tf_op jit(solution)/shard_map/near2/pallas_call | solution.py:153
  57.8 0.0 collective-permute-done.9.t2
  57.8 0.0 collective-permute-done.8.t1
  57.8 4.7 %collective-permute-start.12 = (bf16[296,512]{1,0:T(8,128)(2,1)S(1)}, bf16[296,512]{1,0:T(8,128)(2,1)S(1)}, u32[]{:S(2)}, u32[]{:S(2)}) collective-permute-start(bf16[296,512]{1,0:T(8,128)(2,1)S(1)} %pad_maximum_fusion.t0), channel_id=1, source_target_pairs={{0,4},{4,0},{8,12},{12,8},{16,20},{20,16},{24,28},{28,24},{32,36},... | collective-permute-start | bytes 909320 | tf_op jit(solution)/shard_map/ppermute | solution.py:353
  62.5 0.1 collective-permute-start.13
  62.6 0.4 collective-permute-start.14
  63.0 0.1 collective-permute-start.15
  63.2 0.5 flip.1.down_ref
  63.7 0.0 copy-start.4
  63.7 0.0 copy-start.5
  63.7 0.0 copy-start.6
  63.7 0.0 copy-start.7
  63.8 0.0 copy-start.8
  63.8 0.0 copy-start.9
  63.8 1.6 %halo.1.halo_ref = bf16[296,128]{1,0:T(8,128)(2,1)S(1)} custom-call(bf16[296,512]{1,0:T(8,128)(2,1)S(1)} %collective-permute-done.4.a_ref.below_ref, bf16[296,512]{1,0:T(8,128)(2,1)S(1)} %collective-permute-done.11.c_ref.above_ref, bf16[296,2368]{1,0:T(8,128)(2,1)S(1)} %bitcast.22), custom_call_target="tpu_custom_call" | custom-call | flops 2000000000 | bytes 3000000 | tf_op jit(solution)/shard_map/halo/pallas_call | solution.py:193
  65.4 0.0 collective-permute-done.13.t5
  65.4 0.0 collective-permute-done.14.t6
  65.5 13.8 %last.1 = bf16[296,1024]{1,0:T(8,128)(2,1)} custom-call(bf16[296,512]{1,0:T(8,128)(2,1)S(1)} %pad_maximum_fusion.t0, bf16[296,512]{1,0:T(8,128)(2,1)S(1)} %collective-permute-done.8.t1, bf16[296,512]{1,0:T(8,128)(2,1)S(1)} %collective-permute-done.9.t2, bf16[296,512]{1,0:T(8,128)(2,1)S(1)} %collective-permute-done.10.t3, ...), custom_call_target="tpu_custom_call" | custom-call | flops 8000000000 | bytes 12000000 | tf_op jit(solution)/shard_map/last/pallas_call | solution.py:317
  (23 shorter events, 0.1 us)
Async XLA Ops:
  0.0 6.2 %copy-start.1 = (bf16[2368,296]{0,1:T(8,128)(2,1)S(1)}, bf16[2368,296]{0,1:T(8,128)(2,1)}, u32[]{:S(2)}) copy-start(bf16[2368,296]{0,1:T(8,128)(2,1)} %param.15) | copy-start | bytes 4205572
  1.9 20.2 %slice-start = ((s8[5607424]{0:T(1024)(128)(4,1)}), s8[4194304]{0:T(1024)(128)(4,1)S(1)}, s32[]{:S(2)}) async-start(s8[5607424]{0:T(1024)(128)(4,1)} %bitcast.15), calls=%async_computation | async-start | bytes 8388608
  2.0 20.1 %collective-permute-start.4 = (bf16[296,512]{1,0:T(8,128)(2,1)S(1)}, bf16[296,512]{1,0:T(8,128)(2,1)S(1)}, u32[]{:S(2)}, u32[]{:S(2)}) collective-permute-start(bf16[296,512]{1,0:T(8,128)(2,1)S(1)} %get-tuple-element.51.hi_ref.c_ref.b_ref), channel_id=1, source_target_pairs={{0,1},{1,2},{2,3},{3,4},{4,5},{5,6},{6,7},{7,8},{8,9},{9,10},{10,1... | collective-permute-start | bytes 909320 | tf_op jit(solution)/shard_map/ppermute | solution.py:344
  6.2 15.9 %slice-start.1 = ((s8[5607424]{0:T(1024)(128)(4,1)}), s8[1413120]{0:T(1024)(128)(4,1)S(1)}, s32[]{:S(2)}) async-start(s8[5607424]{0:T(1024)(128)(4,1)} %bitcast.15), calls=%async_computation.1 | async-start | bytes 2826240
  6.2 15.9 %copy-start.2 = (s32[1024,8]{0,1:T(8,128)S(1)}, s32[1024,8]{0,1:T(8,128)}, u32[]{:S(2)}) copy-start(s32[1024,8]{0,1:T(8,128)} %param.18) | copy-start | bytes 98308
  6.2 15.9 %copy-start.3 = (s32[1024,8]{0,1:T(8,128)S(1)}, s32[1024,8]{0,1:T(8,128)}, u32[]{:S(2)}) copy-start(s32[1024,8]{0,1:T(8,128)} %param.19) | copy-start | bytes 98308
  9.1 9.6 %collective-permute-start.1 = (bf16[16,296]{1,0:T(8,128)(2,1)S(1)}, bf16[16,296]{1,0:T(8,128)(2,1)S(1)}, u32[]{:S(2)}, u32[]{:S(2)}) collective-permute-start(bf16[16,296]{1,0:T(8,128)(2,1)S(1)} %get-tuple-element.28), channel_id=1, source_target_pairs={{0,224},{4,228},{8,232},{12,236},{16,240},{20,244},{24,248},{28,25... | collective-permute-start | bytes 28424 | tf_op jit(solution)/shard_map/ppermute | solution.py:353
  14.7 4.0 %collective-permute-start = (bf16[16,296]{1,0:T(8,128)(2,1)S(1)}, bf16[16,296]{1,0:T(8,128)(2,1)S(1)}, u32[]{:S(2)}, u32[]{:S(2)}) collective-permute-start(bf16[16,296]{1,0:T(8,128)(2,1)S(1)} %get-tuple-element.28), channel_id=1, source_target_pairs={{0,32},{4,36},{8,40},{12,44},{16,48},{20,52},{24,56},{28,60},{32,6... | collective-permute-start | bytes 28424 | tf_op jit(solution)/shard_map/ppermute | solution.py:353
  14.7 30.2 %collective-permute-start.11 = (bf16[296,512]{1,0:T(8,128)(2,1)S(1)}, bf16[296,512]{1,0:T(8,128)(2,1)S(1)}, u32[]{:S(2)}, u32[]{:S(2)}) collective-permute-start(bf16[296,512]{1,0:T(8,128)(2,1)S(1)} %get-tuple-element.41.lo_ref.b_ref.a_ref), channel_id=1, source_target_pairs={{1,0},{2,1},{3,2},{4,3},{5,4},{6,5},{7,6},{8,7},{9,8},{10,9},{11,1... | collective-permute-start | bytes 909320 | tf_op jit(solution)/shard_map/ppermute | solution.py:344
  18.7 9.9 %collective-permute-start.3 = (bf16[3,16,296]{2,1,0:T(8,128)(2,1)S(1)}, bf16[3,16,296]{2,1,0:T(8,128)(2,1)S(1)}, u32[]{:S(2)}, u32[]{:S(2)}) collective-permute-start(bf16[3,16,296]{2,1,0:T(8,128)(2,1)S(1)} %pad_maximum_fusion.1.middle_ref), channel_id=1, source_target_pairs={{0,160},{4,164},{8,168},{12,172},{16,176},{20,180},{24,184},{28,18... | collective-permute-start | bytes 85256 | tf_op jit(solution)/shard_map/ppermute | solution.py:353
  21.5 7.1 %collective-permute-start.2 = (bf16[2,16,296]{2,1,0:T(8,128)(2,1)S(1)}, bf16[2,16,296]{2,1,0:T(8,128)(2,1)S(1)}, u32[]{:S(2)}, u32[]{:S(2)}) collective-permute-start(bf16[2,16,296]{2,1,0:T(8,128)(2,1)S(1)} %slice.11), channel_id=1, source_target_pairs={{0,96},{4,100},{8,104},{12,108},{16,112},{20,116},{24,120},{28,124... | collective-permute-start | bytes 56840 | tf_op jit(solution)/shard_map/ppermute | solution.py:353
  28.7 11.6 %collective-permute-start.7 = (bf16[296,128]{1,0:T(8,128)(2,1)S(1)}, bf16[296,128]{1,0:T(8,128)(2,1)S(1)}, u32[]{:S(2)}, u32[]{:S(2)}) collective-permute-start(bf16[296,128]{1,0:T(8,128)(2,1)S(1)} %turn.1), channel_id=1, source_target_pairs={{0,8},{4,12},{8,16},{12,20},{16,24},{20,28},{24,0},{28,4},{32,40},... | collective-permute-start | bytes 227336 | tf_op jit(solution)/shard_map/ppermute | solution.py:353
  30.1 10.2 %collective-permute-start.6 = (bf16[296,128]{1,0:T(8,128)(2,1)S(1)}, bf16[296,128]{1,0:T(8,128)(2,1)S(1)}, u32[]{:S(2)}, u32[]{:S(2)}) collective-permute-start(bf16[296,128]{1,0:T(8,128)(2,1)S(1)} %turn.1), channel_id=1, source_target_pairs={{0,16},{4,20},{8,24},{12,28},{16,0},{20,4},{24,8},{28,12},{32,48},... | collective-permute-start | bytes 227336 | tf_op jit(solution)/shard_map/ppermute | solution.py:353
  32.7 7.6 %collective-permute-start.5 = (bf16[296,128]{1,0:T(8,128)(2,1)S(1)}, bf16[296,128]{1,0:T(8,128)(2,1)S(1)}, u32[]{:S(2)}, u32[]{:S(2)}) collective-permute-start(bf16[296,128]{1,0:T(8,128)(2,1)S(1)} %turn.1), channel_id=1, source_target_pairs={{0,24},{4,28},{8,0},{12,4},{16,8},{20,12},{24,16},{28,20},{32,56},... | collective-permute-start | bytes 227336 | tf_op jit(solution)/shard_map/ppermute | solution.py:353
  40.4 22.8 %copy-start = (bf16[296,2368]{1,0:T(8,128)(2,1)S(1)}, bf16[296,2368]{1,0:T(8,128)(2,1)}, u32[]{:S(2)}) copy-start(bf16[296,2368]{1,0:T(8,128)(2,1)} %down_ref.1) | copy-start | bytes 4205572
  40.4 17.4 %collective-permute-start.10 = (bf16[296,512]{1,0:T(8,128)(2,1)S(1)}, bf16[296,512]{1,0:T(8,128)(2,1)S(1)}, u32[]{:S(2)}, u32[]{:S(2)}) collective-permute-start(bf16[296,512]{1,0:T(8,128)(2,1)S(1)} %pad_maximum_fusion.t0), channel_id=1, source_target_pairs={{0,1},{1,2},{2,3},{3,0},{4,5},{5,6},{6,7},{7,4},{8,9},{9,10},{10,1... | collective-permute-start | bytes 909320 | tf_op jit(solution)/shard_map/ppermute | solution.py:353
  41.5 16.3 %collective-permute-start.9 = (bf16[296,512]{1,0:T(8,128)(2,1)S(1)}, bf16[296,512]{1,0:T(8,128)(2,1)S(1)}, u32[]{:S(2)}, u32[]{:S(2)}) collective-permute-start(bf16[296,512]{1,0:T(8,128)(2,1)S(1)} %pad_maximum_fusion.t0), channel_id=1, source_target_pairs={{0,2},{1,3},{2,0},{3,1},{4,6},{5,7},{6,4},{7,5},{8,10},{9,11},{10,... | collective-permute-start | bytes 909320 | tf_op jit(solution)/shard_map/ppermute | solution.py:353
  44.6 13.2 %collective-permute-start.8 = (bf16[296,512]{1,0:T(8,128)(2,1)S(1)}, bf16[296,512]{1,0:T(8,128)(2,1)S(1)}, u32[]{:S(2)}, u32[]{:S(2)}) collective-permute-start(bf16[296,512]{1,0:T(8,128)(2,1)S(1)} %pad_maximum_fusion.t0), channel_id=1, source_target_pairs={{0,3},{1,0},{2,1},{3,2},{4,7},{5,4},{6,5},{7,6},{8,11},{9,8},{10,9... | collective-permute-start | bytes 909320 | tf_op jit(solution)/shard_map/ppermute | solution.py:353
  57.8 7.5 %collective-permute-start.12 = (bf16[296,512]{1,0:T(8,128)(2,1)S(1)}, bf16[296,512]{1,0:T(8,128)(2,1)S(1)}, u32[]{:S(2)}, u32[]{:S(2)}) collective-permute-start(bf16[296,512]{1,0:T(8,128)(2,1)S(1)} %pad_maximum_fusion.t0), channel_id=1, source_target_pairs={{0,4},{4,0},{8,12},{12,8},{16,20},{20,16},{24,28},{28,24},{32,36},... | collective-permute-start | bytes 909320 | tf_op jit(solution)/shard_map/ppermute | solution.py:353
  62.5 2.8 %collective-permute-start.13 = (bf16[296,512]{1,0:T(8,128)(2,1)S(1)}, bf16[296,512]{1,0:T(8,128)(2,1)S(1)}, u32[]{:S(2)}, u32[]{:S(2)}) collective-permute-start(bf16[296,512]{1,0:T(8,128)(2,1)S(1)} %collective-permute-done.8.t1), channel_id=1, source_target_pairs={{0,4},{4,0},{8,12},{12,8},{16,20},{20,16},{24,28},{28,24},{32,36},... | collective-permute-start | bytes 909320 | tf_op jit(solution)/shard_map/ppermute | solution.py:353
  62.6 2.7 %collective-permute-start.14 = (bf16[296,512]{1,0:T(8,128)(2,1)S(1)}, bf16[296,512]{1,0:T(8,128)(2,1)S(1)}, u32[]{:S(2)}, u32[]{:S(2)}) collective-permute-start(bf16[296,512]{1,0:T(8,128)(2,1)S(1)} %collective-permute-done.9.t2), channel_id=1, source_target_pairs={{0,4},{4,0},{8,12},{12,8},{16,20},{20,16},{24,28},{28,24},{32,36},... | collective-permute-start | bytes 909320 | tf_op jit(solution)/shard_map/ppermute | solution.py:353
  63.0 2.3 %collective-permute-start.15 = (bf16[296,512]{1,0:T(8,128)(2,1)S(1)}, bf16[296,512]{1,0:T(8,128)(2,1)S(1)}, u32[]{:S(2)}, u32[]{:S(2)}) collective-permute-start(bf16[296,512]{1,0:T(8,128)(2,1)S(1)} %collective-permute-done.10.t3), channel_id=1, source_target_pairs={{0,4},{4,0},{8,12},{12,8},{16,20},{20,16},{24,28},{28,24},{32,36},... | collective-permute-start | bytes 909320 | tf_op jit(solution)/shard_map/ppermute | solution.py:353
  63.7 1.7 %copy-start.4 = (s32[128,8]{0,1:T(8,128)S(1)}, s32[128,8]{0,1:T(8,128)}, u32[]{:S(2)}) copy-start(s32[128,8]{0,1:T(8,128)} %param.20) | copy-start | bytes 12292
  63.7 1.7 %copy-start.5 = (s32[128,8]{0,1:T(8,128)S(1)}, s32[128,8]{0,1:T(8,128)}, u32[]{:S(2)}) copy-start(s32[128,8]{0,1:T(8,128)} %param.21) | copy-start | bytes 12292
  63.7 1.7 %copy-start.6 = (s32[16,8]{0,1:T(8,128)S(1)}, s32[16,8]{0,1:T(8,128)}, u32[]{:S(2)}) copy-start(s32[16,8]{0,1:T(8,128)} %param.22) | copy-start | bytes 1540
  63.7 1.7 %copy-start.7 = (s32[16,8]{0,1:T(8,128)S(1)}, s32[16,8]{0,1:T(8,128)}, u32[]{:S(2)}) copy-start(s32[16,8]{0,1:T(8,128)} %param.23) | copy-start | bytes 1540
  63.8 1.7 %copy-start.8 = (s32[2,8]{1,0:T(2,128)S(1)}, s32[2,8]{1,0:T(2,128)}, u32[]{:S(2)}) copy-start(s32[2,8]{1,0:T(2,128)} %src4_ref.1) | copy-start | bytes 196
  63.8 1.7 %copy-start.9 = (s32[2,8]{1,0:T(2,128)S(1)}, s32[2,8]{1,0:T(2,128)}, u32[]{:S(2)}) copy-start(s32[2,8]{1,0:T(2,128)} %cls4_ref.1) | copy-start | bytes 196

commit v8 on v7

--- a/solution.py
+++ b/solution.py
@@ -167,21 +167,21 @@
     )(a, b, c, src, cls, maps)
 
 
-def turn_body(lower_ref, middle_ref, upper_ref, out_ref):
-    parts = [ref[k].astype(F32) for ref in (lower_ref, middle_ref, upper_ref) for k in range(ref.shape[0])]
+def turn_body(even_ref, odd_ref, out_ref):
+    parts = [ref[k].astype(F32) for ref in (even_ref, odd_ref) for k in range(4)]
     out_ref[...] = jnp.concatenate(parts, axis=0).T.astype(BF)
 
 
-def turn(lower, three, upper):
+def turn(fours, between):
     return pl.pallas_call(
         turn_body,
         out_shape=jax.ShapeDtypeStruct((F, 128), BF),
-        in_specs=[VM] * 3,
+        in_specs=[VM] * 2,
         out_specs=VM,
         compiler_params=pltpu.CompilerParams(vmem_limit_bytes=8 * 2**20),
         cost_estimate=pl.CostEstimate(flops=10**8, bytes_accessed=10**5, transcendentals=0),
         name="turn",
-    )(lower, three, upper)
+    )(fours, between)
 
 
 def halo_body(below_ref, above_ref, up_ref, out_ref, stack):
@@ -221,11 +221,11 @@
 def where_held(cell):
     cells, sub = lax.axis_index("cells"), lax.axis_index("sub")
     there = cell >> 6
-    dz = ((there >> 3) - (cells >> 3) + 3) & 7
+    dz = ((there >> 3) - (cells >> 3)) & 7
     dy = ((there >> 1) - (cells >> 1)) & 3
     dc = (there - cells) & 1
     dx = ((cell >> 4) - sub) & 3
-    return (dc * 4 + dx) * 512 + dy * 128 + dz * 16 + (cell & 15)
+    return (dc * 4 + dx) * 512 + dy * 128 + ((dz >> 1) + 4 * (dz & 1)) * 16 + (cell & 15)
 
 
 def last_body(
@@ -389,14 +389,12 @@
     src_seven, cls_seven = sources_seven.T, classes_seven.T
 
     down = flip(downward_maps)
-    minus, plus = along_z(five, 1), along_z(five, -1)
-    three = jnp.stack([minus, five, plus])
-    three, near_lo = tie(three, lo)
-    upper = along_z(three, -3)
-    lower = along_z(three[1:], 3)
+    fours = jnp.stack([five, along_z(five, -2), along_z(five, 4), along_z(five, 2)])
+    fours, near_lo = tie(fours, lo)
+    between = along_z(fours, -1)
     seven_0 = near(0, 1, below, near_lo, hi, src_seven, cls_seven, maps)
-    lower, upper, seven_0 = tie(lower, upper, seven_0)
-    column = turn(lower, three, upper)
+    between, seven_0 = tie(between, seven_0)
+    column = turn(fours, between)
     column, seven_0, near_lo = tie(column, seven_0, near_lo)
     sides = along_y(column, -1), along_y(column, 2), along_y(column, 1)
     seven_1 = near(1, 1, below, near_lo, hi, src_seven, cls_seven, maps)

time: 79.5 us -> 81.6 us (1.026)
  starting transfers between devices: 32.1 us -> 34.1 us
    ppermute x14, starting transfers between devices: 23.8 us -> 25.3 us  [turned(): return lax.ppermute(value, axis, pairs)]
  transfers between devices with their start and end apart: 16 -> 16, of which waited for: 0 -> 0; matrix products, arithmetic and copies ran while one was open for 0% -> 0% of each run, Pallas kernels for 39% -> 38%
where the time goes in v8:
time: 81.6 us; the launch traced here: 81.4 us
  Pallas kernels  44.8 us (55%)
  starting transfers between devices  34.1 us (42%)
  other arithmetic  1.97 us (2%)
    pallas_call x3, Pallas kernels, near(): pl.pallas_call(functools.partial(near_body, block, count), out_shape=jax....  25.9 us
    ppermute x14, starting transfers between devices, turned(): return lax.ppermute(value, axis, pairs)  25.3 us
    pallas_call x1, Pallas kernels, last(): pl.pallas_call(last_body, out_shape=jax.ShapeDtypeStruct((F, 1024), BF),...  13.9 us
    ppermute x2, starting transfers between devices, shifted(): lax.ppermute(value, axis, [(source, source + steps) for source in range(f...  8.79 us
    pallas_call x1, Pallas kernels, rise(): pl.pallas_call(rise_body, out_shape=(jax.ShapeDtypeStruct((F, 128), BF),...  2.8 us
  transfers between devices with their start and end apart: 16, of which 0 were waited for; matrix products, arithmetic and copies ran while one was open for 0% of the time, Pallas kernels for 38%

profile of v8, /device:TPU:1, one launch (start us, length us, event | category | flops | bytes accessed | tf_op | source)
XLA Modules:
  0.0 81.4 jit_solution(14655094972938504472)
XLA Ops:
  0.0 0.8 convert_element_type.3
  0.8 1.1 %multiply_bitcast_fusion = bf16[296,1024]{1,0:T(8,128)(2,1)S(1)} fusion(bf16[1024,296]{0,1:T(8,128)(2,1)} %param.13, bf16[1024]{0:T(1024)(128)(2,1)S(1)} %convert_element_type.3), kind=kLoop, calls=%fused_computation | loop fusion | flops 303104 | bytes 1214464 | tf_op jit(solution)/shard_map/mul | solution.py:383
  1.9 0.0 slice-start
  2.0 4.2 %collective-permute-start.4 = (bf16[296,512]{1,0:T(8,128)(2,1)S(1)}, bf16[296,512]{1,0:T(8,128)(2,1)S(1)}, u32[]{:S(2)}, u32[]{:S(2)}) collective-permute-start(bf16[296,512]{1,0:T(8,128)(2,1)S(1)} %get-tuple-element.49.hi_ref.c_ref.b_ref), channel_id=1, source_target_pairs={{0,1},{1,2},{2,3},{3,4},{4,5},{5,6},{6,7},{7,8},{8,9},{9,10},{10,1... | collective-permute-start | bytes 909320 | tf_op jit(solution)/shard_map/ppermute | solution.py:344
  6.2 0.0 slice-start.1
  6.2 0.0 copy-start.2
  6.2 0.0 copy-start.3
  6.2 2.8 %rise.1 = (bf16[296,128]{1,0:T(8,128)(2,1)S(1)}, bf16[16,296]{1,0:T(8,128)(2,1)S(1)}) custom-call(bf16[296,512]{1,0:T(8,128)(2,1)S(1)} %get-tuple-element.39.lo_ref.b_ref.a_ref, bf16[296,512]{1,0:T(8,128)(2,1)S(1)} %get-tuple-element.49.hi_ref.c_ref.b_ref, bf16[296,2368]{1,0:T(8,128)(2,1)S(1)} %bitcast.22), custom_call_target="tpu_custom_call" | custom-call | flops 8000000000 | bytes 3000000 | tf_op jit(solution)/shard_map/rise/pallas_call | solution.py:65
  9.1 3.0 %collective-permute-start.2 = (bf16[16,296]{1,0:T(8,128)(2,1)S(1)}, bf16[16,296]{1,0:T(8,128)(2,1)S(1)}, u32[]{:S(2)}, u32[]{:S(2)}) collective-permute-start(bf16[16,296]{1,0:T(8,128)(2,1)S(1)} %get-tuple-element.27), channel_id=1, source_target_pairs={{0,64},{4,68},{8,72},{12,76},{16,80},{20,84},{24,88},{28,92},{32,9... | collective-permute-start | bytes 28424 | tf_op jit(solution)/shard_map/ppermute | solution.py:353
  12.1 5.1 %collective-permute-start.1 = (bf16[16,296]{1,0:T(8,128)(2,1)S(1)}, bf16[16,296]{1,0:T(8,128)(2,1)S(1)}, u32[]{:S(2)}, u32[]{:S(2)}) collective-permute-start(bf16[16,296]{1,0:T(8,128)(2,1)S(1)} %get-tuple-element.27), channel_id=1, source_target_pairs={{0,128},{4,132},{8,136},{12,140},{16,144},{20,148},{24,152},{28,15... | collective-permute-start | bytes 28424 | tf_op jit(solution)/shard_map/ppermute | solution.py:353
  17.2 2.4 %collective-permute-start = (bf16[16,296]{1,0:T(8,128)(2,1)S(1)}, bf16[16,296]{1,0:T(8,128)(2,1)S(1)}, u32[]{:S(2)}, u32[]{:S(2)}) collective-permute-start(bf16[16,296]{1,0:T(8,128)(2,1)S(1)} %get-tuple-element.27), channel_id=1, source_target_pairs={{0,192},{4,196},{8,200},{12,204},{16,208},{20,212},{24,216},{28,22... | collective-permute-start | bytes 28424 | tf_op jit(solution)/shard_map/ppermute | solution.py:353
  19.6 4.6 %collective-permute-start.11 = (bf16[296,512]{1,0:T(8,128)(2,1)S(1)}, bf16[296,512]{1,0:T(8,128)(2,1)S(1)}, u32[]{:S(2)}, u32[]{:S(2)}) collective-permute-start(bf16[296,512]{1,0:T(8,128)(2,1)S(1)} %get-tuple-element.39.lo_ref.b_ref.a_ref), channel_id=1, source_target_pairs={{1,0},{2,1},{3,2},{4,3},{5,4},{6,5},{7,6},{8,7},{9,8},{10,9},{11,1... | collective-permute-start | bytes 909320 | tf_op jit(solution)/shard_map/ppermute | solution.py:344
  24.2 0.0 collective-permute-done.2
  24.2 0.0 collective-permute-done
  24.2 0.1 collective-permute-start.3
  24.3 0.0 collective-permute-done.4.a_ref.below_ref
  24.4 6.5 %near0.1.s0 = f32[1,296,256]{2,1,0:T(8,128)S(1)} custom-call(bf16[296,512]{1,0:T(8,128)(2,1)S(1)} %collective-permute-done.4.a_ref.below_ref, bf16[296,512]{1,0:T(8,128)(2,1)S(1)} %get-tuple-element.39.lo_ref.b_ref.a_ref, bf16[296,512]{1,0:T(8,128)(2,1)S(1)} %get-tuple-element.49.hi_ref.c_ref.b_ref, s32[8,1024]{1,0:T(8,128)S(1)} %bitcast.25, ...), custom_call_target="tpu_custom_call" | custom-call | flops 6000000000 | bytes 6000000 | tf_op jit(solution)/shard_map/near0/pallas_call | solution.py:153
  30.8 0.1 turn.1
  30.9 1.4 %collective-permute-start.7 = (bf16[296,128]{1,0:T(8,128)(2,1)S(1)}, bf16[296,128]{1,0:T(8,128)(2,1)S(1)}, u32[]{:S(2)}, u32[]{:S(2)}) collective-permute-start(bf16[296,128]{1,0:T(8,128)(2,1)S(1)} %turn.1), channel_id=1, source_target_pairs={{0,8},{4,12},{8,16},{12,20},{16,24},{20,28},{24,0},{28,4},{32,40},... | collective-permute-start | bytes 227336 | tf_op jit(solution)/shard_map/ppermute | solution.py:353
  32.3 2.6 %collective-permute-start.6 = (bf16[296,128]{1,0:T(8,128)(2,1)S(1)}, bf16[296,128]{1,0:T(8,128)(2,1)S(1)}, u32[]{:S(2)}, u32[]{:S(2)}) collective-permute-start(bf16[296,128]{1,0:T(8,128)(2,1)S(1)} %turn.1), channel_id=1, source_target_pairs={{0,16},{4,20},{8,24},{12,28},{16,0},{20,4},{24,8},{28,12},{32,48},... | collective-permute-start | bytes 227336 | tf_op jit(solution)/shard_map/ppermute | solution.py:353
  34.9 1.1 %collective-permute-start.5 = (bf16[296,128]{1,0:T(8,128)(2,1)S(1)}, bf16[296,128]{1,0:T(8,128)(2,1)S(1)}, u32[]{:S(2)}, u32[]{:S(2)}) collective-permute-start(bf16[296,128]{1,0:T(8,128)(2,1)S(1)} %turn.1), channel_id=1, source_target_pairs={{0,24},{4,28},{8,0},{12,4},{16,8},{20,12},{24,16},{28,20},{32,56},... | collective-permute-start | bytes 227336 | tf_op jit(solution)/shard_map/ppermute | solution.py:353
  36.0 6.5 %near1.1.s1 = f32[1,296,256]{2,1,0:T(8,128)S(1)} custom-call(bf16[296,512]{1,0:T(8,128)(2,1)S(1)} %collective-permute-done.4.a_ref.below_ref, bf16[296,512]{1,0:T(8,128)(2,1)S(1)} %get-tuple-element.39.lo_ref.b_ref.a_ref, bf16[296,512]{1,0:T(8,128)(2,1)S(1)} %get-tuple-element.49.hi_ref.c_ref.b_ref, s32[8,1024]{1,0:T(8,128)S(1)} %bitcast.26, ...), custom_call_target="tpu_custom_call" | custom-call | flops 6000000000 | bytes 6000000 | tf_op jit(solution)/shard_map/near1/pallas_call | solution.py:153
  42.5 0.0 collective-permute-done.7
  42.5 0.0 collective-permute-done.5
  42.6 0.0 copy-start
  42.6 1.0 %collective-permute-start.10 = (bf16[296,512]{1,0:T(8,128)(2,1)S(1)}, bf16[296,512]{1,0:T(8,128)(2,1)S(1)}, u32[]{:S(2)}, u32[]{:S(2)}) collective-permute-start(bf16[296,512]{1,0:T(8,128)(2,1)S(1)} %pad_maximum_fusion.t0), channel_id=1, source_target_pairs={{0,1},{1,2},{2,3},{3,0},{4,5},{5,6},{6,7},{7,4},{8,9},{9,10},{10,1... | collective-permute-start | bytes 909320 | tf_op jit(solution)/shard_map/ppermute | solution.py:353
  43.6 2.7 %collective-permute-start.9 = (bf16[296,512]{1,0:T(8,128)(2,1)S(1)}, bf16[296,512]{1,0:T(8,128)(2,1)S(1)}, u32[]{:S(2)}, u32[]{:S(2)}) collective-permute-start(bf16[296,512]{1,0:T(8,128)(2,1)S(1)} %pad_maximum_fusion.t0), channel_id=1, source_target_pairs={{0,2},{1,3},{2,0},{3,1},{4,6},{5,7},{6,4},{7,5},{8,10},{9,11},{10,... | collective-permute-start | bytes 909320 | tf_op jit(solution)/shard_map/ppermute | solution.py:353
  46.3 0.6 collective-permute-start.8
  46.9 0.0 collective-permute-done.11.c_ref.above_ref
  46.9 12.9 %near2.1.s2 = f32[2,296,256]{2,1,0:T(8,128)S(1)} custom-call(bf16[296,512]{1,0:T(8,128)(2,1)S(1)} %get-tuple-element.39.lo_ref.b_ref.a_ref, bf16[296,512]{1,0:T(8,128)(2,1)S(1)} %get-tuple-element.49.hi_ref.c_ref.b_ref, bf16[296,512]{1,0:T(8,128)(2,1)S(1)} %collective-permute-done.11.c_ref.above_ref, s32[8,1024]{1,0:T(8,128)S(1)} %bitcast.27, ...), custom_call_target="tpu_custom_call" | custom-call | flops 12000000000 | bytes 6000000 | tf_op jit(solution)/shard_map/near2/pallas_call | solution.py:153
  59.9 0.0 collective-permute-done.10.t3
  59.9 0.0 collective-permute-done.9.t2
  59.9 4.7 %collective-permute-start.12 = (bf16[296,512]{1,0:T(8,128)(2,1)S(1)}, bf16[296,512]{1,0:T(8,128)(2,1)S(1)}, u32[]{:S(2)}, u32[]{:S(2)}) collective-permute-start(bf16[296,512]{1,0:T(8,128)(2,1)S(1)} %pad_maximum_fusion.t0), channel_id=1, source_target_pairs={{0,4},{4,0},{8,12},{12,8},{16,20},{20,16},{24,28},{28,24},{32,36},... | collective-permute-start | bytes 909320 | tf_op jit(solution)/shard_map/ppermute | solution.py:353
  64.6 0.1 collective-permute-start.13
  64.7 0.4 collective-permute-start.14
  65.1 0.1 collective-permute-start.15
  65.2 0.5 flip.1.down_ref
  65.8 0.0 copy-start.4
  65.8 0.0 copy-start.5
  65.8 0.0 copy-start.6
  65.8 0.0 copy-start.7
  65.8 0.0 copy-start.8
  65.9 0.0 copy-start.9
  65.9 1.6 %halo.1.halo_ref = bf16[296,128]{1,0:T(8,128)(2,1)S(1)} custom-call(bf16[296,512]{1,0:T(8,128)(2,1)S(1)} %collective-permute-done.4.a_ref.below_ref, bf16[296,512]{1,0:T(8,128)(2,1)S(1)} %collective-permute-done.11.c_ref.above_ref, bf16[296,2368]{1,0:T(8,128)(2,1)S(1)} %bitcast.23), custom_call_target="tpu_custom_call" | custom-call | flops 2000000000 | bytes 3000000 | tf_op jit(solution)/shard_map/halo/pallas_call | solution.py:193
  67.5 0.0 collective-permute-done.12.t4
  67.5 0.0 collective-permute-done.14.t6
  67.5 0.0 collective-permute-done.15.t7
  67.6 13.9 %last.1 = bf16[296,1024]{1,0:T(8,128)(2,1)} custom-call(bf16[296,512]{1,0:T(8,128)(2,1)S(1)} %pad_maximum_fusion.t0, bf16[296,512]{1,0:T(8,128)(2,1)S(1)} %collective-permute-done.8.t1, bf16[296,512]{1,0:T(8,128)(2,1)S(1)} %collective-permute-done.9.t2, bf16[296,512]{1,0:T(8,128)(2,1)S(1)} %collective-permute-done.10.t3, ...), custom_call_target="tpu_custom_call" | custom-call | flops 8000000000 | bytes 12000000 | tf_op jit(solution)/shard_map/last/pallas_call | solution.py:317
  (22 shorter events, 0.1 us)
Async XLA Ops:
  0.0 6.2 %copy-start.1 = (bf16[2368,296]{0,1:T(8,128)(2,1)S(1)}, bf16[2368,296]{0,1:T(8,128)(2,1)}, u32[]{:S(2)}) copy-start(bf16[2368,296]{0,1:T(8,128)(2,1)} %param.15) | copy-start | bytes 4205572
  1.9 22.4 %slice-start = ((s8[5607424]{0:T(1024)(128)(4,1)}), s8[4194304]{0:T(1024)(128)(4,1)S(1)}, s32[]{:S(2)}) async-start(s8[5607424]{0:T(1024)(128)(4,1)} %bitcast.16), calls=%async_computation | async-start | bytes 8388608
  2.0 22.3 %collective-permute-start.4 = (bf16[296,512]{1,0:T(8,128)(2,1)S(1)}, bf16[296,512]{1,0:T(8,128)(2,1)S(1)}, u32[]{:S(2)}, u32[]{:S(2)}) collective-permute-start(bf16[296,512]{1,0:T(8,128)(2,1)S(1)} %get-tuple-element.49.hi_ref.c_ref.b_ref), channel_id=1, source_target_pairs={{0,1},{1,2},{2,3},{3,4},{4,5},{5,6},{6,7},{7,8},{8,9},{9,10},{10,1... | collective-permute-start | bytes 909320 | tf_op jit(solution)/shard_map/ppermute | solution.py:344
  6.2 18.1 %slice-start.1 = ((s8[5607424]{0:T(1024)(128)(4,1)}), s8[1413120]{0:T(1024)(128)(4,1)S(1)}, s32[]{:S(2)}) async-start(s8[5607424]{0:T(1024)(128)(4,1)} %bitcast.16), calls=%async_computation.1 | async-start | bytes 2826240
  6.2 18.1 %copy-start.2 = (s32[1024,8]{0,1:T(8,128)S(1)}, s32[1024,8]{0,1:T(8,128)}, u32[]{:S(2)}) copy-start(s32[1024,8]{0,1:T(8,128)} %param.18) | copy-start | bytes 98308
  6.2 18.1 %copy-start.3 = (s32[1024,8]{0,1:T(8,128)S(1)}, s32[1024,8]{0,1:T(8,128)}, u32[]{:S(2)}) copy-start(s32[1024,8]{0,1:T(8,128)} %param.19) | copy-start | bytes 98308
  9.1 15.1 %collective-permute-start.2 = (bf16[16,296]{1,0:T(8,128)(2,1)S(1)}, bf16[16,296]{1,0:T(8,128)(2,1)S(1)}, u32[]{:S(2)}, u32[]{:S(2)}) collective-permute-start(bf16[16,296]{1,0:T(8,128)(2,1)S(1)} %get-tuple-element.27), channel_id=1, source_target_pairs={{0,64},{4,68},{8,72},{12,76},{16,80},{20,84},{24,88},{28,92},{32,9... | collective-permute-start | bytes 28424 | tf_op jit(solution)/shard_map/ppermute | solution.py:353
  12.1 12.1 %collective-permute-start.1 = (bf16[16,296]{1,0:T(8,128)(2,1)S(1)}, bf16[16,296]{1,0:T(8,128)(2,1)S(1)}, u32[]{:S(2)}, u32[]{:S(2)}) collective-permute-start(bf16[16,296]{1,0:T(8,128)(2,1)S(1)} %get-tuple-element.27), channel_id=1, source_target_pairs={{0,128},{4,132},{8,136},{12,140},{16,144},{20,148},{24,152},{28,15... | collective-permute-start | bytes 28424 | tf_op jit(solution)/shard_map/ppermute | solution.py:353
  17.2 7.0 %collective-permute-start = (bf16[16,296]{1,0:T(8,128)(2,1)S(1)}, bf16[16,296]{1,0:T(8,128)(2,1)S(1)}, u32[]{:S(2)}, u32[]{:S(2)}) collective-permute-start(bf16[16,296]{1,0:T(8,128)(2,1)S(1)} %get-tuple-element.27), channel_id=1, source_target_pairs={{0,192},{4,196},{8,200},{12,204},{16,208},{20,212},{24,216},{28,22... | collective-permute-start | bytes 28424 | tf_op jit(solution)/shard_map/ppermute | solution.py:353
  19.6 27.4 %collective-permute-start.11 = (bf16[296,512]{1,0:T(8,128)(2,1)S(1)}, bf16[296,512]{1,0:T(8,128)(2,1)S(1)}, u32[]{:S(2)}, u32[]{:S(2)}) collective-permute-start(bf16[296,512]{1,0:T(8,128)(2,1)S(1)} %get-tuple-element.39.lo_ref.b_ref.a_ref), channel_id=1, source_target_pairs={{1,0},{2,1},{3,2},{4,3},{5,4},{6,5},{7,6},{8,7},{9,8},{10,9},{11,1... | collective-permute-start | bytes 909320 | tf_op jit(solution)/shard_map/ppermute | solution.py:344
  24.2 6.6 %collective-permute-start.3 = (bf16[4,16,296]{2,1,0:T(8,128)(2,1)S(1)}, bf16[4,16,296]{2,1,0:T(8,128)(2,1)S(1)}, u32[]{:S(2)}, u32[]{:S(2)}) collective-permute-start(bf16[4,16,296]{2,1,0:T(8,128)(2,1)S(1)} %pad_maximum_fusion.1.even_ref), channel_id=1, source_target_pairs={{0,224},{4,228},{8,232},{12,236},{16,240},{20,244},{24,248},{28,25... | collective-permute-start | bytes 113672 | tf_op jit(solution)/shard_map/ppermute | solution.py:353
  30.9 11.6 %collective-permute-start.7 = (bf16[296,128]{1,0:T(8,128)(2,1)S(1)}, bf16[296,128]{1,0:T(8,128)(2,1)S(1)}, u32[]{:S(2)}, u32[]{:S(2)}) collective-permute-start(bf16[296,128]{1,0:T(8,128)(2,1)S(1)} %turn.1), channel_id=1, source_target_pairs={{0,8},{4,12},{8,16},{12,20},{16,24},{20,28},{24,0},{28,4},{32,40},... | collective-permute-start | bytes 227336 | tf_op jit(solution)/shard_map/ppermute | solution.py:353
  32.3 10.2 %collective-permute-start.6 = (bf16[296,128]{1,0:T(8,128)(2,1)S(1)}, bf16[296,128]{1,0:T(8,128)(2,1)S(1)}, u32[]{:S(2)}, u32[]{:S(2)}) collective-permute-start(bf16[296,128]{1,0:T(8,128)(2,1)S(1)} %turn.1), channel_id=1, source_target_pairs={{0,16},{4,20},{8,24},{12,28},{16,0},{20,4},{24,8},{28,12},{32,48},... | collective-permute-start | bytes 227336 | tf_op jit(solution)/shard_map/ppermute | solution.py:353
  34.9 7.6 %collective-permute-start.5 = (bf16[296,128]{1,0:T(8,128)(2,1)S(1)}, bf16[296,128]{1,0:T(8,128)(2,1)S(1)}, u32[]{:S(2)}, u32[]{:S(2)}) collective-permute-start(bf16[296,128]{1,0:T(8,128)(2,1)S(1)} %turn.1), channel_id=1, source_target_pairs={{0,24},{4,28},{8,0},{12,4},{16,8},{20,12},{24,16},{28,20},{32,56},... | collective-permute-start | bytes 227336 | tf_op jit(solution)/shard_map/ppermute | solution.py:353
  42.6 22.6 %copy-start = (bf16[296,2368]{1,0:T(8,128)(2,1)S(1)}, bf16[296,2368]{1,0:T(8,128)(2,1)}, u32[]{:S(2)}) copy-start(bf16[296,2368]{1,0:T(8,128)(2,1)} %down_ref.1) | copy-start | bytes 4205572
  42.6 17.3 %collective-permute-start.10 = (bf16[296,512]{1,0:T(8,128)(2,1)S(1)}, bf16[296,512]{1,0:T(8,128)(2,1)S(1)}, u32[]{:S(2)}, u32[]{:S(2)}) collective-permute-start(bf16[296,512]{1,0:T(8,128)(2,1)S(1)} %pad_maximum_fusion.t0), channel_id=1, source_target_pairs={{0,1},{1,2},{2,3},{3,0},{4,5},{5,6},{6,7},{7,4},{8,9},{9,10},{10,1... | collective-permute-start | bytes 909320 | tf_op jit(solution)/shard_map/ppermute | solution.py:353
  43.6 16.3 %collective-permute-start.9 = (bf16[296,512]{1,0:T(8,128)(2,1)S(1)}, bf16[296,512]{1,0:T(8,128)(2,1)S(1)}, u32[]{:S(2)}, u32[]{:S(2)}) collective-permute-start(bf16[296,512]{1,0:T(8,128)(2,1)S(1)} %pad_maximum_fusion.t0), channel_id=1, source_target_pairs={{0,2},{1,3},{2,0},{3,1},{4,6},{5,7},{6,4},{7,5},{8,10},{9,11},{10,... | collective-permute-start | bytes 909320 | tf_op jit(solution)/shard_map/ppermute | solution.py:353
  46.3 13.6 %collective-permute-start.8 = (bf16[296,512]{1,0:T(8,128)(2,1)S(1)}, bf16[296,512]{1,0:T(8,128)(2,1)S(1)}, u32[]{:S(2)}, u32[]{:S(2)}) collective-permute-start(bf16[296,512]{1,0:T(8,128)(2,1)S(1)} %pad_maximum_fusion.t0), channel_id=1, source_target_pairs={{0,3},{1,0},{2,1},{3,2},{4,7},{5,4},{6,5},{7,6},{8,11},{9,8},{10,9... | collective-permute-start | bytes 909320 | tf_op jit(solution)/shard_map/ppermute | solution.py:353
  59.9 7.5 %collective-permute-start.12 = (bf16[296,512]{1,0:T(8,128)(2,1)S(1)}, bf16[296,512]{1,0:T(8,128)(2,1)S(1)}, u32[]{:S(2)}, u32[]{:S(2)}) collective-permute-start(bf16[296,512]{1,0:T(8,128)(2,1)S(1)} %pad_maximum_fusion.t0), channel_id=1, source_target_pairs={{0,4},{4,0},{8,12},{12,8},{16,20},{20,16},{24,28},{28,24},{32,36},... | collective-permute-start | bytes 909320 | tf_op jit(solution)/shard_map/ppermute | solution.py:353
  64.6 2.8 %collective-permute-start.13 = (bf16[296,512]{1,0:T(8,128)(2,1)S(1)}, bf16[296,512]{1,0:T(8,128)(2,1)S(1)}, u32[]{:S(2)}, u32[]{:S(2)}) collective-permute-start(bf16[296,512]{1,0:T(8,128)(2,1)S(1)} %collective-permute-done.8.t1), channel_id=1, source_target_pairs={{0,4},{4,0},{8,12},{12,8},{16,20},{20,16},{24,28},{28,24},{32,36},... | collective-permute-start | bytes 909320 | tf_op jit(solution)/shard_map/ppermute | solution.py:353
  64.7 2.8 %collective-permute-start.14 = (bf16[296,512]{1,0:T(8,128)(2,1)S(1)}, bf16[296,512]{1,0:T(8,128)(2,1)S(1)}, u32[]{:S(2)}, u32[]{:S(2)}) collective-permute-start(bf16[296,512]{1,0:T(8,128)(2,1)S(1)} %collective-permute-done.9.t2), channel_id=1, source_target_pairs={{0,4},{4,0},{8,12},{12,8},{16,20},{20,16},{24,28},{28,24},{32,36},... | collective-permute-start | bytes 909320 | tf_op jit(solution)/shard_map/ppermute | solution.py:353
  65.1 2.4 %collective-permute-start.15 = (bf16[296,512]{1,0:T(8,128)(2,1)S(1)}, bf16[296,512]{1,0:T(8,128)(2,1)S(1)}, u32[]{:S(2)}, u32[]{:S(2)}) collective-permute-start(bf16[296,512]{1,0:T(8,128)(2,1)S(1)} %collective-permute-done.10.t3), channel_id=1, source_target_pairs={{0,4},{4,0},{8,12},{12,8},{16,20},{20,16},{24,28},{28,24},{32,36},... | collective-permute-start | bytes 909320 | tf_op jit(solution)/shard_map/ppermute | solution.py:353
  65.8 1.7 %copy-start.4 = (s32[128,8]{0,1:T(8,128)S(1)}, s32[128,8]{0,1:T(8,128)}, u32[]{:S(2)}) copy-start(s32[128,8]{0,1:T(8,128)} %param.20) | copy-start | bytes 12292
  65.8 1.7 %copy-start.5 = (s32[128,8]{0,1:T(8,128)S(1)}, s32[128,8]{0,1:T(8,128)}, u32[]{:S(2)}) copy-start(s32[128,8]{0,1:T(8,128)} %param.21) | copy-start | bytes 12292
  65.8 1.7 %copy-start.6 = (s32[16,8]{0,1:T(8,128)S(1)}, s32[16,8]{0,1:T(8,128)}, u32[]{:S(2)}) copy-start(s32[16,8]{0,1:T(8,128)} %param.22) | copy-start | bytes 1540
  65.8 1.7 %copy-start.7 = (s32[16,8]{0,1:T(8,128)S(1)}, s32[16,8]{0,1:T(8,128)}, u32[]{:S(2)}) copy-start(s32[16,8]{0,1:T(8,128)} %param.23) | copy-start | bytes 1540
  65.8 1.7 %copy-start.8 = (s32[2,8]{1,0:T(2,128)S(1)}, s32[2,8]{1,0:T(2,128)}, u32[]{:S(2)}) copy-start(s32[2,8]{1,0:T(2,128)} %src4_ref.1) | copy-start | bytes 196
  65.9 1.7 %copy-start.9 = (s32[2,8]{1,0:T(2,128)S(1)}, s32[2,8]{1,0:T(2,128)}, u32[]{:S(2)}) copy-start(s32[2,8]{1,0:T(2,128)} %cls4_ref.1) | copy-start | bytes 196

commit v9 on v7

--- a/solution.py
+++ b/solution.py
@@ -403,10 +403,11 @@
     *sides, seven_1 = tie(*sides, seven_1)
     plane = jnp.concatenate([column, *sides], axis=1)
     plane, seven_1, near_lo = tie(plane, seven_1, near_lo)
-    tables = [plane, along_x(plane, -1), along_x(plane, 2), along_x(plane, 1)]
+    tables = [along_x(plane, -1), along_x(plane, 2), along_x(plane, 1)]
+    other = along_core(plane, 1)
     seven_2 = near(2, 2, near_lo, hi, above, src_seven, cls_seven, maps)
     *tables, seven_2, late_up = tie(*tables, seven_2, up)
-    tables = tables + [along_core(table, 1) for table in tables]
+    tables = [plane, *tables, other] + [along_core(table, 1) for table in tables]
     halo = halo_six(below, above, late_up)
     sevens = [seven_0, seven_1, seven_2]
 

time: 79.5 us -> 79.5 us (level)
  no operation moved by 1% of the time
where the time goes in v9:
time: 79.5 us; the launch traced here: 79.3 us
  Pallas kernels  44.7 us (56%)
  starting transfers between devices  32.1 us (40%)
  other arithmetic  1.97 us (2%)
    pallas_call x3, Pallas kernels, near(): pl.pallas_call(functools.partial(near_body, block, count), out_shape=jax....  25.9 us
    ppermute x14, starting transfers between devices, turned(): return lax.ppermute(value, axis, pairs)  23.8 us
    pallas_call x1, Pallas kernels, last(): pl.pallas_call(last_body, out_shape=jax.ShapeDtypeStruct((F, 1024), BF),...  13.8 us
    ppermute x2, starting transfers between devices, shifted(): lax.ppermute(value, axis, [(source, source + steps) for source in range(f...  8.23 us
    pallas_call x1, Pallas kernels, rise(): pl.pallas_call(rise_body, out_shape=(jax.ShapeDtypeStruct((F, 128), BF),...  2.8 us
  transfers between devices with their start and end apart: 16, of which 0 were waited for; matrix products, arithmetic and copies ran while one was open for 0% of the time, Pallas kernels for 39%

profile of v9, /device:TPU:1, one launch (start us, length us, event | category | flops | bytes accessed | tf_op | source)
XLA Modules:
  0.0 79.3 jit_solution(2217890288017166551)
XLA Ops:
  0.0 0.8 %convert_element_type.3 = bf16[1024]{0:T(1024)(128)(2,1)S(1)} convert(s32[1024]{0:T(1024)} %param.14) | non-fusion elementwise | flops 1024 | bytes 6144 | tf_op jit(solution)/shard_map/convert_element_type | solution.py:383
  0.8 1.1 %multiply_bitcast_fusion = bf16[296,1024]{1,0:T(8,128)(2,1)S(1)} fusion(bf16[1024,296]{0,1:T(8,128)(2,1)} %param.13, bf16[1024]{0:T(1024)(128)(2,1)S(1)} %convert_element_type.3), kind=kLoop, calls=%fused_computation | loop fusion | flops 303104 | bytes 1214464 | tf_op jit(solution)/shard_map/mul | solution.py:383
  1.9 0.0 slice-start
  2.0 4.2 %collective-permute-start.4 = (bf16[296,512]{1,0:T(8,128)(2,1)S(1)}, bf16[296,512]{1,0:T(8,128)(2,1)S(1)}, u32[]{:S(2)}, u32[]{:S(2)}) collective-permute-start(bf16[296,512]{1,0:T(8,128)(2,1)S(1)} %get-tuple-element.49.hi_ref.c_ref.b_ref), channel_id=1, source_target_pairs={{0,1},{1,2},{2,3},{3,4},{4,5},{5,6},{6,7},{7,8},{8,9},{9,10},{10,1... | collective-permute-start | bytes 909320 | tf_op jit(solution)/shard_map/ppermute | solution.py:344
  6.2 0.0 slice-start.1
  6.2 0.0 copy-start.2
  6.2 0.0 copy-start.3
  6.2 2.8 %rise.1 = (bf16[296,128]{1,0:T(8,128)(2,1)S(1)}, bf16[16,296]{1,0:T(8,128)(2,1)S(1)}) custom-call(bf16[296,512]{1,0:T(8,128)(2,1)S(1)} %get-tuple-element.40.lo_ref.b_ref.a_ref, bf16[296,512]{1,0:T(8,128)(2,1)S(1)} %get-tuple-element.49.hi_ref.c_ref.b_ref, bf16[296,2368]{1,0:T(8,128)(2,1)S(1)} %bitcast.21), custom_call_target="tpu_custom_call" | custom-call | flops 8000000000 | bytes 3000000 | tf_op jit(solution)/shard_map/rise/pallas_call | solution.py:65
  9.1 5.6 %collective-permute-start.1 = (bf16[16,296]{1,0:T(8,128)(2,1)S(1)}, bf16[16,296]{1,0:T(8,128)(2,1)S(1)}, u32[]{:S(2)}, u32[]{:S(2)}) collective-permute-start(bf16[16,296]{1,0:T(8,128)(2,1)S(1)} %get-tuple-element.27), channel_id=1, source_target_pairs={{0,224},{4,228},{8,232},{12,236},{16,240},{20,244},{24,248},{28,25... | collective-permute-start | bytes 28424 | tf_op jit(solution)/shard_map/ppermute | solution.py:353
  14.7 0.0 collective-permute-start
  14.7 4.0 %collective-permute-start.11 = (bf16[296,512]{1,0:T(8,128)(2,1)S(1)}, bf16[296,512]{1,0:T(8,128)(2,1)S(1)}, u32[]{:S(2)}, u32[]{:S(2)}) collective-permute-start(bf16[296,512]{1,0:T(8,128)(2,1)S(1)} %get-tuple-element.40.lo_ref.b_ref.a_ref), channel_id=1, source_target_pairs={{1,0},{2,1},{3,2},{4,3},{5,4},{6,5},{7,6},{8,7},{9,8},{10,9},{11,1... | collective-permute-start | bytes 909320 | tf_op jit(solution)/shard_map/ppermute | solution.py:344
  18.7 0.0 collective-permute-done.1
  18.7 0.0 collective-permute-done
  18.7 2.7 %collective-permute-start.3 = (bf16[3,16,296]{2,1,0:T(8,128)(2,1)S(1)}, bf16[3,16,296]{2,1,0:T(8,128)(2,1)S(1)}, u32[]{:S(2)}, u32[]{:S(2)}) collective-permute-start(bf16[3,16,296]{2,1,0:T(8,128)(2,1)S(1)} %pad_maximum_fusion.1.middle_ref), channel_id=1, source_target_pairs={{0,160},{4,164},{8,168},{12,172},{16,176},{20,180},{24,184},{28,18... | collective-permute-start | bytes 85256 | tf_op jit(solution)/shard_map/ppermute | solution.py:353
  21.5 0.6 collective-permute-start.2
  22.1 0.0 collective-permute-done.4.a_ref.below_ref
  22.1 6.5 %near0.1.s0 = f32[1,296,256]{2,1,0:T(8,128)S(1)} custom-call(bf16[296,512]{1,0:T(8,128)(2,1)S(1)} %collective-permute-done.4.a_ref.below_ref, bf16[296,512]{1,0:T(8,128)(2,1)S(1)} %get-tuple-element.40.lo_ref.b_ref.a_ref, bf16[296,512]{1,0:T(8,128)(2,1)S(1)} %get-tuple-element.49.hi_ref.c_ref.b_ref, s32[8,1024]{1,0:T(8,128)S(1)} %bitcast.24, ...), custom_call_target="tpu_custom_call" | custom-call | flops 6000000000 | bytes 6000000 | tf_op jit(solution)/shard_map/near0/pallas_call | solution.py:153
  28.6 0.0 collective-permute-done.2.lower_ref
  28.6 0.0 collective-permute-done.3.upper_ref
  28.6 0.1 turn.1
  28.7 1.4 %collective-permute-start.7 = (bf16[296,128]{1,0:T(8,128)(2,1)S(1)}, bf16[296,128]{1,0:T(8,128)(2,1)S(1)}, u32[]{:S(2)}, u32[]{:S(2)}) collective-permute-start(bf16[296,128]{1,0:T(8,128)(2,1)S(1)} %turn.1), channel_id=1, source_target_pairs={{0,8},{4,12},{8,16},{12,20},{16,24},{20,28},{24,0},{28,4},{32,40},... | collective-permute-start | bytes 227336 | tf_op jit(solution)/shard_map/ppermute | solution.py:353
  30.1 2.6 %collective-permute-start.6 = (bf16[296,128]{1,0:T(8,128)(2,1)S(1)}, bf16[296,128]{1,0:T(8,128)(2,1)S(1)}, u32[]{:S(2)}, u32[]{:S(2)}) collective-permute-start(bf16[296,128]{1,0:T(8,128)(2,1)S(1)} %turn.1), channel_id=1, source_target_pairs={{0,16},{4,20},{8,24},{12,28},{16,0},{20,4},{24,8},{28,12},{32,48},... | collective-permute-start | bytes 227336 | tf_op jit(solution)/shard_map/ppermute | solution.py:353
  32.7 1.1 %collective-permute-start.5 = (bf16[296,128]{1,0:T(8,128)(2,1)S(1)}, bf16[296,128]{1,0:T(8,128)(2,1)S(1)}, u32[]{:S(2)}, u32[]{:S(2)}) collective-permute-start(bf16[296,128]{1,0:T(8,128)(2,1)S(1)} %turn.1), channel_id=1, source_target_pairs={{0,24},{4,28},{8,0},{12,4},{16,8},{20,12},{24,16},{28,20},{32,56},... | collective-permute-start | bytes 227336 | tf_op jit(solution)/shard_map/ppermute | solution.py:353
  33.8 6.5 %near1.1.s1 = f32[1,296,256]{2,1,0:T(8,128)S(1)} custom-call(bf16[296,512]{1,0:T(8,128)(2,1)S(1)} %collective-permute-done.4.a_ref.below_ref, bf16[296,512]{1,0:T(8,128)(2,1)S(1)} %get-tuple-element.40.lo_ref.b_ref.a_ref, bf16[296,512]{1,0:T(8,128)(2,1)S(1)} %get-tuple-element.49.hi_ref.c_ref.b_ref, s32[8,1024]{1,0:T(8,128)S(1)} %bitcast.25, ...), custom_call_target="tpu_custom_call" | custom-call | flops 6000000000 | bytes 6000000 | tf_op jit(solution)/shard_map/near1/pallas_call | solution.py:153
  40.3 0.0 collective-permute-done.7
  40.3 0.0 collective-permute-done.6
  40.4 0.0 copy-start
  40.4 3.7 %collective-permute-start.12 = (bf16[296,512]{1,0:T(8,128)(2,1)S(1)}, bf16[296,512]{1,0:T(8,128)(2,1)S(1)}, u32[]{:S(2)}, u32[]{:S(2)}) collective-permute-start(bf16[296,512]{1,0:T(8,128)(2,1)S(1)} %pad_maximum_fusion.t0), channel_id=1, source_target_pairs={{0,4},{4,0},{8,12},{12,8},{16,20},{20,16},{24,28},{28,24},{32,36},... | collective-permute-start | bytes 909320 | tf_op jit(solution)/shard_map/ppermute | solution.py:353
  44.1 1.2 %collective-permute-start.10 = (bf16[296,512]{1,0:T(8,128)(2,1)S(1)}, bf16[296,512]{1,0:T(8,128)(2,1)S(1)}, u32[]{:S(2)}, u32[]{:S(2)}) collective-permute-start(bf16[296,512]{1,0:T(8,128)(2,1)S(1)} %pad_maximum_fusion.t0), channel_id=1, source_target_pairs={{0,1},{1,2},{2,3},{3,0},{4,5},{5,6},{6,7},{7,4},{8,9},{9,10},{10,1... | collective-permute-start | bytes 909320 | tf_op jit(solution)/shard_map/ppermute | solution.py:353
  45.3 1.2 %collective-permute-start.9 = (bf16[296,512]{1,0:T(8,128)(2,1)S(1)}, bf16[296,512]{1,0:T(8,128)(2,1)S(1)}, u32[]{:S(2)}, u32[]{:S(2)}) collective-permute-start(bf16[296,512]{1,0:T(8,128)(2,1)S(1)} %pad_maximum_fusion.t0), channel_id=1, source_target_pairs={{0,2},{1,3},{2,0},{3,1},{4,6},{5,7},{6,4},{7,5},{8,10},{9,11},{10,... | collective-permute-start | bytes 909320 | tf_op jit(solution)/shard_map/ppermute | solution.py:353
  46.6 2.1 %collective-permute-start.8 = (bf16[296,512]{1,0:T(8,128)(2,1)S(1)}, bf16[296,512]{1,0:T(8,128)(2,1)S(1)}, u32[]{:S(2)}, u32[]{:S(2)}) collective-permute-start(bf16[296,512]{1,0:T(8,128)(2,1)S(1)} %pad_maximum_fusion.t0), channel_id=1, source_target_pairs={{0,3},{1,0},{2,1},{3,2},{4,7},{5,4},{6,5},{7,6},{8,11},{9,8},{10,9... | collective-permute-start | bytes 909320 | tf_op jit(solution)/shard_map/ppermute | solution.py:353
  48.7 12.9 %near2.1.s2 = f32[2,296,256]{2,1,0:T(8,128)S(1)} custom-call(bf16[296,512]{1,0:T(8,128)(2,1)S(1)} %get-tuple-element.40.lo_ref.b_ref.a_ref, bf16[296,512]{1,0:T(8,128)(2,1)S(1)} %get-tuple-element.49.hi_ref.c_ref.b_ref, bf16[296,512]{1,0:T(8,128)(2,1)S(1)} %collective-permute-done.11.c_ref.above_ref, s32[8,1024]{1,0:T(8,128)S(1)} %bitcast.26, ...), custom_call_target="tpu_custom_call" | custom-call | flops 12000000000 | bytes 6000000 | tf_op jit(solution)/shard_map/near2/pallas_call | solution.py:153
  61.6 0.0 collective-permute-done.10.t3
  61.6 0.0 collective-permute-done.9.t2
  61.6 1.0 %collective-permute-start.13 = (bf16[296,512]{1,0:T(8,128)(2,1)S(1)}, bf16[296,512]{1,0:T(8,128)(2,1)S(1)}, u32[]{:S(2)}, u32[]{:S(2)}) collective-permute-start(bf16[296,512]{1,0:T(8,128)(2,1)S(1)} %collective-permute-done.8.t1), channel_id=1, source_target_pairs={{0,4},{4,0},{8,12},{12,8},{16,20},{20,16},{24,28},{28,24},{32,36},... | collective-permute-start | bytes 909320 | tf_op jit(solution)/shard_map/ppermute | solution.py:353
  62.6 0.1 collective-permute-start.14
  62.7 0.4 collective-permute-start.15
  63.2 0.5 flip.1.down_ref
  63.7 0.0 copy-start.4
  63.7 0.0 copy-start.5
  63.7 0.0 copy-start.6
  63.7 0.0 copy-start.7
  63.8 0.0 copy-start.8
  63.8 0.0 copy-start.9
  63.8 1.6 %halo.1.halo_ref = bf16[296,128]{1,0:T(8,128)(2,1)S(1)} custom-call(bf16[296,512]{1,0:T(8,128)(2,1)S(1)} %collective-permute-done.4.a_ref.below_ref, bf16[296,512]{1,0:T(8,128)(2,1)S(1)} %collective-permute-done.11.c_ref.above_ref, bf16[296,2368]{1,0:T(8,128)(2,1)S(1)} %bitcast.22), custom_call_target="tpu_custom_call" | custom-call | flops 2000000000 | bytes 3000000 | tf_op jit(solution)/shard_map/halo/pallas_call | solution.py:193
  65.4 0.0 collective-permute-done.13.t5
  65.4 0.0 collective-permute-done.14.t6
  65.5 13.8 %last.1 = bf16[296,1024]{1,0:T(8,128)(2,1)} custom-call(bf16[296,512]{1,0:T(8,128)(2,1)S(1)} %pad_maximum_fusion.t0, bf16[296,512]{1,0:T(8,128)(2,1)S(1)} %collective-permute-done.8.t1, bf16[296,512]{1,0:T(8,128)(2,1)S(1)} %collective-permute-done.9.t2, bf16[296,512]{1,0:T(8,128)(2,1)S(1)} %collective-permute-done.10.t3, ...), custom_call_target="tpu_custom_call" | custom-call | flops 8000000000 | bytes 12000000 | tf_op jit(solution)/shard_map/last/pallas_call | solution.py:317
  (23 shorter events, 0.1 us)
Async XLA Ops:
  0.0 6.2 %copy-start.1 = (bf16[2368,296]{0,1:T(8,128)(2,1)S(1)}, bf16[2368,296]{0,1:T(8,128)(2,1)}, u32[]{:S(2)}) copy-start(bf16[2368,296]{0,1:T(8,128)(2,1)} %param.15) | copy-start | bytes 4205572
  1.9 20.2 %slice-start = ((s8[5607424]{0:T(1024)(128)(4,1)}), s8[4194304]{0:T(1024)(128)(4,1)S(1)}, s32[]{:S(2)}) async-start(s8[5607424]{0:T(1024)(128)(4,1)} %bitcast.15), calls=%async_computation | async-start | bytes 8388608
  2.0 20.1 %collective-permute-start.4 = (bf16[296,512]{1,0:T(8,128)(2,1)S(1)}, bf16[296,512]{1,0:T(8,128)(2,1)S(1)}, u32[]{:S(2)}, u32[]{:S(2)}) collective-permute-start(bf16[296,512]{1,0:T(8,128)(2,1)S(1)} %get-tuple-element.49.hi_ref.c_ref.b_ref), channel_id=1, source_target_pairs={{0,1},{1,2},{2,3},{3,4},{4,5},{5,6},{6,7},{7,8},{8,9},{9,10},{10,1... | collective-permute-start | bytes 909320 | tf_op jit(solution)/shard_map/ppermute | solution.py:344
  6.2 15.9 %slice-start.1 = ((s8[5607424]{0:T(1024)(128)(4,1)}), s8[1413120]{0:T(1024)(128)(4,1)S(1)}, s32[]{:S(2)}) async-start(s8[5607424]{0:T(1024)(128)(4,1)} %bitcast.15), calls=%async_computation.1 | async-start | bytes 2826240
  6.2 15.9 %copy-start.2 = (s32[1024,8]{0,1:T(8,128)S(1)}, s32[1024,8]{0,1:T(8,128)}, u32[]{:S(2)}) copy-start(s32[1024,8]{0,1:T(8,128)} %param.18) | copy-start | bytes 98308
  6.2 15.9 %copy-start.3 = (s32[1024,8]{0,1:T(8,128)S(1)}, s32[1024,8]{0,1:T(8,128)}, u32[]{:S(2)}) copy-start(s32[1024,8]{0,1:T(8,128)} %param.19) | copy-start | bytes 98308
  9.1 9.6 %collective-permute-start.1 = (bf16[16,296]{1,0:T(8,128)(2,1)S(1)}, bf16[16,296]{1,0:T(8,128)(2,1)S(1)}, u32[]{:S(2)}, u32[]{:S(2)}) collective-permute-start(bf16[16,296]{1,0:T(8,128)(2,1)S(1)} %get-tuple-element.27), channel_id=1, source_target_pairs={{0,224},{4,228},{8,232},{12,236},{16,240},{20,244},{24,248},{28,25... | collective-permute-start | bytes 28424 | tf_op jit(solution)/shard_map/ppermute | solution.py:353
  14.7 4.0 %collective-permute-start = (bf16[16,296]{1,0:T(8,128)(2,1)S(1)}, bf16[16,296]{1,0:T(8,128)(2,1)S(1)}, u32[]{:S(2)}, u32[]{:S(2)}) collective-permute-start(bf16[16,296]{1,0:T(8,128)(2,1)S(1)} %get-tuple-element.27), channel_id=1, source_target_pairs={{0,32},{4,36},{8,40},{12,44},{16,48},{20,52},{24,56},{28,60},{32,6... | collective-permute-start | bytes 28424 | tf_op jit(solution)/shard_map/ppermute | solution.py:353
  14.7 34.0 %collective-permute-start.11 = (bf16[296,512]{1,0:T(8,128)(2,1)S(1)}, bf16[296,512]{1,0:T(8,128)(2,1)S(1)}, u32[]{:S(2)}, u32[]{:S(2)}) collective-permute-start(bf16[296,512]{1,0:T(8,128)(2,1)S(1)} %get-tuple-element.40.lo_ref.b_ref.a_ref), channel_id=1, source_target_pairs={{1,0},{2,1},{3,2},{4,3},{5,4},{6,5},{7,6},{8,7},{9,8},{10,9},{11,1... | collective-permute-start | bytes 909320 | tf_op jit(solution)/shard_map/ppermute | solution.py:344
  18.7 9.9 %collective-permute-start.3 = (bf16[3,16,296]{2,1,0:T(8,128)(2,1)S(1)}, bf16[3,16,296]{2,1,0:T(8,128)(2,1)S(1)}, u32[]{:S(2)}, u32[]{:S(2)}) collective-permute-start(bf16[3,16,296]{2,1,0:T(8,128)(2,1)S(1)} %pad_maximum_fusion.1.middle_ref), channel_id=1, source_target_pairs={{0,160},{4,164},{8,168},{12,172},{16,176},{20,180},{24,184},{28,18... | collective-permute-start | bytes 85256 | tf_op jit(solution)/shard_map/ppermute | solution.py:353
  21.5 7.1 %collective-permute-start.2 = (bf16[2,16,296]{2,1,0:T(8,128)(2,1)S(1)}, bf16[2,16,296]{2,1,0:T(8,128)(2,1)S(1)}, u32[]{:S(2)}, u32[]{:S(2)}) collective-permute-start(bf16[2,16,296]{2,1,0:T(8,128)(2,1)S(1)} %slice.11), channel_id=1, source_target_pairs={{0,96},{4,100},{8,104},{12,108},{16,112},{20,116},{24,120},{28,124... | collective-permute-start | bytes 56840 | tf_op jit(solution)/shard_map/ppermute | solution.py:353
  28.7 11.6 %collective-permute-start.7 = (bf16[296,128]{1,0:T(8,128)(2,1)S(1)}, bf16[296,128]{1,0:T(8,128)(2,1)S(1)}, u32[]{:S(2)}, u32[]{:S(2)}) collective-permute-start(bf16[296,128]{1,0:T(8,128)(2,1)S(1)} %turn.1), channel_id=1, source_target_pairs={{0,8},{4,12},{8,16},{12,20},{16,24},{20,28},{24,0},{28,4},{32,40},... | collective-permute-start | bytes 227336 | tf_op jit(solution)/shard_map/ppermute | solution.py:353
  30.1 10.2 %collective-permute-start.6 = (bf16[296,128]{1,0:T(8,128)(2,1)S(1)}, bf16[296,128]{1,0:T(8,128)(2,1)S(1)}, u32[]{:S(2)}, u32[]{:S(2)}) collective-permute-start(bf16[296,128]{1,0:T(8,128)(2,1)S(1)} %turn.1), channel_id=1, source_target_pairs={{0,16},{4,20},{8,24},{12,28},{16,0},{20,4},{24,8},{28,12},{32,48},... | collective-permute-start | bytes 227336 | tf_op jit(solution)/shard_map/ppermute | solution.py:353
  32.7 7.6 %collective-permute-start.5 = (bf16[296,128]{1,0:T(8,128)(2,1)S(1)}, bf16[296,128]{1,0:T(8,128)(2,1)S(1)}, u32[]{:S(2)}, u32[]{:S(2)}) collective-permute-start(bf16[296,128]{1,0:T(8,128)(2,1)S(1)} %turn.1), channel_id=1, source_target_pairs={{0,24},{4,28},{8,0},{12,4},{16,8},{20,12},{24,16},{28,20},{32,56},... | collective-permute-start | bytes 227336 | tf_op jit(solution)/shard_map/ppermute | solution.py:353
  40.4 22.8 %copy-start = (bf16[296,2368]{1,0:T(8,128)(2,1)S(1)}, bf16[296,2368]{1,0:T(8,128)(2,1)}, u32[]{:S(2)}) copy-start(bf16[296,2368]{1,0:T(8,128)(2,1)} %down_ref.1) | copy-start | bytes 4205572
  40.4 25.0 %collective-permute-start.12 = (bf16[296,512]{1,0:T(8,128)(2,1)S(1)}, bf16[296,512]{1,0:T(8,128)(2,1)S(1)}, u32[]{:S(2)}, u32[]{:S(2)}) collective-permute-start(bf16[296,512]{1,0:T(8,128)(2,1)S(1)} %pad_maximum_fusion.t0), channel_id=1, source_target_pairs={{0,4},{4,0},{8,12},{12,8},{16,20},{20,16},{24,28},{28,24},{32,36},... | collective-permute-start | bytes 909320 | tf_op jit(solution)/shard_map/ppermute | solution.py:353
  44.1 17.5 %collective-permute-start.10 = (bf16[296,512]{1,0:T(8,128)(2,1)S(1)}, bf16[296,512]{1,0:T(8,128)(2,1)S(1)}, u32[]{:S(2)}, u32[]{:S(2)}) collective-permute-start(bf16[296,512]{1,0:T(8,128)(2,1)S(1)} %pad_maximum_fusion.t0), channel_id=1, source_target_pairs={{0,1},{1,2},{2,3},{3,0},{4,5},{5,6},{6,7},{7,4},{8,9},{9,10},{10,1... | collective-permute-start | bytes 909320 | tf_op jit(solution)/shard_map/ppermute | solution.py:353
  45.3 16.3 %collective-permute-start.9 = (bf16[296,512]{1,0:T(8,128)(2,1)S(1)}, bf16[296,512]{1,0:T(8,128)(2,1)S(1)}, u32[]{:S(2)}, u32[]{:S(2)}) collective-permute-start(bf16[296,512]{1,0:T(8,128)(2,1)S(1)} %pad_maximum_fusion.t0), channel_id=1, source_target_pairs={{0,2},{1,3},{2,0},{3,1},{4,6},{5,7},{6,4},{7,5},{8,10},{9,11},{10,... | collective-permute-start | bytes 909320 | tf_op jit(solution)/shard_map/ppermute | solution.py:353
  46.6 15.0 %collective-permute-start.8 = (bf16[296,512]{1,0:T(8,128)(2,1)S(1)}, bf16[296,512]{1,0:T(8,128)(2,1)S(1)}, u32[]{:S(2)}, u32[]{:S(2)}) collective-permute-start(bf16[296,512]{1,0:T(8,128)(2,1)S(1)} %pad_maximum_fusion.t0), channel_id=1, source_target_pairs={{0,3},{1,0},{2,1},{3,2},{4,7},{5,4},{6,5},{7,6},{8,11},{9,8},{10,9... | collective-permute-start | bytes 909320 | tf_op jit(solution)/shard_map/ppermute | solution.py:353
  61.6 3.8 %collective-permute-start.13 = (bf16[296,512]{1,0:T(8,128)(2,1)S(1)}, bf16[296,512]{1,0:T(8,128)(2,1)S(1)}, u32[]{:S(2)}, u32[]{:S(2)}) collective-permute-start(bf16[296,512]{1,0:T(8,128)(2,1)S(1)} %collective-permute-done.8.t1), channel_id=1, source_target_pairs={{0,4},{4,0},{8,12},{12,8},{16,20},{20,16},{24,28},{28,24},{32,36},... | collective-permute-start | bytes 909320 | tf_op jit(solution)/shard_map/ppermute | solution.py:353
  62.6 2.7 %collective-permute-start.14 = (bf16[296,512]{1,0:T(8,128)(2,1)S(1)}, bf16[296,512]{1,0:T(8,128)(2,1)S(1)}, u32[]{:S(2)}, u32[]{:S(2)}) collective-permute-start(bf16[296,512]{1,0:T(8,128)(2,1)S(1)} %collective-permute-done.9.t2), channel_id=1, source_target_pairs={{0,4},{4,0},{8,12},{12,8},{16,20},{20,16},{24,28},{28,24},{32,36},... | collective-permute-start | bytes 909320 | tf_op jit(solution)/shard_map/ppermute | solution.py:353
  62.7 2.7 %collective-permute-start.15 = (bf16[296,512]{1,0:T(8,128)(2,1)S(1)}, bf16[296,512]{1,0:T(8,128)(2,1)S(1)}, u32[]{:S(2)}, u32[]{:S(2)}) collective-permute-start(bf16[296,512]{1,0:T(8,128)(2,1)S(1)} %collective-permute-done.10.t3), channel_id=1, source_target_pairs={{0,4},{4,0},{8,12},{12,8},{16,20},{20,16},{24,28},{28,24},{32,36},... | collective-permute-start | bytes 909320 | tf_op jit(solution)/shard_map/ppermute | solution.py:353
  63.7 1.7 %copy-start.4 = (s32[128,8]{0,1:T(8,128)S(1)}, s32[128,8]{0,1:T(8,128)}, u32[]{:S(2)}) copy-start(s32[128,8]{0,1:T(8,128)} %param.20) | copy-start | bytes 12292
  63.7 1.7 %copy-start.5 = (s32[128,8]{0,1:T(8,128)S(1)}, s32[128,8]{0,1:T(8,128)}, u32[]{:S(2)}) copy-start(s32[128,8]{0,1:T(8,128)} %param.21) | copy-start | bytes 12292
  63.7 1.7 %copy-start.6 = (s32[16,8]{0,1:T(8,128)S(1)}, s32[16,8]{0,1:T(8,128)}, u32[]{:S(2)}) copy-start(s32[16,8]{0,1:T(8,128)} %param.22) | copy-start | bytes 1540
  63.7 1.7 %copy-start.7 = (s32[16,8]{0,1:T(8,128)S(1)}, s32[16,8]{0,1:T(8,128)}, u32[]{:S(2)}) copy-start(s32[16,8]{0,1:T(8,128)} %param.23) | copy-start | bytes 1540
  63.8 1.7 %copy-start.8 = (s32[2,8]{1,0:T(2,128)S(1)}, s32[2,8]{1,0:T(2,128)}, u32[]{:S(2)}) copy-start(s32[2,8]{1,0:T(2,128)} %src4_ref.1) | copy-start | bytes 196
  63.8 1.7 %copy-start.9 = (s32[2,8]{1,0:T(2,128)S(1)}, s32[2,8]{1,0:T(2,128)}, u32[]{:S(2)}) copy-start(s32[2,8]{1,0:T(2,128)} %cls4_ref.1) | copy-start | bytes 196

commit v10 on v9

--- a/solution.py
+++ b/solution.py
@@ -380,7 +380,8 @@
 ):
     leaves = leaf_multipoles.T
     up, maps = upward_maps.T, transfer_maps.T
-    masked = leaves * occupancy.astype(BF)[None, :]
+    rows = lax.broadcasted_iota(jnp.int32, leaves.shape, 0)
+    masked = jnp.where(occupancy[None, :] + rows > rows, leaves, jnp.zeros_like(leaves))
     lo, hi = masked[:, :512], masked[:, 512:]
     below = shifted(hi, ("cells", "sub"), 1)
     above = shifted(lo, ("cells", "sub"), -1)

time: 79.5 us -> 78.8 us (level)
    select_n x0 -> x1, other arithmetic: none -> 1.46 us  [body(): jnp.where(occupancy[None, :] + rows > rows, leaves, jnp.zeros_like(leaves))]
    mul x1 -> x0, other arithmetic: 1.11 us -> none  [body(): masked = leaves * occupancy.astype(BF)[None, :]]
    convert_element_type x1 -> x0, other arithmetic: 0.8 us -> none  [body(): masked = leaves * occupancy.astype(BF)[None, :]]
where the time goes in v10:
time: 78.8 us; the launch traced here: 78.7 us
  Pallas kernels  44.8 us (57%)
  starting transfers between devices  31.9 us (40%)
  other arithmetic  1.51 us (2%)
    pallas_call x3, Pallas kernels, near(): pl.pallas_call(functools.partial(near_body, block, count), out_shape=jax....  25.9 us
    ppermute x14, starting transfers between devices, turned(): return lax.ppermute(value, axis, pairs)  23.6 us
    pallas_call x1, Pallas kernels, last(): pl.pallas_call(last_body, out_shape=jax.ShapeDtypeStruct((F, 1024), BF),...  13.8 us
    ppermute x2, starting transfers between devices, shifted(): lax.ppermute(value, axis, [(source, source + steps) for source in range(f...  8.23 us
    pallas_call x1, Pallas kernels, rise(): pl.pallas_call(rise_body, out_shape=(jax.ShapeDtypeStruct((F, 128), BF),...  2.8 us
    pallas_call x1, Pallas kernels, halo_six(): pl.pallas_call(halo_body, out_shape=jax.ShapeDtypeStruct((F, 128), BF), i...  1.58 us
  transfers between devices with their start and end apart: 16, of which 0 were waited for; matrix products, arithmetic and copies ran while one was open for 0% of the time, Pallas kernels for 39%

profile of v10, /device:TPU:1, one launch (start us, length us, event | category | flops | bytes accessed | tf_op | source)
XLA Modules:
  0.0 78.7 jit_solution(2427937810268877239)
XLA Ops:
  0.0 1.5 %fusion = bf16[296,1024]{1,0:T(8,128)(2,1)S(1)} fusion(bf16[1024,296]{0,1:T(8,128)(2,1)} %param.13, s32[1024]{0:T(1024)} %param.14), kind=kLoop, calls=%fused_computation.1 | loop fusion | flops 909312 | bytes 1216512 | tf_op jit(solution)/shard_map/jit(_where)/select_n | solution.py:384
  1.5 0.0 slice-start
  1.5 4.2 %collective-permute-start.4 = (bf16[296,512]{1,0:T(8,128)(2,1)S(1)}, bf16[296,512]{1,0:T(8,128)(2,1)S(1)}, u32[]{:S(2)}, u32[]{:S(2)}) collective-permute-start(bf16[296,512]{1,0:T(8,128)(2,1)S(1)} %get-tuple-element.49.hi_ref.c_ref.b_ref), channel_id=1, source_target_pairs={{0,1},{1,2},{2,3},{3,4},{4,5},{5,6},{6,7},{7,8},{8,9},{9,10},{10,1... | collective-permute-start | bytes 909320 | tf_op jit(solution)/shard_map/ppermute | solution.py:344
  5.8 0.0 slice-start.1
  5.8 0.0 copy-start.2
  5.8 0.0 copy-start.3
  5.8 2.8 %rise.1 = (bf16[296,128]{1,0:T(8,128)(2,1)S(1)}, bf16[16,296]{1,0:T(8,128)(2,1)S(1)}) custom-call(bf16[296,512]{1,0:T(8,128)(2,1)S(1)} %get-tuple-element.40.lo_ref.b_ref.a_ref, bf16[296,512]{1,0:T(8,128)(2,1)S(1)} %get-tuple-element.49.hi_ref.c_ref.b_ref, bf16[296,2368]{1,0:T(8,128)(2,1)S(1)} %bitcast.21), custom_call_target="tpu_custom_call" | custom-call | flops 8000000000 | bytes 3000000 | tf_op jit(solution)/shard_map/rise/pallas_call | solution.py:65
  8.6 5.6 %collective-permute-start.1 = (bf16[16,296]{1,0:T(8,128)(2,1)S(1)}, bf16[16,296]{1,0:T(8,128)(2,1)S(1)}, u32[]{:S(2)}, u32[]{:S(2)}) collective-permute-start(bf16[16,296]{1,0:T(8,128)(2,1)S(1)} %get-tuple-element.27), channel_id=1, source_target_pairs={{0,224},{4,228},{8,232},{12,236},{16,240},{20,244},{24,248},{28,25... | collective-permute-start | bytes 28424 | tf_op jit(solution)/shard_map/ppermute | solution.py:353
  14.2 0.0 collective-permute-start
  14.2 4.0 %collective-permute-start.11 = (bf16[296,512]{1,0:T(8,128)(2,1)S(1)}, bf16[296,512]{1,0:T(8,128)(2,1)S(1)}, u32[]{:S(2)}, u32[]{:S(2)}) collective-permute-start(bf16[296,512]{1,0:T(8,128)(2,1)S(1)} %get-tuple-element.40.lo_ref.b_ref.a_ref), channel_id=1, source_target_pairs={{1,0},{2,1},{3,2},{4,3},{5,4},{6,5},{7,6},{8,7},{9,8},{10,9},{11,1... | collective-permute-start | bytes 909320 | tf_op jit(solution)/shard_map/ppermute | solution.py:344
  18.2 0.0 collective-permute-done.1
  18.2 0.0 collective-permute-done
  18.3 2.7 %collective-permute-start.3 = (bf16[3,16,296]{2,1,0:T(8,128)(2,1)S(1)}, bf16[3,16,296]{2,1,0:T(8,128)(2,1)S(1)}, u32[]{:S(2)}, u32[]{:S(2)}) collective-permute-start(bf16[3,16,296]{2,1,0:T(8,128)(2,1)S(1)} %pad_maximum_fusion.1.middle_ref), channel_id=1, source_target_pairs={{0,160},{4,164},{8,168},{12,172},{16,176},{20,180},{24,184},{28,18... | collective-permute-start | bytes 85256 | tf_op jit(solution)/shard_map/ppermute | solution.py:353
  21.0 0.6 collective-permute-start.2
  21.6 0.0 collective-permute-done.4.a_ref.below_ref
  21.7 6.5 %near0.1.s0 = f32[1,296,256]{2,1,0:T(8,128)S(1)} custom-call(bf16[296,512]{1,0:T(8,128)(2,1)S(1)} %collective-permute-done.4.a_ref.below_ref, bf16[296,512]{1,0:T(8,128)(2,1)S(1)} %get-tuple-element.40.lo_ref.b_ref.a_ref, bf16[296,512]{1,0:T(8,128)(2,1)S(1)} %get-tuple-element.49.hi_ref.c_ref.b_ref, s32[8,1024]{1,0:T(8,128)S(1)} %bitcast.24, ...), custom_call_target="tpu_custom_call" | custom-call | flops 6000000000 | bytes 6000000 | tf_op jit(solution)/shard_map/near0/pallas_call | solution.py:153
  28.1 0.0 collective-permute-done.2.lower_ref
  28.2 0.0 collective-permute-done.3.upper_ref
  28.2 0.1 turn.1
  28.3 1.4 %collective-permute-start.7 = (bf16[296,128]{1,0:T(8,128)(2,1)S(1)}, bf16[296,128]{1,0:T(8,128)(2,1)S(1)}, u32[]{:S(2)}, u32[]{:S(2)}) collective-permute-start(bf16[296,128]{1,0:T(8,128)(2,1)S(1)} %turn.1), channel_id=1, source_target_pairs={{0,8},{4,12},{8,16},{12,20},{16,24},{20,28},{24,0},{28,4},{32,40},... | collective-permute-start | bytes 227336 | tf_op jit(solution)/shard_map/ppermute | solution.py:353
  29.6 2.6 %collective-permute-start.6 = (bf16[296,128]{1,0:T(8,128)(2,1)S(1)}, bf16[296,128]{1,0:T(8,128)(2,1)S(1)}, u32[]{:S(2)}, u32[]{:S(2)}) collective-permute-start(bf16[296,128]{1,0:T(8,128)(2,1)S(1)} %turn.1), channel_id=1, source_target_pairs={{0,16},{4,20},{8,24},{12,28},{16,0},{20,4},{24,8},{28,12},{32,48},... | collective-permute-start | bytes 227336 | tf_op jit(solution)/shard_map/ppermute | solution.py:353
  32.3 1.1 %collective-permute-start.5 = (bf16[296,128]{1,0:T(8,128)(2,1)S(1)}, bf16[296,128]{1,0:T(8,128)(2,1)S(1)}, u32[]{:S(2)}, u32[]{:S(2)}) collective-permute-start(bf16[296,128]{1,0:T(8,128)(2,1)S(1)} %turn.1), channel_id=1, source_target_pairs={{0,24},{4,28},{8,0},{12,4},{16,8},{20,12},{24,16},{28,20},{32,56},... | collective-permute-start | bytes 227336 | tf_op jit(solution)/shard_map/ppermute | solution.py:353
  33.3 6.5 %near1.1.s1 = f32[1,296,256]{2,1,0:T(8,128)S(1)} custom-call(bf16[296,512]{1,0:T(8,128)(2,1)S(1)} %collective-permute-done.4.a_ref.below_ref, bf16[296,512]{1,0:T(8,128)(2,1)S(1)} %get-tuple-element.40.lo_ref.b_ref.a_ref, bf16[296,512]{1,0:T(8,128)(2,1)S(1)} %get-tuple-element.49.hi_ref.c_ref.b_ref, s32[8,1024]{1,0:T(8,128)S(1)} %bitcast.25, ...), custom_call_target="tpu_custom_call" | custom-call | flops 6000000000 | bytes 6000000 | tf_op jit(solution)/shard_map/near1/pallas_call | solution.py:153
  39.8 0.0 collective-permute-done.7
  39.9 0.0 copy-start
  39.9 3.6 %collective-permute-start.12 = (bf16[296,512]{1,0:T(8,128)(2,1)S(1)}, bf16[296,512]{1,0:T(8,128)(2,1)S(1)}, u32[]{:S(2)}, u32[]{:S(2)}) collective-permute-start(bf16[296,512]{1,0:T(8,128)(2,1)S(1)} %pad_maximum_fusion.t0), channel_id=1, source_target_pairs={{0,4},{4,0},{8,12},{12,8},{16,20},{20,16},{24,28},{28,24},{32,36},... | collective-permute-start | bytes 909320 | tf_op jit(solution)/shard_map/ppermute | solution.py:353
  43.5 1.2 %collective-permute-start.10 = (bf16[296,512]{1,0:T(8,128)(2,1)S(1)}, bf16[296,512]{1,0:T(8,128)(2,1)S(1)}, u32[]{:S(2)}, u32[]{:S(2)}) collective-permute-start(bf16[296,512]{1,0:T(8,128)(2,1)S(1)} %pad_maximum_fusion.t0), channel_id=1, source_target_pairs={{0,1},{1,2},{2,3},{3,0},{4,5},{5,6},{6,7},{7,4},{8,9},{9,10},{10,1... | collective-permute-start | bytes 909320 | tf_op jit(solution)/shard_map/ppermute | solution.py:353
  44.7 1.2 %collective-permute-start.9 = (bf16[296,512]{1,0:T(8,128)(2,1)S(1)}, bf16[296,512]{1,0:T(8,128)(2,1)S(1)}, u32[]{:S(2)}, u32[]{:S(2)}) collective-permute-start(bf16[296,512]{1,0:T(8,128)(2,1)S(1)} %pad_maximum_fusion.t0), channel_id=1, source_target_pairs={{0,2},{1,3},{2,0},{3,1},{4,6},{5,7},{6,4},{7,5},{8,10},{9,11},{10,... | collective-permute-start | bytes 909320 | tf_op jit(solution)/shard_map/ppermute | solution.py:353
  45.9 2.1 %collective-permute-start.8 = (bf16[296,512]{1,0:T(8,128)(2,1)S(1)}, bf16[296,512]{1,0:T(8,128)(2,1)S(1)}, u32[]{:S(2)}, u32[]{:S(2)}) collective-permute-start(bf16[296,512]{1,0:T(8,128)(2,1)S(1)} %pad_maximum_fusion.t0), channel_id=1, source_target_pairs={{0,3},{1,0},{2,1},{3,2},{4,7},{5,4},{6,5},{7,6},{8,11},{9,8},{10,9... | collective-permute-start | bytes 909320 | tf_op jit(solution)/shard_map/ppermute | solution.py:353
  48.0 0.0 collective-permute-done.11.c_ref.above_ref
  48.0 12.9 %near2.1.s2 = f32[2,296,256]{2,1,0:T(8,128)S(1)} custom-call(bf16[296,512]{1,0:T(8,128)(2,1)S(1)} %get-tuple-element.40.lo_ref.b_ref.a_ref, bf16[296,512]{1,0:T(8,128)(2,1)S(1)} %get-tuple-element.49.hi_ref.c_ref.b_ref, bf16[296,512]{1,0:T(8,128)(2,1)S(1)} %collective-permute-done.11.c_ref.above_ref, s32[8,1024]{1,0:T(8,128)S(1)} %bitcast.26, ...), custom_call_target="tpu_custom_call" | custom-call | flops 12000000000 | bytes 6000000 | tf_op jit(solution)/shard_map/near2/pallas_call | solution.py:153
  61.0 0.0 collective-permute-done.10.t3
  61.0 0.0 collective-permute-done.8.t1
  61.0 1.0 %collective-permute-start.13 = (bf16[296,512]{1,0:T(8,128)(2,1)S(1)}, bf16[296,512]{1,0:T(8,128)(2,1)S(1)}, u32[]{:S(2)}, u32[]{:S(2)}) collective-permute-start(bf16[296,512]{1,0:T(8,128)(2,1)S(1)} %collective-permute-done.8.t1), channel_id=1, source_target_pairs={{0,4},{4,0},{8,12},{12,8},{16,20},{20,16},{24,28},{28,24},{32,36},... | collective-permute-start | bytes 909320 | tf_op jit(solution)/shard_map/ppermute | solution.py:353
  62.0 0.1 collective-permute-start.14
  62.1 0.4 collective-permute-start.15
  62.5 0.5 flip.1.down_ref
  63.1 0.0 copy-start.4
  63.1 0.0 copy-start.5
  63.1 0.0 copy-start.6
  63.1 0.0 copy-start.7
  63.1 0.0 copy-start.8
  63.1 0.0 copy-start.9
  63.2 1.6 %halo.1.halo_ref = bf16[296,128]{1,0:T(8,128)(2,1)S(1)} custom-call(bf16[296,512]{1,0:T(8,128)(2,1)S(1)} %collective-permute-done.4.a_ref.below_ref, bf16[296,512]{1,0:T(8,128)(2,1)S(1)} %collective-permute-done.11.c_ref.above_ref, bf16[296,2368]{1,0:T(8,128)(2,1)S(1)} %bitcast.22), custom_call_target="tpu_custom_call" | custom-call | flops 2000000000 | bytes 3000000 | tf_op jit(solution)/shard_map/halo/pallas_call | solution.py:193
  64.7 0.0 collective-permute-done.12.t4
  64.8 0.0 collective-permute-done.14.t6
  64.8 0.0 collective-permute-done.15.t7
  64.8 13.8 %last.1 = bf16[296,1024]{1,0:T(8,128)(2,1)} custom-call(bf16[296,512]{1,0:T(8,128)(2,1)S(1)} %pad_maximum_fusion.t0, bf16[296,512]{1,0:T(8,128)(2,1)S(1)} %collective-permute-done.8.t1, bf16[296,512]{1,0:T(8,128)(2,1)S(1)} %collective-permute-done.9.t2, bf16[296,512]{1,0:T(8,128)(2,1)S(1)} %collective-permute-done.10.t3, ...), custom_call_target="tpu_custom_call" | custom-call | flops 8000000000 | bytes 12000000 | tf_op jit(solution)/shard_map/last/pallas_call | solution.py:317
  (22 shorter events, 0.1 us)
Async XLA Ops:
  0.0 5.7 %copy-start.1 = (bf16[2368,296]{0,1:T(8,128)(2,1)S(1)}, bf16[2368,296]{0,1:T(8,128)(2,1)}, u32[]{:S(2)}) copy-start(bf16[2368,296]{0,1:T(8,128)(2,1)} %param.15) | copy-start | bytes 4205572
  1.5 20.2 %slice-start = ((s8[5607424]{0:T(1024)(128)(4,1)}), s8[4194304]{0:T(1024)(128)(4,1)S(1)}, s32[]{:S(2)}) async-start(s8[5607424]{0:T(1024)(128)(4,1)} %bitcast.15), calls=%async_computation | async-start | bytes 8388608
  1.5 20.1 %collective-permute-start.4 = (bf16[296,512]{1,0:T(8,128)(2,1)S(1)}, bf16[296,512]{1,0:T(8,128)(2,1)S(1)}, u32[]{:S(2)}, u32[]{:S(2)}) collective-permute-start(bf16[296,512]{1,0:T(8,128)(2,1)S(1)} %get-tuple-element.49.hi_ref.c_ref.b_ref), channel_id=1, source_target_pairs={{0,1},{1,2},{2,3},{3,4},{4,5},{5,6},{6,7},{7,8},{8,9},{9,10},{10,1... | collective-permute-start | bytes 909320 | tf_op jit(solution)/shard_map/ppermute | solution.py:344
  5.8 15.9 %slice-start.1 = ((s8[5607424]{0:T(1024)(128)(4,1)}), s8[1413120]{0:T(1024)(128)(4,1)S(1)}, s32[]{:S(2)}) async-start(s8[5607424]{0:T(1024)(128)(4,1)} %bitcast.15), calls=%async_computation.1 | async-start | bytes 2826240
  5.8 15.9 %copy-start.2 = (s32[1024,8]{0,1:T(8,128)S(1)}, s32[1024,8]{0,1:T(8,128)}, u32[]{:S(2)}) copy-start(s32[1024,8]{0,1:T(8,128)} %param.18) | copy-start | bytes 98308
  5.8 15.9 %copy-start.3 = (s32[1024,8]{0,1:T(8,128)S(1)}, s32[1024,8]{0,1:T(8,128)}, u32[]{:S(2)}) copy-start(s32[1024,8]{0,1:T(8,128)} %param.19) | copy-start | bytes 98308
  8.6 9.6 %collective-permute-start.1 = (bf16[16,296]{1,0:T(8,128)(2,1)S(1)}, bf16[16,296]{1,0:T(8,128)(2,1)S(1)}, u32[]{:S(2)}, u32[]{:S(2)}) collective-permute-start(bf16[16,296]{1,0:T(8,128)(2,1)S(1)} %get-tuple-element.27), channel_id=1, source_target_pairs={{0,224},{4,228},{8,232},{12,236},{16,240},{20,244},{24,248},{28,25... | collective-permute-start | bytes 28424 | tf_op jit(solution)/shard_map/ppermute | solution.py:353
  14.2 4.0 %collective-permute-start = (bf16[16,296]{1,0:T(8,128)(2,1)S(1)}, bf16[16,296]{1,0:T(8,128)(2,1)S(1)}, u32[]{:S(2)}, u32[]{:S(2)}) collective-permute-start(bf16[16,296]{1,0:T(8,128)(2,1)S(1)} %get-tuple-element.27), channel_id=1, source_target_pairs={{0,32},{4,36},{8,40},{12,44},{16,48},{20,52},{24,56},{28,60},{32,6... | collective-permute-start | bytes 28424 | tf_op jit(solution)/shard_map/ppermute | solution.py:353
  14.2 33.8 %collective-permute-start.11 = (bf16[296,512]{1,0:T(8,128)(2,1)S(1)}, bf16[296,512]{1,0:T(8,128)(2,1)S(1)}, u32[]{:S(2)}, u32[]{:S(2)}) collective-permute-start(bf16[296,512]{1,0:T(8,128)(2,1)S(1)} %get-tuple-element.40.lo_ref.b_ref.a_ref), channel_id=1, source_target_pairs={{1,0},{2,1},{3,2},{4,3},{5,4},{6,5},{7,6},{8,7},{9,8},{10,9},{11,1... | collective-permute-start | bytes 909320 | tf_op jit(solution)/shard_map/ppermute | solution.py:344
  18.3 9.9 %collective-permute-start.3 = (bf16[3,16,296]{2,1,0:T(8,128)(2,1)S(1)}, bf16[3,16,296]{2,1,0:T(8,128)(2,1)S(1)}, u32[]{:S(2)}, u32[]{:S(2)}) collective-permute-start(bf16[3,16,296]{2,1,0:T(8,128)(2,1)S(1)} %pad_maximum_fusion.1.middle_ref), channel_id=1, source_target_pairs={{0,160},{4,164},{8,168},{12,172},{16,176},{20,180},{24,184},{28,18... | collective-permute-start | bytes 85256 | tf_op jit(solution)/shard_map/ppermute | solution.py:353
  21.0 7.1 %collective-permute-start.2 = (bf16[2,16,296]{2,1,0:T(8,128)(2,1)S(1)}, bf16[2,16,296]{2,1,0:T(8,128)(2,1)S(1)}, u32[]{:S(2)}, u32[]{:S(2)}) collective-permute-start(bf16[2,16,296]{2,1,0:T(8,128)(2,1)S(1)} %slice.11), channel_id=1, source_target_pairs={{0,96},{4,100},{8,104},{12,108},{16,112},{20,116},{24,120},{28,124... | collective-permute-start | bytes 56840 | tf_op jit(solution)/shard_map/ppermute | solution.py:353
  28.3 11.6 %collective-permute-start.7 = (bf16[296,128]{1,0:T(8,128)(2,1)S(1)}, bf16[296,128]{1,0:T(8,128)(2,1)S(1)}, u32[]{:S(2)}, u32[]{:S(2)}) collective-permute-start(bf16[296,128]{1,0:T(8,128)(2,1)S(1)} %turn.1), channel_id=1, source_target_pairs={{0,8},{4,12},{8,16},{12,20},{16,24},{20,28},{24,0},{28,4},{32,40},... | collective-permute-start | bytes 227336 | tf_op jit(solution)/shard_map/ppermute | solution.py:353
  29.6 10.2 %collective-permute-start.6 = (bf16[296,128]{1,0:T(8,128)(2,1)S(1)}, bf16[296,128]{1,0:T(8,128)(2,1)S(1)}, u32[]{:S(2)}, u32[]{:S(2)}) collective-permute-start(bf16[296,128]{1,0:T(8,128)(2,1)S(1)} %turn.1), channel_id=1, source_target_pairs={{0,16},{4,20},{8,24},{12,28},{16,0},{20,4},{24,8},{28,12},{32,48},... | collective-permute-start | bytes 227336 | tf_op jit(solution)/shard_map/ppermute | solution.py:353
  32.3 7.6 %collective-permute-start.5 = (bf16[296,128]{1,0:T(8,128)(2,1)S(1)}, bf16[296,128]{1,0:T(8,128)(2,1)S(1)}, u32[]{:S(2)}, u32[]{:S(2)}) collective-permute-start(bf16[296,128]{1,0:T(8,128)(2,1)S(1)} %turn.1), channel_id=1, source_target_pairs={{0,24},{4,28},{8,0},{12,4},{16,8},{20,12},{24,16},{28,20},{32,56},... | collective-permute-start | bytes 227336 | tf_op jit(solution)/shard_map/ppermute | solution.py:353
  39.9 22.6 %copy-start = (bf16[296,2368]{1,0:T(8,128)(2,1)S(1)}, bf16[296,2368]{1,0:T(8,128)(2,1)}, u32[]{:S(2)}) copy-start(bf16[296,2368]{1,0:T(8,128)(2,1)} %down_ref.1) | copy-start | bytes 4205572
  39.9 24.8 %collective-permute-start.12 = (bf16[296,512]{1,0:T(8,128)(2,1)S(1)}, bf16[296,512]{1,0:T(8,128)(2,1)S(1)}, u32[]{:S(2)}, u32[]{:S(2)}) collective-permute-start(bf16[296,512]{1,0:T(8,128)(2,1)S(1)} %pad_maximum_fusion.t0), channel_id=1, source_target_pairs={{0,4},{4,0},{8,12},{12,8},{16,20},{20,16},{24,28},{28,24},{32,36},... | collective-permute-start | bytes 909320 | tf_op jit(solution)/shard_map/ppermute | solution.py:353
  43.5 17.5 %collective-permute-start.10 = (bf16[296,512]{1,0:T(8,128)(2,1)S(1)}, bf16[296,512]{1,0:T(8,128)(2,1)S(1)}, u32[]{:S(2)}, u32[]{:S(2)}) collective-permute-start(bf16[296,512]{1,0:T(8,128)(2,1)S(1)} %pad_maximum_fusion.t0), channel_id=1, source_target_pairs={{0,1},{1,2},{2,3},{3,0},{4,5},{5,6},{6,7},{7,4},{8,9},{9,10},{10,1... | collective-permute-start | bytes 909320 | tf_op jit(solution)/shard_map/ppermute | solution.py:353
  44.7 16.3 %collective-permute-start.9 = (bf16[296,512]{1,0:T(8,128)(2,1)S(1)}, bf16[296,512]{1,0:T(8,128)(2,1)S(1)}, u32[]{:S(2)}, u32[]{:S(2)}) collective-permute-start(bf16[296,512]{1,0:T(8,128)(2,1)S(1)} %pad_maximum_fusion.t0), channel_id=1, source_target_pairs={{0,2},{1,3},{2,0},{3,1},{4,6},{5,7},{6,4},{7,5},{8,10},{9,11},{10,... | collective-permute-start | bytes 909320 | tf_op jit(solution)/shard_map/ppermute | solution.py:353
  45.9 15.1 %collective-permute-start.8 = (bf16[296,512]{1,0:T(8,128)(2,1)S(1)}, bf16[296,512]{1,0:T(8,128)(2,1)S(1)}, u32[]{:S(2)}, u32[]{:S(2)}) collective-permute-start(bf16[296,512]{1,0:T(8,128)(2,1)S(1)} %pad_maximum_fusion.t0), channel_id=1, source_target_pairs={{0,3},{1,0},{2,1},{3,2},{4,7},{5,4},{6,5},{7,6},{8,11},{9,8},{10,9... | collective-permute-start | bytes 909320 | tf_op jit(solution)/shard_map/ppermute | solution.py:353
  61.0 3.7 %collective-permute-start.13 = (bf16[296,512]{1,0:T(8,128)(2,1)S(1)}, bf16[296,512]{1,0:T(8,128)(2,1)S(1)}, u32[]{:S(2)}, u32[]{:S(2)}) collective-permute-start(bf16[296,512]{1,0:T(8,128)(2,1)S(1)} %collective-permute-done.8.t1), channel_id=1, source_target_pairs={{0,4},{4,0},{8,12},{12,8},{16,20},{20,16},{24,28},{28,24},{32,36},... | collective-permute-start | bytes 909320 | tf_op jit(solution)/shard_map/ppermute | solution.py:353
  62.0 2.7 %collective-permute-start.14 = (bf16[296,512]{1,0:T(8,128)(2,1)S(1)}, bf16[296,512]{1,0:T(8,128)(2,1)S(1)}, u32[]{:S(2)}, u32[]{:S(2)}) collective-permute-start(bf16[296,512]{1,0:T(8,128)(2,1)S(1)} %collective-permute-done.9.t2), channel_id=1, source_target_pairs={{0,4},{4,0},{8,12},{12,8},{16,20},{20,16},{24,28},{28,24},{32,36},... | collective-permute-start | bytes 909320 | tf_op jit(solution)/shard_map/ppermute | solution.py:353
  62.1 2.7 %collective-permute-start.15 = (bf16[296,512]{1,0:T(8,128)(2,1)S(1)}, bf16[296,512]{1,0:T(8,128)(2,1)S(1)}, u32[]{:S(2)}, u32[]{:S(2)}) collective-permute-start(bf16[296,512]{1,0:T(8,128)(2,1)S(1)} %collective-permute-done.10.t3), channel_id=1, source_target_pairs={{0,4},{4,0},{8,12},{12,8},{16,20},{20,16},{24,28},{28,24},{32,36},... | collective-permute-start | bytes 909320 | tf_op jit(solution)/shard_map/ppermute | solution.py:353
  63.1 1.7 %copy-start.4 = (s32[128,8]{0,1:T(8,128)S(1)}, s32[128,8]{0,1:T(8,128)}, u32[]{:S(2)}) copy-start(s32[128,8]{0,1:T(8,128)} %param.20) | copy-start | bytes 12292
  63.1 1.7 %copy-start.5 = (s32[128,8]{0,1:T(8,128)S(1)}, s32[128,8]{0,1:T(8,128)}, u32[]{:S(2)}) copy-start(s32[128,8]{0,1:T(8,128)} %param.21) | copy-start | bytes 12292
  63.1 1.7 %copy-start.6 = (s32[16,8]{0,1:T(8,128)S(1)}, s32[16,8]{0,1:T(8,128)}, u32[]{:S(2)}) copy-start(s32[16,8]{0,1:T(8,128)} %param.22) | copy-start | bytes 1540
  63.1 1.7 %copy-start.7 = (s32[16,8]{0,1:T(8,128)S(1)}, s32[16,8]{0,1:T(8,128)}, u32[]{:S(2)}) copy-start(s32[16,8]{0,1:T(8,128)} %param.23) | copy-start | bytes 1540
  63.1 1.7 %copy-start.8 = (s32[2,8]{1,0:T(2,128)S(1)}, s32[2,8]{1,0:T(2,128)}, u32[]{:S(2)}) copy-start(s32[2,8]{1,0:T(2,128)} %src4_ref.1) | copy-start | bytes 196
  63.1 1.7 %copy-start.9 = (s32[2,8]{1,0:T(2,128)S(1)}, s32[2,8]{1,0:T(2,128)}, u32[]{:S(2)}) copy-start(s32[2,8]{1,0:T(2,128)} %cls4_ref.1) | copy-start | bytes 196
